TPU v7x, 32 devices: a whole 2x2x4 slice. The times are simulated.
32 devices in a mesh: section: 2 (over core), group: 4 (over z), member: 4 (over y, x).
Axes of the slice: x: 2, y: 2, z: 4, core: 2. Of those that a mesh axis runs over, the one named last changes fastest.
Arguments:
- tokens: bfloat16 [65536, 384], P(('group', 'member')), may hold values from -6 to 6
- segment: int32 [65536], P(('group', 'member')), may hold values from -1 to 5, as said below
- cotangent: bfloat16 [65536, 384], P(('group', 'member')), may hold values from -6 to 6
- attn_gain: float32 [2, 384], P('section'), may hold values from 0.1 to 1.9
- attn_shift: float32 [2, 384], P('section'), may hold values from -3 to 3
- qkv_weight: bfloat16 [2, 384, 1152], P('section'), may hold values from -0.3125 to 0.3125
- qv_bias: float32 [2, 768], P('section'), may hold values from -3 to 3
- proj_weight: bfloat16 [2, 384, 384], P('section'), may hold values from -2.5 to 2.5
- proj_bias: float32 [2, 384], P('section'), may hold values from -3 to 3
- mlp_gain: float32 [2, 384], P('section'), may hold values from 0.1 to 1.9
- mlp_shift: float32 [2, 384], P('section'), may hold values from -3 to 3
- fc1_weight: bfloat16 [2, 384, 1536], P('section'), may hold values from -0.3125 to 0.3125
- fc1_bias: float32 [2, 1536], P('section'), may hold values from -3 to 3
- fc2_weight: bfloat16 [2, 1536, 384], P('section'), may hold values from -0.15625 to 0.15625
- fc2_bias: float32 [2, 384], P('section'), may hold values from -3 to 3
Outputs:
- activations: bfloat16 [2, 65536, 384], P('section', ('group', 'member'))
- in_grads: float32 [2, 65536, 384], P('section', ('group', 'member'))
- grad_attn_gain: float32 [2, 384], P('section', 'member')
- grad_attn_shift: float32 [2, 384], P('section', 'member')
- grad_qkv_weight: float32 [2, 384, 1152], P('section', 'member')
- grad_qv_bias: float32 [2, 768], P('section', 'member')
- grad_proj_weight: float32 [2, 384, 384], P('section', 'member')
- grad_proj_bias: float32 [2, 384], P('section', 'member')
- grad_mlp_gain: float32 [2, 384], P('section', 'member')
- grad_mlp_shift: float32 [2, 384], P('section', 'member')
- grad_fc1_weight: float32 [2, 384, 1536], P('section', 'member')
- grad_fc1_bias: float32 [2, 1536], P('section', 'member')
- grad_fc2_weight: float32 [2, 1536, 384], P('section', 'member')
- grad_fc2_bias: float32 [2, 384], P('section', 'member')
Inputs may be any that keep to these rules, and one draw needn't show every extreme that they name: Sequences are consecutive runs of 256 rows. Even-numbered sequences hold one global crop: segment 0 on their first 197 rows, -1 after. Odd-numbered ones hold 4 to 6 local crops of 37 rows each, numbered 0, 1, ... in order, then -1 on the remaining rows.
All inputs are finite; a program needn't handle non-finite values.
Results may differ from a plain program's by a relative error of at most 0.017.
Values may be sent and summed in bfloat16 or wider, within the bound.
A program may use at most 384 MiB of HBM per device.

v0:
```python
from functools import partial

import jax
import jax.numpy as jnp
from jax import lax
from jax.sharding import PartitionSpec as P

H = 6
HD = 64
S = 256
MICRO = 8
SEQ_MB = 2


norm_eps = 1e-06


def from_behind(value, axis, steps):
    count = lax.axis_size(axis)
    first, last = (max(0, -steps), min(count, count - steps))
    return lax.ppermute(value, axis, [(source, source + steps) for source in range(first, last)])


def row_parts(values):
    average = jnp.mean(values, axis=1, keepdims=True)
    centered = values - average
    inverse = lax.rsqrt(jnp.mean(centered * centered, axis=1, keepdims=True) + norm_eps)
    return (centered * inverse, inverse)


def norm_back(values, gain, grad_out):
    scaled, inverse = row_parts(values)
    grad_scaled = grad_out * gain
    centered_grad = grad_scaled - jnp.mean(grad_scaled, axis=1, keepdims=True)
    grad_values = inverse * (
        centered_grad - scaled * jnp.mean(grad_scaled * scaled, axis=1, keepdims=True)
    )
    return (grad_values, jnp.sum(grad_out * scaled, axis=0), jnp.sum(grad_out, axis=0))


def mask_for(segment_ids):
    same = segment_ids[:, :, None] == segment_ids[:, None, :]
    allowed = (
        same & (segment_ids[:, None, :] >= 0) | jnp.eye(segment_ids.shape[1], dtype=bool)[None]
    )
    return allowed[:, None]


def masked_scores(queries, key_rows, allowed):
    raw = jnp.einsum("bqhd,bkhd->bhqk", queries, key_rows, preferred_element_type=jnp.float32)
    return jnp.where(allowed, raw * HD ** (-0.5), -1e30)


def split_heads(mixed, sequences):
    shaped = mixed.reshape(sequences, -1, 3, H, HD)
    return (shaped[:, :, 0], shaped[:, :, 1], shaped[:, :, 2])


def layer_forward(hidden_low, segment_ids, params):
    (
        attn_gain,
        attn_shift,
        qkv_weight,
        qv_bias,
        proj_weight,
        proj_bias,
        mlp_gain,
        mlp_shift,
        fc1_weight,
        fc1_bias,
        fc2_weight,
        fc2_bias,
    ) = params
    hidden = hidden_low.astype(jnp.float32)
    width = hidden.shape[1]
    sequences = segment_ids.shape[0]
    scaled, unused = row_parts(hidden)
    normed = (scaled * attn_gain + attn_shift).astype(jnp.bfloat16)
    bias_full = jnp.concatenate(
        [qv_bias[:width], jnp.zeros((width,), jnp.float32), qv_bias[width:]]
    )
    mixed = (jnp.dot(normed, qkv_weight, preferred_element_type=jnp.float32) + bias_full).astype(
        jnp.bfloat16
    )
    queries, key_rows, value_rows = split_heads(mixed, sequences)
    scores = masked_scores(queries, key_rows, mask_for(segment_ids))
    peak = jnp.max(scores, axis=-1, keepdims=True)
    exponent = jnp.exp(scores - peak)
    row_total = jnp.sum(exponent, axis=-1, keepdims=True)
    log_total = peak + jnp.log(row_total)
    probs_low = (exponent / row_total).astype(jnp.bfloat16)
    context = jnp.einsum(
        "bhqk,bkhd->bqhd", probs_low, value_rows, preferred_element_type=jnp.float32
    )
    context = context.astype(jnp.bfloat16).reshape(-1, width)
    after = hidden + jnp.dot(context, proj_weight, preferred_element_type=jnp.float32) + proj_bias
    scaled_two, unused_two = row_parts(after)
    normed_two = (scaled_two * mlp_gain + mlp_shift).astype(jnp.bfloat16)
    before = jnp.dot(normed_two, fc1_weight, preferred_element_type=jnp.float32) + fc1_bias
    active = jax.nn.gelu(before, approximate=False).astype(jnp.bfloat16)
    output = after + jnp.dot(active, fc2_weight, preferred_element_type=jnp.float32) + fc2_bias
    return (
        output,
        (hidden_low, normed, mixed, log_total, context, after, normed_two, before, active),
    )


def layer_backward(grad_low, kept, segment_ids, params):
    (
        attn_gain,
        attn_shift,
        qkv_weight,
        qv_bias,
        proj_weight,
        proj_bias,
        mlp_gain,
        mlp_shift,
        fc1_weight,
        fc1_bias,
        fc2_weight,
        fc2_bias,
    ) = params
    hidden_low, normed, mixed, log_total, context, after, normed_two, before, active = kept
    width = after.shape[1]
    sequences = segment_ids.shape[0]
    grad_fc2_bias = jnp.sum(grad_low.astype(jnp.float32), axis=0)
    grad_fc2_weight = jnp.einsum("rf,rd->fd", active, grad_low, preferred_element_type=jnp.float32)
    grad_active = jnp.einsum("rd,fd->rf", grad_low, fc2_weight, preferred_element_type=jnp.float32)
    unused, gelu_pull = jax.vjp(partial(jax.nn.gelu, approximate=False), before)
    grad_before = gelu_pull(grad_active)[0].astype(jnp.bfloat16)
    grad_fc1_bias = jnp.sum(grad_before.astype(jnp.float32), axis=0)
    grad_fc1_weight = jnp.einsum(
        "rd,rf->df", normed_two, grad_before, preferred_element_type=jnp.float32
    )
    grad_normed_two = jnp.einsum(
        "rf,df->rd", grad_before, fc1_weight, preferred_element_type=jnp.float32
    )
    grad_norm_two, grad_mlp_gain, grad_mlp_shift = norm_back(after, mlp_gain, grad_normed_two)
    grad_after = grad_low.astype(jnp.float32) + grad_norm_two
    grad_branch = grad_after.astype(jnp.bfloat16)
    grad_proj_bias = jnp.sum(grad_branch.astype(jnp.float32), axis=0)
    grad_proj_weight = jnp.einsum(
        "rc,rd->cd", context, grad_branch, preferred_element_type=jnp.float32
    )
    grad_context = jnp.einsum(
        "rd,cd->rc", grad_branch, proj_weight, preferred_element_type=jnp.float32
    )
    grad_context = grad_context.astype(jnp.bfloat16).reshape(sequences, -1, H, HD)
    queries, key_rows, value_rows = split_heads(mixed, sequences)
    scores = masked_scores(queries, key_rows, mask_for(segment_ids))
    probs = jnp.exp(scores - log_total)
    probs_low = probs.astype(jnp.bfloat16)
    grad_values = jnp.einsum(
        "bhqk,bqhd->bkhd", probs_low, grad_context, preferred_element_type=jnp.float32
    )
    grad_probs = jnp.einsum(
        "bqhd,bkhd->bhqk", grad_context, value_rows, preferred_element_type=jnp.float32
    )
    inner = jnp.sum(probs * grad_probs, axis=-1, keepdims=True)
    grad_raw = (probs * (grad_probs - inner) * HD ** (-0.5)).astype(jnp.bfloat16)
    grad_queries = jnp.einsum(
        "bhqk,bkhd->bqhd", grad_raw, key_rows, preferred_element_type=jnp.float32
    )
    grad_keys = jnp.einsum("bhqk,bqhd->bkhd", grad_raw, queries, preferred_element_type=jnp.float32)
    grad_mixed = jnp.stack([grad_queries, grad_keys, grad_values], axis=2).reshape(-1, 3 * width)
    grad_mixed = grad_mixed.astype(jnp.bfloat16)
    column_sums = jnp.sum(grad_mixed.astype(jnp.float32), axis=0)
    grad_qv_bias = jnp.concatenate([column_sums[:width], column_sums[2 * width :]])
    grad_qkv_weight = jnp.einsum(
        "rd,re->de", normed, grad_mixed, preferred_element_type=jnp.float32
    )
    grad_normed = jnp.einsum(
        "re,de->rd", grad_mixed, qkv_weight, preferred_element_type=jnp.float32
    )
    grad_norm_one, grad_attn_gain, grad_attn_shift = norm_back(
        hidden_low.astype(jnp.float32), attn_gain, grad_normed
    )
    grad_hidden = grad_after + grad_norm_one
    return (
        grad_hidden,
        (
            grad_attn_gain,
            grad_attn_shift,
            grad_qkv_weight,
            grad_qv_bias,
            grad_proj_weight,
            grad_proj_bias,
            grad_mlp_gain,
            grad_mlp_shift,
            grad_fc1_weight,
            grad_fc1_bias,
            grad_fc2_weight,
            grad_fc2_bias,
        ),
    )


def per_device(
    tokens,
    segment,
    cotangent,
    attn_gain,
    attn_shift,
    qkv_weight,
    qv_bias,
    proj_weight,
    proj_bias,
    mlp_gain,
    mlp_shift,
    fc1_weight,
    fc1_bias,
    fc2_weight,
    fc2_bias,
):
    section = lax.axis_index("section")
    params = tuple(
        (
            item[0]
            for item in (
                attn_gain,
                attn_shift,
                qkv_weight,
                qv_bias,
                proj_weight,
                proj_bias,
                mlp_gain,
                mlp_shift,
                fc1_weight,
                fc1_bias,
                fc2_weight,
                fc2_bias,
            )
        )
    )
    width = tokens.shape[1]
    row_count = SEQ_MB * S
    inputs = tokens.reshape(MICRO, row_count, width)
    upstream = cotangent.reshape(MICRO, row_count, width)
    segments = segment.reshape(MICRO, SEQ_MB, S)
    outputs = jnp.zeros((MICRO, row_count, width), jnp.bfloat16)
    received = jnp.zeros((row_count, width), jnp.bfloat16)
    kept_store = ()
    for moment in range(MICRO + 1):
        index = jnp.clip(moment - section, 0, MICRO - 1)
        hidden_low = jnp.where(section == 0, inputs[index], received)
        result, kept = layer_forward(hidden_low, segments[index], params)
        result_low = result.astype(jnp.bfloat16)
        outputs = outputs.at[index].set(result_low)
        if moment == 0:
            kept_store = tuple((jnp.zeros((MICRO,) + item.shape, item.dtype) for item in kept))
        kept_store = tuple((store.at[index].set(item) for store, item in zip(kept_store, kept)))
        if moment < MICRO:
            received = from_behind(result_low, "section", 1)
    grad_store = jnp.zeros((MICRO, row_count, width), jnp.float32)
    coming = jnp.zeros((row_count, width), jnp.bfloat16)
    totals = ()
    for moment in range(MICRO + 1):
        position = moment - 1 + section
        valid = (position >= 0) & (position < MICRO)
        index = jnp.clip(position, 0, MICRO - 1)
        incoming = jnp.where(section == 1, upstream[index], coming)
        incoming = jnp.where(valid, incoming, jnp.zeros_like(incoming))
        kept = tuple((store[index] for store in kept_store))
        grad_hidden, grads = layer_backward(incoming, kept, segments[index], params)
        sent = grad_hidden.astype(jnp.bfloat16)
        keep_value = jnp.where(section == 1, sent.astype(jnp.float32), grad_hidden)
        grad_store = grad_store.at[index].set(jnp.where(valid, keep_value, grad_store[index]))
        if moment == 0:
            totals = grads
        else:
            totals = tuple((running + term for running, term in zip(totals, grads)))
        if moment < MICRO:
            coming = from_behind(sent, "section", -1)
    partial_rows = (
        lax.psum_scatter(
            totals[0].astype(jnp.bfloat16), "member", scatter_dimension=0, tiled=True
        ).astype(jnp.float32),
        lax.psum_scatter(
            totals[1].astype(jnp.bfloat16), "member", scatter_dimension=0, tiled=True
        ).astype(jnp.float32),
        lax.psum_scatter(
            totals[2].astype(jnp.bfloat16), "member", scatter_dimension=0, tiled=True
        ).astype(jnp.float32),
        lax.psum_scatter(
            totals[3].astype(jnp.bfloat16), "member", scatter_dimension=0, tiled=True
        ).astype(jnp.float32),
        lax.psum_scatter(
            totals[4].astype(jnp.bfloat16), "member", scatter_dimension=0, tiled=True
        ).astype(jnp.float32),
        lax.psum_scatter(
            totals[5].astype(jnp.bfloat16), "member", scatter_dimension=0, tiled=True
        ).astype(jnp.float32),
        lax.psum_scatter(
            totals[6].astype(jnp.bfloat16), "member", scatter_dimension=0, tiled=True
        ).astype(jnp.float32),
        lax.psum_scatter(
            totals[7].astype(jnp.bfloat16), "member", scatter_dimension=0, tiled=True
        ).astype(jnp.float32),
        lax.psum_scatter(
            totals[8].astype(jnp.bfloat16), "member", scatter_dimension=0, tiled=True
        ).astype(jnp.float32),
        lax.psum_scatter(
            totals[9].astype(jnp.bfloat16), "member", scatter_dimension=0, tiled=True
        ).astype(jnp.float32),
        lax.psum_scatter(
            totals[10].astype(jnp.bfloat16), "member", scatter_dimension=0, tiled=True
        ).astype(jnp.float32),
        lax.psum_scatter(
            totals[11].astype(jnp.bfloat16), "member", scatter_dimension=0, tiled=True
        ).astype(jnp.float32),
    )
    shards = (
        lax.psum(partial_rows[0].astype(jnp.bfloat16), "group").astype(jnp.float32),
        lax.psum(partial_rows[1].astype(jnp.bfloat16), "group").astype(jnp.float32),
        lax.psum(partial_rows[2].astype(jnp.bfloat16), "group").astype(jnp.float32),
        lax.psum(partial_rows[3].astype(jnp.bfloat16), "group").astype(jnp.float32),
        lax.psum(partial_rows[4].astype(jnp.bfloat16), "group").astype(jnp.float32),
        lax.psum(partial_rows[5].astype(jnp.bfloat16), "group").astype(jnp.float32),
        lax.psum(partial_rows[6].astype(jnp.bfloat16), "group").astype(jnp.float32),
        lax.psum(partial_rows[7].astype(jnp.bfloat16), "group").astype(jnp.float32),
        lax.psum(partial_rows[8].astype(jnp.bfloat16), "group").astype(jnp.float32),
        lax.psum(partial_rows[9].astype(jnp.bfloat16), "group").astype(jnp.float32),
        lax.psum(partial_rows[10].astype(jnp.bfloat16), "group").astype(jnp.float32),
        lax.psum(partial_rows[11].astype(jnp.bfloat16), "group").astype(jnp.float32),
    )
    return (
        outputs.reshape(-1, width)[None],
        grad_store.reshape(-1, width)[None],
        shards[0][None],
        shards[1][None],
        shards[2][None],
        shards[3][None],
        shards[4][None],
        shards[5][None],
        shards[6][None],
        shards[7][None],
        shards[8][None],
        shards[9][None],
        shards[10][None],
        shards[11][None],
    )


def solution(mesh):
    placed = (
        P(("group", "member"), None),
        P(("group", "member")),
        P(("group", "member"), None),
        P("section", None),
        P("section", None),
        P("section", None, None),
        P("section", None),
        P("section", None, None),
        P("section", None),
        P("section", None),
        P("section", None),
        P("section", None, None),
        P("section", None),
        P("section", None, None),
        P("section", None),
    )
    return jax.shard_map(
        per_device,
        mesh=mesh,
        in_specs=placed,
        out_specs=(
            P("section", ("group", "member"), None),
            P("section", ("group", "member"), None),
            P("section", "member"),
            P("section", "member"),
            P("section", "member", None),
            P("section", "member"),
            P("section", "member", None),
            P("section", "member"),
            P("section", "member"),
            P("section", "member"),
            P("section", "member", None),
            P("section", "member"),
            P("section", "member", None),
            P("section", "member"),
        ),
        check_vma=False,
    )
```

profile of v0, /device:TPU:0, one launch (start us, length us, event | category | flops | bytes accessed | tf_op | source)
XLA Modules:
  0.0 1362.7 jit_solution(13824378937941243672)
XLA Ops:
  42.7 9.8 bitcast_dynamic-update-slice_fusion.1
  56.9 14.5 %collective-permute-start = (bf16[512,384]{1,0:T(8,128)(2,1)}, bf16[512,384]{1,0:T(8,128)(2,1)}, u32[]{:S(2)}, u32[]{:S(2)}) collective-permute-start(bf16[512,384]{1,0:T(8,128)(2,1)} %get-tuple-element.1650), channel_id=1, source_target_pairs={{0,16},{1,17},{2,18},{3,19},{4,20},{5,21},{6,22},{7,23},{8,24},{9,... | collective-permute-start | bytes 1179656 | tf_op jit(solution)/shard_map/ppermute | solution.py:21
  86.7 11.5 broadcast_in_dim.192
  133.9 11.0 fusion.463
  185.0 11.0 fusion.462
  235.7 11.0 fusion.461
  286.3 10.9 fusion.460
  336.7 11.0 fusion.459
  387.3 11.0 fusion.458
  437.9 11.0 fusion.457
  487.7 10.9 fusion.456
  503.5 10.8 convert_reduce_fusion.8
  746.9 9.8 convert_reduce_fusion.7
  816.1 10.0 convert_reduce_fusion.6
  880.4 9.7 convert_reduce_fusion.5
  943.9 9.7 convert_reduce_fusion.4
  1003.4 9.5 convert_reduce_fusion.3
  1108.0 9.4 convert_reduce_fusion.1
  1159.6 9.5 convert_reduce_fusion
  1239.7 17.2 %all-reduce.8 = (bf16[384]{0:T(512)(128)(2,1)S(1)}, bf16[384]{0:T(512)(128)(2,1)S(1)}, bf16[768]{0:T(1024)(128)(2,1)S(1)}, bf16[384]{0:T(512)(128)(2,1)S(1)}, bf...) all-reduce(bf16[384]{0:T(512)(128)(2,1)S(1)} %add_convert_fusion.15, ...), channel_id=2, replica_groups=mesh['section'=2,'group'=4,'member'=4] {'member'}, use_global_device_ids=true, to_apply=%region_171.172.clone | all-reduce | flops 4608 | bytes 18432
  1257.1 10.3 reduce-scatter.11.cloned.1.call-done
  1267.4 31.4 %reduce-scatter.9.cloned.1.call-done = bf16[96,1536]{1,0:T(8,128)(2,1)} async-done(((bf16[384,1536]{1,0:T(8,128)(2,1)}), bf16[96,1536]{1,0:T(8,128)(2,1)}) %reduce-scatter.9.cloned.1.call-update) | async-done | bytes 294928 | tf_op jit(solution)/shard_map/reduce_scatter | solution.py:299
  1299.1 11.9 all-reduce.9
  1318.6 30.4 %all-reduce.13.cloned.1.call-done = (bf16[1,96,1152]{2,1,0:T(8,128)(2,1)}, bf16[1,96,384]{2,1,0:T(8,128)(2,1)}, bf16[1,96,1536]{2,1,0:T(8,128)(2,1)}, bf16[1,384,384]{2,1,0:T(8,128)(2,1)}) async-done(((bf16[1,96,1152]{2,1,0:T(8,128)(2,1)}, bf16[1,96,384]{2,1,0:T(8,128)(2,1)}, bf16[1,96,1536]{2,1,0:T(8,128)(2,1)}, bf16[1,384,384]{2,1,0:T(8,128)(2,1)}), (bf16[1,96,1152]{2,1,0:T(8,128)(2,1)}, ...) | async-done | bytes 884752 | tf_op jit(solution)/shard_map/psum | solution.py:315
  (1275 shorter events, 1039.3 us)
Async XLA Ops:
  7.2 35.5 %copy-start = (bf16[1,384,1536]{2,1,0:T(8,128)(2,1)S(1)}, bf16[1,384,1536]{2,1,0:T(8,128)(2,1)}, u32[]{:S(2)}) copy-start(bf16[1,384,1536]{2,1,0:T(8,128)(2,1)} %param.224) | copy-start | bytes 3538948
  7.2 1249.9 %reduce-scatter.7.cloned.1.call-start = ((), (), s32[]{:S(2)}) async-start(), calls=%async_computation.5 | async-start | bytes 368640 | tf_op jit(solution)/shard_map/reduce_scatter | solution.py:287
  37.0 411.9 %copy-start.256 = (f32[384]{0:T(512)}, f32[384]{0:T(512)S(1)}, u32[]{:S(2)}) copy-start(f32[384]{0:T(512)S(1)} %reduce.370) | copy-start | bytes 4612
  56.9 19.4 %copy-start.133 = (s32[3]{0:T(128)S(1)}, s32[3]{0:T(128)}, u32[]{:S(2)}) copy-start(s32[3]{0:T(128)} %constant.2163.clone.1) | copy-start | bytes 40
  56.9 57.3 %collective-permute-start = (bf16[512,384]{1,0:T(8,128)(2,1)}, bf16[512,384]{1,0:T(8,128)(2,1)}, u32[]{:S(2)}, u32[]{:S(2)}) collective-permute-start(bf16[512,384]{1,0:T(8,128)(2,1)} %get-tuple-element.1650), channel_id=1, source_target_pairs={{0,16},{1,17},{2,18},{3,19},{4,20},{5,21},{6,22},{7,23},{8,24},{9,... | collective-permute-start | bytes 1179656 | tf_op jit(solution)/shard_map/ppermute | solution.py:21
  148.4 17.1 %collective-permute-start.1 = (bf16[512,384]{1,0:T(8,128)(2,1)}, bf16[512,384]{1,0:T(8,128)(2,1)}, u32[]{:S(2)}, u32[]{:S(2)}) collective-permute-start(bf16[512,384]{1,0:T(8,128)(2,1)} %get-tuple-element.1657), channel_id=1, source_target_pairs={{0,16},{1,17},{2,18},{3,19},{4,20},{5,21},{6,22},{7,23},{8,24},{9,... | collective-permute-start | bytes 1179656 | tf_op jit(solution)/shard_map/ppermute | solution.py:21
  199.5 16.7 %collective-permute-start.2 = (bf16[512,384]{1,0:T(8,128)(2,1)}, bf16[512,384]{1,0:T(8,128)(2,1)}, u32[]{:S(2)}, u32[]{:S(2)}) collective-permute-start(bf16[512,384]{1,0:T(8,128)(2,1)} %get-tuple-element.1664), channel_id=1, source_target_pairs={{0,16},{1,17},{2,18},{3,19},{4,20},{5,21},{6,22},{7,23},{8,24},{9,... | collective-permute-start | bytes 1179656 | tf_op jit(solution)/shard_map/ppermute | solution.py:21
  250.2 16.8 %collective-permute-start.3 = (bf16[512,384]{1,0:T(8,128)(2,1)}, bf16[512,384]{1,0:T(8,128)(2,1)}, u32[]{:S(2)}, u32[]{:S(2)}) collective-permute-start(bf16[512,384]{1,0:T(8,128)(2,1)} %get-tuple-element.1671), channel_id=1, source_target_pairs={{0,16},{1,17},{2,18},{3,19},{4,20},{5,21},{6,22},{7,23},{8,24},{9,... | collective-permute-start | bytes 1179656 | tf_op jit(solution)/shard_map/ppermute | solution.py:21
  300.6 16.6 %collective-permute-start.4 = (bf16[512,384]{1,0:T(8,128)(2,1)}, bf16[512,384]{1,0:T(8,128)(2,1)}, u32[]{:S(2)}, u32[]{:S(2)}) collective-permute-start(bf16[512,384]{1,0:T(8,128)(2,1)} %get-tuple-element.1678), channel_id=1, source_target_pairs={{0,16},{1,17},{2,18},{3,19},{4,20},{5,21},{6,22},{7,23},{8,24},{9,... | collective-permute-start | bytes 1179656 | tf_op jit(solution)/shard_map/ppermute | solution.py:21
  351.2 16.8 %collective-permute-start.5 = (bf16[512,384]{1,0:T(8,128)(2,1)}, bf16[512,384]{1,0:T(8,128)(2,1)}, u32[]{:S(2)}, u32[]{:S(2)}) collective-permute-start(bf16[512,384]{1,0:T(8,128)(2,1)} %get-tuple-element.1685), channel_id=1, source_target_pairs={{0,16},{1,17},{2,18},{3,19},{4,20},{5,21},{6,22},{7,23},{8,24},{9,... | collective-permute-start | bytes 1179656 | tf_op jit(solution)/shard_map/ppermute | solution.py:21
  401.7 16.7 %collective-permute-start.6 = (bf16[512,384]{1,0:T(8,128)(2,1)}, bf16[512,384]{1,0:T(8,128)(2,1)}, u32[]{:S(2)}, u32[]{:S(2)}) collective-permute-start(bf16[512,384]{1,0:T(8,128)(2,1)} %get-tuple-element.1692), channel_id=1, source_target_pairs={{0,16},{1,17},{2,18},{3,19},{4,20},{5,21},{6,22},{7,23},{8,24},{9,... | collective-permute-start | bytes 1179656 | tf_op jit(solution)/shard_map/ppermute | solution.py:21
  452.4 14.5 %collective-permute-start.7 = (bf16[512,384]{1,0:T(8,128)(2,1)}, bf16[512,384]{1,0:T(8,128)(2,1)}, u32[]{:S(2)}, u32[]{:S(2)}) collective-permute-start(bf16[512,384]{1,0:T(8,128)(2,1)} %get-tuple-element.1699), channel_id=1, source_target_pairs={{0,16},{1,17},{2,18},{3,19},{4,20},{5,21},{6,22},{7,23},{8,24},{9,... | collective-permute-start | bytes 1179656 | tf_op jit(solution)/shard_map/ppermute | solution.py:21
  592.6 152.3 %collective-permute-start.8 = (bf16[512,384]{1,0:T(8,128)(2,1)}, bf16[512,384]{1,0:T(8,128)(2,1)}, u32[]{:S(2)}, u32[]{:S(2)}) collective-permute-start(bf16[512,384]{1,0:T(8,128)(2,1)} %get-tuple-element.1458), channel_id=1, source_target_pairs={{16,0},{17,1},{18,2},{19,3},{20,4},{21,5},{22,6},{23,7},{24,8},{25... | collective-permute-start | bytes 1179656 | tf_op jit(solution)/shard_map/ppermute | solution.py:21
  796.4 17.8 %collective-permute-start.9 = (bf16[512,384]{1,0:T(8,128)(2,1)S(1)}, bf16[512,384]{1,0:T(8,128)(2,1)}, u32[]{:S(2)}, u32[]{:S(2)}) collective-permute-start(bf16[512,384]{1,0:T(8,128)(2,1)S(1)} %get-tuple-element.1454), channel_id=1, source_target_pairs={{16,0},{17,1},{18,2},{19,3},{20,4},{21,5},{22,6},{23,7},{24,8},{25... | collective-permute-start | bytes 1179656 | tf_op jit(solution)/shard_map/ppermute | solution.py:21
  860.5 14.0 %collective-permute-start.10 = (bf16[512,384]{1,0:T(8,128)(2,1)S(1)}, bf16[512,384]{1,0:T(8,128)(2,1)}, u32[]{:S(2)}, u32[]{:S(2)}) collective-permute-start(bf16[512,384]{1,0:T(8,128)(2,1)S(1)} %get-tuple-element.1450), channel_id=1, source_target_pairs={{16,0},{17,1},{18,2},{19,3},{20,4},{21,5},{22,6},{23,7},{24,8},{25... | collective-permute-start | bytes 1179656 | tf_op jit(solution)/shard_map/ppermute | solution.py:21
  924.4 13.6 collective-permute-start.11
  987.9 13.6 collective-permute-start.12
  1046.7 7.8 collective-permute-start.13
  1099.0 7.8 collective-permute-start.14
  1151.2 7.2 collective-permute-start.15
  1176.7 80.4 %reduce-scatter.5.cloned.1.call-start = ((), (), s32[]{:S(2)}) async-start(), calls=%async_computation.4 | async-start | bytes 1105920 | tf_op jit(solution)/shard_map/reduce_scatter | solution.py:281
  1198.3 69.1 %reduce-scatter.11.cloned.1.call-start = ((), (), s32[]{:S(2)}) async-start(), calls=%async_computation.7 | async-start | bytes 1474560 | tf_op jit(solution)/shard_map/reduce_scatter | solution.py:305
  1213.3 85.4 %reduce-scatter.9.cloned.1.call-start = ((), (), s32[]{:S(2)}) async-start(), calls=%async_computation.6 | async-start | bytes 1474560 | tf_op jit(solution)/shard_map/reduce_scatter | solution.py:299
  1234.4 114.7 %all-reduce.13.cloned.1.call-start = ((), (), s32[]{:S(2)}) async-start(), calls=%async_computation.8 | async-start | bytes 1769472 | tf_op jit(solution)/shard_map/psum | solution.py:315
  (296 other events, 1880.9 us)
Sparse Core Ops, SparseCore 0:
  1176.8 29.2 reduce-scatter.6
  1209.0 26.7 reduce-scatter.4
  1238.7 28.6 reduce-scatter.10
  1270.2 28.5 reduce-scatter.8
  1301.2 47.7 all-reduce.12
where the time goes:
time: 1370 us; the launch traced here: 1360 us
  matrix products  645 us (47%)
  other arithmetic  290 us (21%)
  local copies, waits for them, and re-layouts  263 us (19%)
  waiting for transfers between devices  73.6 us (5%)
  starting transfers between devices  41.8 us (3%)
  blocking collectives  29.1 us (2%)
  between operations  20.3 us (1%)
    scatter x60, other arithmetic, per_device(): store.at[index].set(item)  165 us
    dot_general x9, matrix products, layer_forward(): jnp.dot(normed_two, fc1_weight, preferred_element_type=jnp.float32)  97.6 us
    dot_general x9, matrix products, layer_backward(): jnp.einsum('rd,fd->rf', grad_low, fc2_weight, preferred_element_type=jnp....  87.7 us
    dot_general x9, matrix products, layer_backward(): jnp.einsum('bhqk,bkhd->bqhd', grad_raw, key_rows, preferred_element_type=...  57.5 us
    dot_general x9, matrix products, layer_backward(): jnp.einsum('bhqk,bqhd->bkhd', grad_raw, queries, preferred_element_type=j...  57.4 us
    slice x18, local copies, waits for them, and re-layouts, split_heads(): return (shaped[:, :, 0], shaped[:, :, 1], shaped[:, :, 2])  42.8 us
    ppermute x16, starting transfers between devices, from_behind(): lax.ppermute(value, axis, [(source, source + steps) for source in range(f...  41.4 us
    dot_general x9, matrix products, layer_backward(): jnp.einsum('rd,rf->df', normed_two, grad_before, preferred_element_type=j...  39.4 us
  transfers between devices with their start and end apart: 21, of which 4 were waited for; matrix products, arithmetic and copies ran while one was open for 31% of the time, Pallas kernels for 0%

commit v1 on v0

v1 whole, which is shorter than its diff:
```python
import jax
import jax.numpy as jnp
from jax import lax
from jax.experimental import pallas as pl
from jax.experimental.pallas import tpu as pltpu
from jax.sharding import PartitionSpec as P

HD = 64
S = 256
HALF = S // 2
GLOBAL_LEN = 197
LOCAL_LEN = 37
PAIR = 2 * HD
STEP = 2 * S
EPS = 1e-06
SCALE = HD ** (-0.5)
LOG2E = 1.4426950408889634
CHUNK = 512
F32 = jnp.float32
BF16 = jnp.bfloat16
MIB = 1 << 20

ATTN_GAIN, ATTN_SHIFT, Q_BIAS, V_BIAS, PROJ_BIAS, MLP_GAIN, MLP_SHIFT, FC2_BIAS, FC1_BIAS = range(9)
VECTORS = 16


def up16(value):
    return -(-value // 16) * 16


def key_windows(local):
    if not local:
        return ((0, up16(GLOBAL_LEN)),) * 2
    first_end = ((HALF - 1) // LOCAL_LEN + 1) * LOCAL_LEN
    second_start = HALF // LOCAL_LEN * LOCAL_LEN // 16 * 16
    return ((0, up16(first_end)), (second_start, up16(S // LOCAL_LEN * LOCAL_LEN)))


WINDOWS = tuple((local, key_windows(local)) for local in (False, True))
PROB_ROWS = sum(hi - lo for _, windows in WINDOWS for lo, hi in windows)


def prob_offset(pair, sequence, block):
    spans = [hi - lo for _, windows in WINDOWS for lo, hi in windows]
    return pair * PROB_ROWS + sum(spans[: 2 * sequence + block])


def nn(left, right):
    return jnp.dot(left, right, preferred_element_type=F32)


def nt(left, right):
    return lax.dot_general(left, right, (((1,), (1,)), ((), ())), preferred_element_type=F32)


def tn(left, right):
    return lax.dot_general(left, right, (((0,), (0,)), ((), ())), preferred_element_type=F32)


def column_sums(values):
    return jnp.sum(values.reshape(values.shape[0] // 8, 8, values.shape[1]), axis=0)


def normalized(values):
    centered = values - jnp.mean(values, axis=1, keepdims=True)
    inverse = lax.rsqrt(jnp.mean(centered * centered, axis=1, keepdims=True) + EPS)
    return centered * inverse, inverse


def norm_back(scaled, inverse, gain, grad):
    grad_scaled = grad * gain
    first = jnp.mean(grad_scaled, axis=1, keepdims=True)
    second = jnp.mean(grad_scaled * scaled, axis=1, keepdims=True)
    return inverse * (grad_scaled - first - scaled * second)


def crop_of(index):
    total = jnp.zeros_like(index)
    for crop in range(1, S // LOCAL_LEN + 1):
        total = total + (index >= crop * LOCAL_LEN).astype(jnp.int32)
    return total


def mask_bias(local, block, lo, hi):
    if not local:
        rows = lax.broadcasted_iota(jnp.int32, (hi - lo, HALF), 0) + lo
        return jnp.where(rows < GLOBAL_LEN, 0.0, -1e30)
    keys = crop_of(lax.broadcasted_iota(jnp.int32, (hi - lo, HALF), 0) + lo)
    queries = crop_of(lax.broadcasted_iota(jnp.int32, (hi - lo, HALF), 1) + block * HALF)
    return jnp.where(keys == queries, 0.0, -1e30)


def split_pair(rows):
    lane = lax.broadcasted_iota(jnp.int32, (1, PAIR), 1)
    first = (lane < HD).astype(rows.dtype)
    second = (lane >= HD).astype(rows.dtype)
    return jnp.concatenate([rows * first, rows * second], axis=0)


def padded(rows, lo, hi):
    parts = [rows]
    if lo:
        parts = [jnp.zeros((lo, rows.shape[1]), rows.dtype)] + parts
    if hi < S:
        parts = parts + [jnp.zeros((S - hi, rows.shape[1]), rows.dtype)]
    return jnp.concatenate(parts, axis=0) if len(parts) > 1 else rows


def diagonal(values):
    return jnp.concatenate([values[:HD, :HALF], values[HD:, HALF:]], axis=0)


def attend(seg, qkv, prob, ctx_t, width):
    for sequence, (local, windows) in enumerate(WINDOWS):
        base = sequence * S
        valid = seg[0:1, base : base + S] >= 0
        biases = [mask_bias(local, block, lo, hi) for block, (lo, hi) in enumerate(windows)]
        for pair in range(width // PAIR):
            left = pair * PAIR
            queries = qkv[base : base + S, left : left + PAIR]
            keys = qkv[base : base + S, width + left : width + left + PAIR]
            values_t = qkv[base : base + S, 2 * width + left : 2 * width + left + PAIR].T
            for block, (lo, hi) in enumerate(windows):
                at = block * HALF
                valid_here = valid[:, at : at + HALF]
                raw = nt(keys[lo:hi], split_pair(queries[at : at + HALF]))
                bias = biases[block]
                scores = raw * (SCALE * LOG2E) + jnp.concatenate([bias, bias], axis=1)
                exponent = jnp.exp2(scores - jnp.max(scores, axis=0, keepdims=True))
                total = jnp.sum(exponent, axis=0, keepdims=True)
                inverse = jnp.where(jnp.concatenate([valid_here, valid_here], axis=1), 1.0 / total, 0.0)
                probs = (exponent * inverse).astype(BF16)
                offset = prob_offset(pair, sequence, block)
                prob[offset : offset + hi - lo, :] = probs
                context = diagonal(nn(values_t, padded(probs, lo, hi)))
                own = values_t[:, at : at + HALF].astype(F32)
                ctx_t[left : left + PAIR, base + at : base + at + HALF] = jnp.where(
                    valid_here, context, own
                ).astype(BF16)


def attend_back(seg, qkv, prob, grad_context, grad_qkv, width):
    for sequence, (local, windows) in enumerate(WINDOWS):
        base = sequence * S
        valid = (seg[0:1, base : base + S] >= 0).astype(jnp.int32)
        count = jnp.sum(valid, axis=1, keepdims=True)
        padding = lax.broadcasted_iota(jnp.int32, (S, PAIR), 0) >= count
        for pair in range(width // PAIR):
            left = pair * PAIR
            queries = qkv[base : base + S, left : left + PAIR]
            keys = qkv[base : base + S, width + left : width + left + PAIR]
            values = qkv[base : base + S, 2 * width + left : 2 * width + left + PAIR]
            grads = grad_context[base : base + S, left : left + PAIR]
            keys_t = keys.T
            grad_values = jnp.where(padding, grads.astype(F32), 0.0)
            grad_keys = jnp.zeros((S, PAIR), F32)
            for block, (lo, hi) in enumerate(windows):
                at = block * HALF
                grads_here = split_pair(grads[at : at + HALF])
                offset = prob_offset(pair, sequence, block)
                probs_low = prob[offset : offset + hi - lo, :]
                probs = probs_low.astype(F32)
                product = probs * nt(values[lo:hi], grads_here)
                inner = jnp.sum(product, axis=0, keepdims=True)
                grad_raw = (product - probs * inner).astype(BF16)
                grad_values = grad_values + padded(nn(probs_low, grads_here), lo, hi)
                grad_keys = grad_keys + padded(
                    nn(grad_raw, split_pair(queries[at : at + HALF])), lo, hi
                )
                grad_queries = diagonal(nn(keys_t, padded(grad_raw, lo, hi))) * SCALE
                grad_qkv[base + at : base + at + HALF, left : left + PAIR] = grad_queries.astype(
                    BF16
                ).T
            grad_qkv[base : base + S, width + left : width + left + PAIR] = (
                grad_keys * SCALE
            ).astype(BF16)
            grad_qkv[base : base + S, 2 * width + left : 2 * width + left + PAIR] = (
                grad_values.astype(BF16)
            )


def vector(vec, row, count=1):
    parts = [vec[0, row + i : row + i + 1, :] for i in range(count)]
    return parts[0] if count == 1 else jnp.concatenate(parts, axis=1)


def forward(x, seg, weights, kept, y):
    vec, w_qkv, w_proj, w_fc1, w_fc2 = weights
    xhat1, r1, qkv, prob, ctx_t, xhat2, r2, act, dgelu = kept
    rows, width = x.shape
    hidden = w_fc1.shape[2]
    for top in range(0, rows, S):
        here = slice(top, top + S)
        scaled, inverse = normalized(x[here, :].astype(F32))
        xhat1[here, :] = scaled.astype(BF16)
        r1[here, :] = inverse
        normed = (scaled * vector(vec, ATTN_GAIN) + vector(vec, ATTN_SHIFT)).astype(BF16)
        for part, bias in ((0, Q_BIAS), (1, None), (2, V_BIAS)):
            mixed = nn(normed, w_qkv[0, :, part * width : (part + 1) * width])
            if bias is not None:
                mixed = mixed + vector(vec, bias)
            qkv[here, part * width : (part + 1) * width] = mixed.astype(BF16)
    attend(seg, qkv, prob, ctx_t, width)
    for top in range(0, rows, S):
        here = slice(top, top + S)
        after = (
            x[here, :].astype(F32) + tn(ctx_t[:, here], w_proj[0]) + vector(vec, PROJ_BIAS)
        )
        scaled, inverse = normalized(after)
        xhat2[here, :] = scaled.astype(BF16)
        r2[here, :] = inverse
        normed = (scaled * vector(vec, MLP_GAIN) + vector(vec, MLP_SHIFT)).astype(BF16)
        output = after + vector(vec, FC2_BIAS)
        for left in range(0, hidden, CHUNK):
            cols = slice(left, left + CHUNK)
            bias = jnp.concatenate(
                [vec[0, FC1_BIAS + i : FC1_BIAS + i + 1, :] for i in range(hidden // width)], axis=1
            )[:, cols]
            pre = nn(normed, w_fc1[0, :, cols]) + bias
            phi_sum = 0.5 + 0.5 * lax.erf(pre * (0.5**0.5))
            density = jnp.exp2(pre * pre * (-0.5 * LOG2E)) * (1.0 / (2.0 * jnp.pi) ** 0.5)
            active = (pre * phi_sum).astype(BF16)
            act[here, cols] = active
            dgelu[here, cols] = (phi_sum + pre * density).astype(BF16)
            output = output + nn(active, w_fc2[0, cols, :])
        y[here, :] = output.astype(BF16)


def backward(dout, seg, weights, kept, sums, grad_context, grad_qkv, write):
    vec, w_qkv, w_proj, w_fc1, w_fc2 = weights
    xhat1, r1, qkv, prob, ctx_t, xhat2, r2, act, dgelu = kept
    sum_qkv, sum_proj, sum_fc1, sum_fc2, sum_vec = sums
    rows, width = dout.shape
    hidden = w_fc1.shape[2]

    def add(row, values):
        for i in range(values.shape[1] // width):
            at = (row + i) * 8
            sum_vec[at : at + 8, :] += column_sums(values[:, i * width : (i + 1) * width])

    top_grad = dout[...]
    top_wide = top_grad.astype(F32)
    add(FC2_BIAS, top_wide)
    top_t = top_grad.T
    scaled = xhat2[...].astype(F32)
    normed_t = (scaled * vector(vec, MLP_GAIN) + vector(vec, MLP_SHIFT)).astype(BF16).T
    grad_normed = jnp.zeros((rows, width), F32)
    column_parts = []
    for left in range(0, hidden, CHUNK):
        cols = slice(left, left + CHUNK)
        grad_pre = nt(top_grad, w_fc2[0, cols, :]) * dgelu[:, cols].astype(F32)
        column_parts.append(column_sums(grad_pre))
        grad_pre = grad_pre.astype(BF16)
        grad_normed = grad_normed + nt(grad_pre, w_fc1[0, :, cols])
        sum_fc1[:, cols] += nn(normed_t, grad_pre)
        sum_fc2[:, cols] += nn(top_t, act[:, cols])
    columns = jnp.concatenate(column_parts, axis=1)
    for i in range(hidden // width):
        at = (FC1_BIAS + i) * 8
        sum_vec[at : at + 8, :] += columns[:, i * width : (i + 1) * width]
    add(MLP_GAIN, grad_normed * scaled)
    add(MLP_SHIFT, grad_normed)
    grad_after = top_wide + norm_back(scaled, r2[...], vector(vec, MLP_GAIN), grad_normed)
    add(PROJ_BIAS, grad_after)
    grad_branch = grad_after.astype(BF16)
    sum_proj[...] += nn(ctx_t[...], grad_branch)
    grad_context[...] = nt(grad_branch, w_proj[0]).astype(BF16)

    attend_back(seg, qkv, prob, grad_context, grad_qkv, width)

    scaled = xhat1[...].astype(F32)
    normed_t = (scaled * vector(vec, ATTN_GAIN) + vector(vec, ATTN_SHIFT)).astype(BF16).T
    grad_normed = jnp.zeros((rows, width), F32)
    for part, row in ((0, Q_BIAS), (1, None), (2, V_BIAS)):
        cols = slice(part * width, (part + 1) * width)
        piece = grad_qkv[:, cols]
        if row is not None:
            add(row, piece.astype(F32))
        sum_qkv[:, cols] += nn(normed_t, piece)
        grad_normed = grad_normed + nt(piece, w_qkv[0, :, cols])
    add(ATTN_GAIN, grad_normed * scaled)
    add(ATTN_SHIFT, grad_normed)
    write(grad_after + norm_back(scaled, r1[...], vector(vec, ATTN_GAIN), grad_normed))


def write_sums(sums, members, grad_mlp, grad_attn, grad_vec):
    sum_qkv, sum_proj, sum_fc1, sum_fc2, sum_vec = sums
    width, hidden = sum_fc1.shape
    share = width // members
    parts = hidden // width
    for member in range(members):
        rows = slice(member * share, (member + 1) * share)
        for part in range(parts):
            at = (member * parts + part) * share
            grad_mlp[0, at : at + share, :] = sum_fc1[rows, part * width : (part + 1) * width].astype(BF16)
        pieces = (
            (0, 0, sum_proj[rows, :]),
            (0, 1, sum_qkv[rows, :width]),
            (1, 0, sum_qkv[rows, width : 2 * width]),
            (1, 1, sum_qkv[rows, 2 * width :]),
        )
        for half, slot, piece in pieces:
            at = (member * 2 + slot) * share
            grad_attn[half, at : at + share, :] = piece.astype(BF16)
    for part in range(parts):
        cols = slice(part * width, (part + 1) * width)
        grad_mlp[1, cols, :] = sum_fc2[:, cols].astype(BF16).T
    grad_vec[...] = jnp.sum(sum_vec[...].reshape(VECTORS, 8, width), axis=1)


def clear(refs):
    for ref in refs:
        ref[...] = jnp.zeros_like(ref)


def kept_shapes(steps, width, hidden):
    return (
        ((steps * STEP, width), BF16, (STEP, width), 0),
        ((steps * STEP, 1), F32, (STEP, 1), 0),
        ((steps * STEP, 3 * width), BF16, (STEP, 3 * width), 0),
        ((steps * PROB_ROWS * (width // PAIR), S), BF16, (PROB_ROWS * (width // PAIR), S), 0),
        ((width, steps * STEP), BF16, (width, STEP), 1),
        ((steps * STEP, width), BF16, (STEP, width), 0),
        ((steps * STEP, 1), F32, (STEP, 1), 0),
        ((steps * STEP, hidden), BF16, (STEP, hidden), 0),
        ((steps * STEP, hidden), BF16, (STEP, hidden), 0),
    )


def spec(block, axis, first=None):
    if axis == 0:
        if first is None:
            return pl.BlockSpec(block, lambda i, s: (i, 0))
        return pl.BlockSpec(block, lambda i, s: (s[0] * first + i, 0))
    if first is None:
        return pl.BlockSpec(block, lambda i, s: (0, i))
    return pl.BlockSpec(block, lambda i, s: (0, s[0] * first + i))


def weight_specs(weights, layer):
    return [
        pl.BlockSpec((1,) + w.shape[1:], lambda i, s: (layer, 0, 0), pipeline_mode=pl.Buffered(1))
        for w in weights
    ]


def sum_scratch(width, hidden):
    return [
        pltpu.VMEM((width, 3 * width), F32),
        pltpu.VMEM((width, width), F32),
        pltpu.VMEM((width, hidden), F32),
        pltpu.VMEM((width, hidden), F32),
        pltpu.VMEM((8 * VECTORS, width), F32),
    ]


def grad_outs(width, hidden):
    shapes = [((2, hidden, width), BF16), ((2, 2 * width, width), BF16), ((VECTORS, width), F32)]
    outs = [jax.ShapeDtypeStruct(shape, dtype) for shape, dtype in shapes]
    specs = [
        pl.BlockSpec(shape, lambda i, s, n=len(shape): (0,) * n, pipeline_mode=pl.Buffered(1))
        for shape, _ in shapes
    ]
    return outs, specs


def kernel_call(body, steps, in_specs, out_specs, out_shape, scratch, name, flops):
    return pl.pallas_call(
        body,
        grid_spec=pltpu.PrefetchScalarGridSpec(
            num_scalar_prefetch=1,
            grid=(steps,),
            in_specs=in_specs,
            out_specs=out_specs,
            scratch_shapes=scratch,
        ),
        out_shape=out_shape,
        compiler_params=pltpu.CompilerParams(vmem_limit_bytes=60 * MIB),
        cost_estimate=pl.CostEstimate(flops=flops, bytes_accessed=30 * MIB, transcendentals=0),
        name=name,
    )


def first_forward(section, x, seg, weights, steps):
    width, hidden = x.shape[1], weights[3].shape[2]
    shapes = kept_shapes(steps, width, hidden)

    def body(s, x, seg, vec, w_qkv, w_proj, w_fc1, w_fc2, y, *kept):
        forward(x, seg, (vec, w_qkv, w_proj, w_fc1, w_fc2), kept, y)

    return kernel_call(
        body,
        steps,
        [spec((STEP, width), 0, steps), spec((1, STEP), 1, steps)] + weight_specs(weights, 0),
        [spec((STEP, width), 0)] + [spec(block, axis) for _, _, block, axis in shapes],
        [jax.ShapeDtypeStruct((steps * STEP, width), BF16)]
        + [jax.ShapeDtypeStruct(shape, dtype) for shape, dtype, _, _ in shapes],
        [],
        "forward_first",
        steps * STEP * 4000000,
    )(section, x, seg, *weights)


def second_layer(section, x, seg, cotangent, weights, steps, members):
    width, hidden = x.shape[1], weights[3].shape[2]
    shapes = kept_shapes(steps, width, hidden)
    outs, specs = grad_outs(width, hidden)

    def body(s, x, seg, cot, vec, w_qkv, w_proj, w_fc1, w_fc2, y, g, g_mlp, g_attn, g_vec, *scratch):
        sums, kept, (grad_context, grad_qkv) = scratch[:5], scratch[5:-2], scratch[-2:]
        weights = (vec, w_qkv, w_proj, w_fc1, w_fc2)
        step = pl.program_id(0)

        @pl.when(step == 0)
        def _():
            clear(sums)

        forward(x, seg, weights, kept, y)

        def write(values):
            g[...] = values.astype(BF16)

        backward(cot, seg, weights, kept, sums, grad_context, grad_qkv, write)

        @pl.when(step == steps - 1)
        def _():
            write_sums(sums, members, g_mlp, g_attn, g_vec)

    rows = jax.ShapeDtypeStruct((steps * STEP, width), BF16)
    return kernel_call(
        body,
        steps,
        [spec((STEP, width), 0), spec((1, STEP), 1, steps), spec((STEP, width), 0, steps)]
        + weight_specs(weights, 1),
        [spec((STEP, width), 0), spec((STEP, width), 0)] + specs,
        [rows, rows] + outs,
        sum_scratch(width, hidden)
        + [pltpu.VMEM(block, dtype) for _, dtype, block, _ in shapes]
        + [pltpu.VMEM((STEP, width), BF16), pltpu.VMEM((STEP, 3 * width), BF16)],
        "second_layer",
        steps * STEP * 12000000,
    )(section, x, seg, cotangent, *weights)


def first_backward(section, seg, dout, kept, weights, steps, members):
    width, hidden = dout.shape[1], weights[3].shape[2]
    shapes = kept_shapes(steps, width, hidden)
    outs, specs = grad_outs(width, hidden)

    def body(s, seg, dout, vec, w_qkv, w_proj, w_fc1, w_fc2, *refs):
        kept, (g, g_mlp, g_attn, g_vec) = refs[:9], refs[9:13]
        sums, (grad_context, grad_qkv) = refs[13:18], refs[18:]
        weights = (vec, w_qkv, w_proj, w_fc1, w_fc2)
        step = pl.program_id(0)

        @pl.when(step == 0)
        def _():
            clear(sums)

        def write(values):
            g[...] = values

        backward(dout, seg, weights, kept, sums, grad_context, grad_qkv, write)

        @pl.when(step == steps - 1)
        def _():
            write_sums(sums, members, g_mlp, g_attn, g_vec)

    return kernel_call(
        body,
        steps,
        [spec((1, STEP), 1, steps), spec((STEP, width), 0)]
        + weight_specs(weights, 0)
        + [spec(block, axis) for _, _, block, axis in shapes],
        [spec((STEP, width), 0)] + specs,
        [jax.ShapeDtypeStruct((steps * STEP, width), F32)] + outs,
        sum_scratch(width, hidden)
        + [pltpu.VMEM((STEP, width), BF16), pltpu.VMEM((STEP, 3 * width), BF16)],
        "backward_first",
        steps * STEP * 8000000,
    )(section, seg, dout, *weights, *kept)


def pack_vectors(vectors, width):
    flat = jnp.concatenate([v.reshape(-1, width) for v in vectors], axis=0)
    return jnp.pad(flat, ((0, VECTORS - flat.shape[0]), (0, 0)))[None]


def local_part(section, tokens, segment, cotangent, weights, steps, members):
    y0, *kept = first_forward(section, tokens, segment, weights, steps)
    y1, g1, *grads1 = second_layer(section, y0, segment, cotangent, weights, steps, members)
    g0, *grads0 = first_backward(section, segment, g1, kept, weights, steps, members)
    return y0, y1, g0, g1, grads0, grads1


def swap(value):
    return lax.ppermute(value, "section", [(0, 1), (1, 0)])


def gather_weights(own, here):
    other = [swap(w) for w in own]
    return [
        jnp.concatenate([jnp.where(here, mine, got), jnp.where(here, got, mine)], axis=0)
        for mine, got in zip(own, other)
    ]


def per_device(
    tokens,
    segment,
    cotangent,
    attn_gain,
    attn_shift,
    qkv_weight,
    qv_bias,
    proj_weight,
    proj_bias,
    mlp_gain,
    mlp_shift,
    fc1_weight,
    fc1_bias,
    fc2_weight,
    fc2_bias,
):
    section = lax.axis_index("section")
    here = section == 0
    members = lax.axis_size("member")
    rows, width = tokens.shape
    steps = rows // 2 // STEP
    vec = pack_vectors(
        (attn_gain, attn_shift, qv_bias, proj_bias, mlp_gain, mlp_shift, fc2_bias, fc1_bias), width
    )
    weights = gather_weights([vec, qkv_weight, proj_weight, fc1_weight, fc2_weight], here)
    y0, y1, g0, g1, grads0, grads1 = local_part(
        section.reshape(1).astype(jnp.int32), tokens, segment.reshape(1, rows), cotangent, weights, steps, members
    )

    def joined(mine, got):
        return jnp.where(here, jnp.concatenate([mine, got]), jnp.concatenate([got, mine]))[None]

    def paired(first, second):
        return joined(jnp.where(here, first, second), swap(jnp.where(here, second, first)))

    activations = paired(y0, y1)
    g0_low = g0.astype(BF16)
    in_grads = joined(
        jnp.where(here, g0, g1.astype(F32)), swap(jnp.where(here, g1, g0_low)).astype(F32)
    )

    def reduced(first, second):
        total = lax.psum_scatter(jnp.stack([first, second]), "section", scatter_dimension=0, tiled=True)
        total = total.reshape(2, members, -1, width)
        total = lax.psum_scatter(total, "member", scatter_dimension=1, tiled=True)
        return lax.psum(total, "group")[:, 0].astype(F32)

    mlp = reduced(grads0[0], grads1[0])
    attn = reduced(grads0[1], grads1[1])
    vectors = lax.psum(
        jnp.where(here, grads0[2] + swap(grads0[2]), grads1[2] + swap(grads1[2])), ("member", "group")
    )
    member = lax.axis_index("member")
    hidden = fc1_weight.shape[2]
    share = width // members
    fc1 = mlp[0].reshape(hidden // width, share, width).transpose(1, 0, 2).reshape(share, hidden)
    proj = attn[0, :share]
    qkv = jnp.concatenate([attn[0, share:], attn[1, :share], attn[1, share:]], axis=1)

    def piece(row, count=1):
        flat = vectors[row : row + count].reshape(-1)
        size = flat.shape[0] // members
        return lax.dynamic_slice(flat, (member * size,), (size,))[None]

    return (
        activations,
        in_grads,
        piece(ATTN_GAIN),
        piece(ATTN_SHIFT),
        qkv[None],
        piece(Q_BIAS, 2),
        proj[None],
        piece(PROJ_BIAS),
        piece(MLP_GAIN),
        piece(MLP_SHIFT),
        fc1[None],
        piece(FC1_BIAS, hidden // width),
        mlp[1][None],
        piece(FC2_BIAS),
    )


def solution(mesh):
    row = P("section", None)
    mat = P("section", None, None)
    tokens = P(("group", "member"), None)
    split = P("section", "member")
    split_mat = P("section", "member", None)
    stacked = P("section", ("group", "member"), None)
    return jax.shard_map(
        per_device,
        mesh=mesh,
        in_specs=(
            tokens, P(("group", "member")), tokens,
            row, row, mat, row, mat, row, row, row, mat, row, mat, row,
        ),
        out_specs=(
            stacked, stacked,
            split, split, split_mat, split, split_mat, split, split, split, split_mat, split, split_mat, split,
        ),
        check_vma=False,
    )
```

time: 1370 us -> 386 us (0.28)
  matrix products: 645 us -> 0 us
  other arithmetic: 290 us -> 38.6 us
  local copies, waits for them, and re-layouts: 263 us -> 16 us
  Pallas kernels: 0 us -> 148 us
  blocking collectives: 29.1 us -> 78.6 us
  starting transfers between devices: 41.8 us -> 2.45 us
    dot_general x171 -> x0, matrix products: 645 us -> none  [the longest x9 97.6 us: layer_forward(): jnp.dot(normed_two, fc1_weight, preferred_element_type=jnp.float32)]
    scatter x69 -> x0, other arithmetic: 193 us -> none  [the longest x60 165 us: per_device(): store.at[index].set(item)]
    pallas_call x0 -> x3, Pallas kernels: none -> 148 us  [the longest x1 70.1 us: second_layer(): kernel_call(body, steps, [spec((STEP, width), 0), spec((1, STEP), 1, step...]
    psum x1, blocking collectives: 11.9 us -> 78.6 us  [per_device(): lax.psum(jnp.where(here, grads0[2] + swap(grads0[2]), grads1[2] + swap(gr...]
    another operation x54 -> x1, local copies, waits for them, and re-layouts: 66.5 us -> 1.05 us  [per_device(): fc1[None]]
    reduce_sum x66 -> x0, other arithmetic: 58.6 us -> none  [the longest x9 16.6 us: layer_backward(): grad_proj_bias = jnp.sum(grad_branch.astype(jnp.float32), axis=0)]
    slice x46 -> x6, local copies, waits for them, and re-layouts: 50.7 us -> 2.59 us  [the longest x1 1.05 us: per_device(): mlp[0].reshape(hidden // width, share, width).transpose(1, 0, 2)]
    reshape x19 -> x5, local copies, waits for them, and re-layouts: 41.9 us -> 2.51 us  [the longest x1 2.47 us: reduced(): total = total.reshape(2, members, -1, width)]
  transfers between devices with their start and end apart: 21 -> 14, of which waited for: 4 -> 6; matrix products, arithmetic and copies ran while one was open for 31% -> 11% of each run, Pallas kernels for 0% -> 0%
where the time goes in v1:
time: 386 us; the launch traced here: 379 us
  Pallas kernels  148 us (38%)
  waiting for transfers between devices  81.4 us (21%)
  blocking collectives  78.6 us (20%)
  other arithmetic  38.6 us (10%)
  local copies, waits for them, and re-layouts  16 us (4%)
  between operations  14.4 us (4%)
    psum x1, blocking collectives, per_device(): lax.psum(jnp.where(here, grads0[2] + swap(grads0[2]), grads1[2] + swap(gr...  78.6 us
    pallas_call x1, Pallas kernels, second_layer(): kernel_call(body, steps, [spec((STEP, width), 0), spec((1, STEP), 1, step...  70.1 us
    pallas_call x1, Pallas kernels, first_backward(): kernel_call(body, steps, [spec((1, STEP), 1, steps), spec((STEP, width),...  42.9 us
    psum x1, waiting for transfers between devices, reduced(): return lax.psum(total, 'group')[:, 0].astype(F32)  41.1 us
    pallas_call x1, Pallas kernels, first_forward(): kernel_call(body, steps, [spec((STEP, width), 0, steps), spec((1, STEP),...  34.5 us
    reduce_scatter x2, waiting for transfers between devices, reduced(): lax.psum_scatter(jnp.stack([first, second]), 'section', scatter_dimension...  21.3 us
    unnamed x7, waiting for transfers between devices  16.1 us
    select_n x2, other arithmetic, joined(): jnp.where(here, jnp.concatenate([mine, got]), jnp.concatenate([got, mine]))  8.94 us
  transfers between devices with their start and end apart: 14, of which 6 were waited for; matrix products, arithmetic and copies ran while one was open for 11% of the time, Pallas kernels for 0%

profile of v1, /device:TPU:0, one launch (start us, length us, event | category | flops | bytes accessed | tf_op | source)
XLA Modules:
  0.0 379.1 jit_solution(2787724977932507219)
XLA Ops:
  13.5 2.4 collective-permute-done.2
  17.8 1.3 broadcast_select_fusion.6
  19.2 1.4 pad_maximum_fusion.4.w_qkv
  21.0 1.6 pad_maximum_fusion.1.w_fc1
  22.8 1.7 pad_maximum_fusion.2.w_fc2
  24.5 34.5 %forward_first.1 = (bf16[2048,384]{1,0:T(8,128)(2,1)}, bf16[2048,384]{1,0:T(8,128)(2,1)}, f32[2048,1]{1,0:T(8,128)}, bf16[2048,1152]{1,0:T(8,128)(2,1)}, bf16[84...) custom-call(s32[1]{0:T(128)} %bitcast.6.s, ...), custom_call_target="tpu_custom_call" | custom-call | flops 8192000000 | bytes 31457280 | tf_op jit(solution)/shard_map/forward_first/pallas_call | solution.py:391
  59.0 70.1 %second_layer.1 = (bf16[2048,384]{1,0:T(8,128)(2,1)}, bf16[2048,384]{1,0:T(8,128)(2,1)}, bf16[2,1536,384]{2,1,0:T(8,128)(2,1)}, bf16[2,768,384]{2,1,0:T(8,128)(2,1)}, f32[16,384]{1,0:T(8,128)}) custom-call(s32[1]{0:T(128)} %bitcast.6.s, bf16[2048,384]{1,0:T(8,128)(2,1)} %get-tuple-element.33.x, s32[1,4096]{1,0:T(1,128)} %bitcast.54, bf16[4096,384]{1,0:T(8,128)(2,1)} %cot.1, ...), custom_call_target="tpu_custom_call" | custom-call | flops 24576000000 | bytes 31457280 | tf_op jit(solution)/shard_map/second_layer/pallas_call | solution.py:430
  129.2 42.9 %backward_first.1 = (f32[2048,384]{1,0:T(8,128)}, bf16[2,1536,384]{2,1,0:T(8,128)(2,1)}, bf16[2,768,384]{2,1,0:T(8,128)(2,1)}, f32[16,384]{1,0:T(8,128)}) custom-call(s32[1]{0:T(128)} %bitcast.6.s, s32[1,4096]{1,0:T(1,128)} %bitcast.55, bf16[2048,384]{1,0:T(8,128)(2,1)} %get-tuple-element.35.dout, f32[2,16,384]{2,1,0:T(8,128)} %pad_maximum_fusion.6.vec, ...), custom_call_target="tpu_custom_call" | custom-call | flops 16384000000 | bytes 31457280 | tf_op jit(solution)/shard_map/backward_first/pallas_call | solution.py:469
  172.1 4.4 %pad_maximum_fusion = bf16[2,2,1536,384]{3,2,1,0:T(8,128)(2,1)} fusion(bf16[1,2,1536,384]{3,2,1,0:T(8,128)(2,1)S(1)} %bitcast.46, bf16[1,2,1536,384]{3,2,1,0:T(8,128)(2,1)} %bitcast.47), kind=kLoop, calls=%fused_computation.1 | loop fusion | flops 2359296 | bytes 9437184 | tf_op jit(solution)/shard_map/stack | solution.py:551
  176.6 1.2 copy-done.6
  178.1 1.7 pad_maximum_fusion.3
  179.9 12.0 %reduce-scatter.11.cloned.1.call-done = bf16[1,2,1536,384]{3,2,1,0:T(8,128)(2,1)} async-done(((bf16[2,2,1536,384]{3,2,1,0:T(8,128)(2,1)}), bf16[1,2,1536,384]{3,2,1,0:T(8,128)(2,1)}) %reduce-scatter.11.cloned.1.call-update) | async-done | bytes 2359312 | tf_op jit(solution)/shard_map/reduce_scatter | solution.py:551
  193.1 2.9 convert_select_fusion
  196.0 9.3 %reduce-scatter.9.cloned.1.call-done = bf16[1,2,768,384]{3,2,1,0:T(8,128)(2,1)} async-done(((bf16[2,2,768,384]{3,2,1,0:T(8,128)(2,1)}), bf16[1,2,768,384]{3,2,1,0:T(8,128)(2,1)}) %reduce-scatter.9.cloned.1.call-update) | async-done | bytes 1179664 | tf_op jit(solution)/shard_map/reduce_scatter | solution.py:551
  205.3 2.5 copy.31
  207.9 4.0 %select_bitcast_fusion.1 = (bf16[1,2048,384]{2,1,0:T(8,128)(2,1)}, bf16[2048,384]{1,0:T(8,128)(2,1)}) fusion(bf16[2048,384]{1,0:T(8,128)(2,1)} %get-tuple-element.33.x, bf16[2048,384]{1,0:T(8,128)(2,1)} %get-tuple-element.34, pred[]{:T(512)S(6)} %eq.3), kind=kLoop, calls=%fused_computation.10 | loop fusion | flops 1572864 | bytes 6291457 | tf_op jit(solution)/shard_map/concatenate | solution.py:539
  212.0 2.0 select_bitcast_fusion
  214.1 78.6 %psum.21 = f32[16,384]{1,0:T(8,128)S(1)} all-reduce(f32[16,384]{1,0:T(8,128)S(1)} %add_select_fusion), channel_id=1, replica_groups=mesh['section'=2,'group'=4,'member'=4] {'member','group'}, use_global_device_ids=true, to_apply=%region_0.1 | all-reduce | flops 6144 | bytes 49152 | tf_op jit(solution)/shard_map/psum | solution.py:558
  295.8 1.6 bitcast_convert_fusion
  297.4 2.6 constant_dynamic-slice_fusion.6
  300.0 16.0 %reduce-scatter.13.cloned.1.call-done = bf16[2,1,192,384]{3,2,0,1:T(8,128)(2,1)} async-done(((bf16[2,4,192,384]{3,2,0,1:T(8,128)(2,1)}), bf16[2,1,192,384]{3,2,0,1:T(8,128)(2,1)}) %reduce-scatter.13.cloned.1.call-update) | async-done | bytes 294928
  316.0 5.4 %maximum_select_fusion.1 = bf16[1,4096,384]{2,1,0:T(8,128)(2,1)} fusion(bf16[1,2048,384]{2,1,0:T(8,128)(2,1)} %bitcast.10, bf16[1,2048,384]{2,1,0:T(8,128)(2,1)} %get-tuple-element.54, pred[]{:T(512)S(6)} %eq.3), kind=kLoop, calls=%fused_computation.2 | loop fusion | flops 14155776 | bytes 6291457 | tf_op jit(solution)/shard_map/jit(_where)/select_n | solution.py:539
  321.4 3.5 maximum_select_fusion
  325.0 41.1 %all-reduce.9.cloned.1.call-done = (bf16[2,192,384]{2,1,0:T(8,128)(2,1)}, bf16[2,1,384,384]{3,2,1,0:T(8,128)(2,1)}) async-done(((bf16[2,192,384]{2,1,0:T(8,128)(2,1)}, bf16[2,1,384,384]{3,2,1,0:T(8,128)(2,1)}), (bf16[2,192,384]{2,1,0:T(8,128)(2,1)}, bf16[2,1,384,384]{3,2,1,0:T(8,128)(2,1)})) %all-reduce.9.cloned.1.call-update) | async-done | bytes 884752 | tf_op jit(solution)/shard_map/psum | solution.py:554
  (89 shorter events, 19.9 us)
Async XLA Ops:
  7.2 10.7 %copy-start.8 = (bf16[1,384,1152]{2,1,0:T(8,128)(2,1)S(1)}, bf16[1,384,1152]{2,1,0:T(8,128)(2,1)}, u32[]{:S(2)}) copy-start(bf16[1,384,1152]{2,1,0:T(8,128)(2,1)} %param.20) | copy-start | bytes 2654212
  7.2 184.7 %reduce-scatter.11.cloned.1.call-start = ((), (), s32[]{:S(2)}) async-start(), calls=%async_computation.4 | async-start | bytes 7077888 | tf_op jit(solution)/shard_map/reduce_scatter | solution.py:551
  7.2 10.6 %collective-permute-start.1 = (bf16[1,384,1152]{2,1,0:T(8,128)(2,1)}, bf16[1,384,1152]{2,1,0:T(8,128)(2,1)}, u32[]{:S(2)}, u32[]{:S(2)}) collective-permute-start(bf16[1,384,1152]{2,1,0:T(8,128)(2,1)} %param.20), channel_id=1, source_target_pairs={{0,16},{16,0},{1,17},{17,1},{2,18},{18,2},{3,19},{19,3},{4,20},{20... | collective-permute-start | bytes 2654216 | tf_op jit(solution)/shard_map/ppermute | solution.py:497
  10.6 1.5 collective-permute-start
  10.8 9.9 %collective-permute-start.3 = (bf16[1,384,1536]{2,1,0:T(8,128)(2,1)}, bf16[1,384,1536]{2,1,0:T(8,128)(2,1)S(1)}, u32[]{:S(2)}, u32[]{:S(2)}) collective-permute-start(bf16[1,384,1536]{2,1,0:T(8,128)(2,1)} %param.26), channel_id=1, source_target_pairs={{0,16},{16,0},{1,17},{17,1},{2,18},{18,2},{3,19},{19,3},{4,20},{20... | collective-permute-start | bytes 3538952 | tf_op jit(solution)/shard_map/ppermute | solution.py:497
  11.1 11.5 %collective-permute-start.4 = (bf16[1,1536,384]{2,1,0:T(8,128)(2,1)}, bf16[1,1536,384]{2,1,0:T(8,128)(2,1)S(1)}, u32[]{:S(2)}, u32[]{:S(2)}) collective-permute-start(bf16[1,1536,384]{2,1,0:T(8,128)(2,1)} %param.28), channel_id=1, source_target_pairs={{0,16},{16,0},{1,17},{17,1},{2,18},{18,2},{3,19},{19,3},{4,20},{20... | collective-permute-start | bytes 3538952 | tf_op jit(solution)/shard_map/ppermute | solution.py:497
  11.3 4.7 %collective-permute-start.2 = (bf16[1,384,384]{2,1,0:T(8,128)(2,1)}, bf16[1,384,384]{2,1,0:T(8,128)(2,1)S(1)}, u32[]{:S(2)}, u32[]{:S(2)}) collective-permute-start(bf16[1,384,384]{2,1,0:T(8,128)(2,1)} %param.22), channel_id=1, source_target_pairs={{0,16},{16,0},{1,17},{17,1},{2,18},{18,2},{3,19},{19,3},{4,20},{20... | collective-permute-start | bytes 884744 | tf_op jit(solution)/shard_map/ppermute | solution.py:497
  19.2 1.7 copy-start.4
  129.2 42.9 %copy-start.3 = (bf16[2,1536,384]{2,1,0:T(8,128)(2,1)S(1)}, bf16[2,1536,384]{2,1,0:T(8,128)(2,1)}, u32[]{:S(2)}) copy-start(bf16[2,1536,384]{2,1,0:T(8,128)(2,1)} %get-tuple-element.51) | copy-start | bytes 7077892
  176.5 28.8 %reduce-scatter.9.cloned.1.call-start = ((), (), s32[]{:S(2)}) async-start(), calls=%async_computation.3 | async-start | bytes 3538944 | tf_op jit(solution)/shard_map/reduce_scatter | solution.py:551
  179.8 12.2 %copy-start.13 = (u32[32]{0:T(128)S(1)}, u32[32]{0:T(128)}, u32[]{:S(2)}) copy-start(u32[32]{0:T(128)} %constant.46) | copy-start | bytes 388
  179.8 12.7 %copy-start.12 = (f32[16,384]{1,0:T(8,128)S(1)}, f32[16,384]{1,0:T(8,128)}, u32[]{:S(2)}) copy-start(f32[16,384]{1,0:T(8,128)} %get-tuple-element.46) | copy-start | bytes 73732
  179.8 12.9 %copy-start.11 = (f32[16,384]{1,0:T(8,128)S(1)}, f32[16,384]{1,0:T(8,128)}, u32[]{:S(2)}) copy-start(f32[16,384]{1,0:T(8,128)} %get-tuple-element.47) | copy-start | bytes 73732
  179.8 13.3 %copy-start = (f32[2048,384]{1,0:T(8,128)S(1)}, f32[2048,384]{1,0:T(8,128)}, u32[]{:S(2)}) copy-start(f32[2048,384]{1,0:T(8,128)} %get-tuple-element.45) | copy-start | bytes 9437188
  179.9 117.5 %all-reduce.7.cloned.1.call-start = ((), (), s32[]{:S(2)}) async-start(), calls=%async_computation.5 | async-start | bytes 4718592
  191.9 124.1 %reduce-scatter.13.cloned.1.call-start = ((), (), s32[]{:S(2)}) async-start(), calls=%async_computation.6 | async-start | bytes 1474560
  192.6 21.5 %collective-permute-start.7 = (f32[16,384]{1,0:T(8,128)S(1)}, f32[16,384]{1,0:T(8,128)S(1)}, u32[]{:S(2)}, u32[]{:S(2)}) collective-permute-start(f32[16,384]{1,0:T(8,128)S(1)} %copy-done.12), channel_id=1, source_target_pairs={{0,16},{16,0},{1,17},{17,1},{2,18},{18,2},{3,19},{19,3},{4,20},{20... | collective-permute-start | bytes 73736 | tf_op jit(solution)/shard_map/ppermute | solution.py:497
  192.7 21.3 %collective-permute-start.8 = (f32[16,384]{1,0:T(8,128)S(1)}, f32[16,384]{1,0:T(8,128)S(1)}, u32[]{:S(2)}, u32[]{:S(2)}) collective-permute-start(f32[16,384]{1,0:T(8,128)S(1)} %copy-done.11), channel_id=1, source_target_pairs={{0,16},{16,0},{1,17},{17,1},{2,18},{18,2},{3,19},{19,3},{4,20},{20... | collective-permute-start | bytes 73736 | tf_op jit(solution)/shard_map/ppermute | solution.py:497
  196.0 99.8 %collective-permute-start.6 = (bf16[2048,384]{1,0:T(8,128)(2,1)}, bf16[2048,384]{1,0:T(8,128)(2,1)}, u32[]{:S(2)}, u32[]{:S(2)}) collective-permute-start(bf16[2048,384]{1,0:T(8,128)(2,1)} %convert_select_fusion), channel_id=1, source_target_pairs={{0,16},{16,0},{1,17},{17,1},{2,18},{18,2},{3,19},{19,3},{4,20},{20... | collective-permute-start | bytes 4718600 | tf_op jit(solution)/shard_map/ppermute | solution.py:497
  207.8 158.3 %all-reduce.9.cloned.1.call-start = ((), (), s32[]{:S(2)}) async-start(), calls=%async_computation.7 | async-start | bytes 1769472 | tf_op jit(solution)/shard_map/psum | solution.py:554
  207.9 4.2 %copy-start.2 = (bf16[2048,384]{1,0:T(8,128)(2,1)S(1)}, bf16[2048,384]{1,0:T(8,128)(2,1)}, u32[]{:S(2)}) copy-start(bf16[2048,384]{1,0:T(8,128)(2,1)} %get-tuple-element.35.dout) | copy-start | bytes 4718596
  211.8 104.2 %collective-permute-start.5 = (bf16[2048,384]{1,0:T(8,128)(2,1)}, bf16[2048,384]{1,0:T(8,128)(2,1)}, u32[]{:S(2)}, u32[]{:S(2)}) collective-permute-start(bf16[2048,384]{1,0:T(8,128)(2,1)} %get-tuple-element.55), channel_id=1, source_target_pairs={{0,16},{16,0},{1,17},{17,1},{2,18},{18,2},{3,19},{19,3},{4,20},{20... | collective-permute-start | bytes 4718600 | tf_op jit(solution)/shard_map/ppermute | solution.py:497
  316.0 5.4 %copy-start.1 = (f32[1,2048,384]{2,1,0:T(8,128)S(1)}, f32[1,2048,384]{2,1,0:T(8,128)}, u32[]{:S(2)}) copy-start(f32[1,2048,384]{2,1,0:T(8,128)} %select_bitcast_fusion) | copy-start | bytes 9437188
  366.1 2.2 copy-start.9
  (4 other events, 5.3 us)
Sparse Core Ops, SparseCore 0:
  176.6 15.2 reduce-scatter.10
  194.2 11.0 reduce-scatter.8
  208.4 75.9 all-reduce.6
  287.5 28.4 reduce-scatter.12
  319.0 47.0 all-reduce.8

commit v2 on v1

--- a/solution.py
+++ b/solution.py
@@ -19,6 +19,7 @@
 F32 = jnp.float32
 BF16 = jnp.bfloat16
 MIB = 1 << 20
+MESH = pl.DeviceIdType.MESH
 
 ATTN_GAIN, ATTN_SHIFT, Q_BIAS, V_BIAS, PROJ_BIAS, MLP_GAIN, MLP_SHIFT, FC2_BIAS, FC1_BIAS = range(9)
 VECTORS = 16
@@ -226,18 +227,22 @@
         y[here, :] = output.astype(BF16)
 
 
-def backward(dout, seg, weights, kept, sums, grad_context, grad_qkv, write):
-    vec, w_qkv, w_proj, w_fc1, w_fc2 = weights
-    xhat1, r1, qkv, prob, ctx_t, xhat2, r2, act, dgelu = kept
-    sum_qkv, sum_proj, sum_fc1, sum_fc2, sum_vec = sums
-    rows, width = dout.shape
-    hidden = w_fc1.shape[2]
-
+def adder(sum_vec, width):
     def add(row, values):
         for i in range(values.shape[1] // width):
             at = (row + i) * 8
             sum_vec[at : at + 8, :] += column_sums(values[:, i * width : (i + 1) * width])
 
+    return add
+
+
+def backward_mlp(dout, weights, kept, sums, write):
+    vec, _, w_proj, w_fc1, w_fc2 = weights
+    ctx_t, xhat2, r2, act, dgelu = kept
+    _, sum_proj, sum_fc1, sum_fc2, sum_vec = sums
+    rows, width = dout.shape
+    hidden = w_fc1.shape[2]
+    add = adder(sum_vec, width)
     top_grad = dout[...]
     top_wide = top_grad.astype(F32)
     add(FC2_BIAS, top_wide)
@@ -264,10 +269,16 @@
     add(PROJ_BIAS, grad_after)
     grad_branch = grad_after.astype(BF16)
     sum_proj[...] += nn(ctx_t[...], grad_branch)
-    grad_context[...] = nt(grad_branch, w_proj[0]).astype(BF16)
-
+    write(grad_after, nt(grad_branch, w_proj[0]).astype(BF16))
+
+
+def backward_attn(grad_after, grad_context, seg, weights, kept, sums, grad_qkv, write):
+    vec, w_qkv, _, _, _ = weights
+    xhat1, r1, qkv, prob = kept
+    sum_qkv, sum_vec = sums[0], sums[4]
+    rows, width = grad_after.shape
+    add = adder(sum_vec, width)
     attend_back(seg, qkv, prob, grad_context, grad_qkv, width)
-
     scaled = xhat1[...].astype(F32)
     normed_t = (scaled * vector(vec, ATTN_GAIN) + vector(vec, ATTN_SHIFT)).astype(BF16).T
     grad_normed = jnp.zeros((rows, width), F32)
@@ -280,32 +291,47 @@
         grad_normed = grad_normed + nt(piece, w_qkv[0, :, cols])
     add(ATTN_GAIN, grad_normed * scaled)
     add(ATTN_SHIFT, grad_normed)
-    write(grad_after + norm_back(scaled, r1[...], vector(vec, ATTN_GAIN), grad_normed))
-
-
-def write_sums(sums, members, grad_mlp, grad_attn, grad_vec):
-    sum_qkv, sum_proj, sum_fc1, sum_fc2, sum_vec = sums
-    width, hidden = sum_fc1.shape
+    write(grad_after[...] + norm_back(scaled, r1[...], vector(vec, ATTN_GAIN), grad_normed))
+
+
+def half_rows(share):
+    return up16(share // 2)
+
+
+def write_blocks(sums, members, blocks, out):
+    sum_qkv, sum_proj, sum_fc1, sum_fc2, _ = sums
+    width = sum_proj.shape[0]
     share = width // members
-    parts = hidden // width
-    for member in range(members):
-        rows = slice(member * share, (member + 1) * share)
-        for part in range(parts):
-            at = (member * parts + part) * share
-            grad_mlp[0, at : at + share, :] = sum_fc1[rows, part * width : (part + 1) * width].astype(BF16)
-        pieces = (
-            (0, 0, sum_proj[rows, :]),
-            (0, 1, sum_qkv[rows, :width]),
-            (1, 0, sum_qkv[rows, width : 2 * width]),
-            (1, 1, sum_qkv[rows, 2 * width :]),
-        )
-        for half, slot, piece in pieces:
-            at = (member * 2 + slot) * share
-            grad_attn[half, at : at + share, :] = piece.astype(BF16)
-    for part in range(parts):
-        cols = slice(part * width, (part + 1) * width)
-        grad_mlp[1, cols, :] = sum_fc2[:, cols].astype(BF16).T
-    grad_vec[...] = jnp.sum(sum_vec[...].reshape(VECTORS, 8, width), axis=1)
+    size = half_rows(share)
+    parts = sum_fc1.shape[1] // width
+
+    def store(rows, member, block):
+        at = (member * len(blocks) + blocks.index(block)) * size
+        out[0, at : at + size, :] = rows[:size]
+        out[1, at : at + size, :] = rows[share - size :]
+
+    for block in blocks:
+        if block < parts:
+            whole = sum_fc1[:, block * width : (block + 1) * width]
+        elif block < 2 * parts:
+            chunk = block - parts
+            whole = sum_fc2[:, chunk * width : (chunk + 1) * width].astype(BF16).T
+            for place in range(members):
+                row = chunk * members + place
+                store(whole[place * share : (place + 1) * share], row // parts, parts + row % parts)
+            continue
+        elif block == 2 * parts:
+            whole = sum_proj[...]
+        else:
+            part = block - 2 * parts - 1
+            whole = sum_qkv[:, part * width : (part + 1) * width]
+        whole = whole.astype(BF16)
+        for member in range(members):
+            store(whole[member * share : (member + 1) * share], member, block)
+
+
+def vector_sums(sum_vec):
+    return jnp.sum(sum_vec[...].reshape(VECTORS, 8, sum_vec.shape[1]), axis=1).astype(BF16)
 
 
 def clear(refs):
@@ -352,16 +378,6 @@
         pltpu.VMEM((width, hidden), F32),
         pltpu.VMEM((8 * VECTORS, width), F32),
     ]
-
-
-def grad_outs(width, hidden):
-    shapes = [((2, hidden, width), BF16), ((2, 2 * width, width), BF16), ((VECTORS, width), F32)]
-    outs = [jax.ShapeDtypeStruct(shape, dtype) for shape, dtype in shapes]
-    specs = [
-        pl.BlockSpec(shape, lambda i, s, n=len(shape): (0,) * n, pipeline_mode=pl.Buffered(1))
-        for shape, _ in shapes
-    ]
-    return outs, specs
 
 
 def kernel_call(body, steps, in_specs, out_specs, out_shape, scratch, name, flops):
@@ -404,10 +420,11 @@
 def second_layer(section, x, seg, cotangent, weights, steps, members):
     width, hidden = x.shape[1], weights[3].shape[2]
     shapes = kept_shapes(steps, width, hidden)
-    outs, specs = grad_outs(width, hidden)
-
-    def body(s, x, seg, cot, vec, w_qkv, w_proj, w_fc1, w_fc2, y, g, g_mlp, g_attn, g_vec, *scratch):
-        sums, kept, (grad_context, grad_qkv) = scratch[:5], scratch[5:-2], scratch[-2:]
+    blocks = range(2 * (hidden // width) + 4)
+    grads = (2, members * len(blocks) * half_rows(width // members), width)
+
+    def body(s, x, seg, cot, vec, w_qkv, w_proj, w_fc1, w_fc2, y_own, y_send, g, g_out, g_vec, *scratch):
+        sums, kept, (grad_after, grad_context, grad_qkv, y) = scratch[:5], scratch[5:-4], scratch[-4:]
         weights = (vec, w_qkv, w_proj, w_fc1, w_fc2)
         step = pl.program_id(0)
 
@@ -416,15 +433,24 @@
             clear(sums)
 
         forward(x, seg, weights, kept, y)
-
-        def write(values):
+        first = s[0] == 0
+        y_own[...] = jnp.where(first, x[...], y[...])
+        y_send[...] = jnp.where(first, y[...], x[...])
+
+        def after_mlp(after, context):
+            grad_after[...] = after
+            grad_context[...] = context
+
+        def after_attn(values):
             g[...] = values.astype(BF16)
 
-        backward(cot, seg, weights, kept, sums, grad_context, grad_qkv, write)
+        backward_mlp(cot, weights, kept[4:], sums, after_mlp)
+        backward_attn(grad_after, grad_context, seg, weights, kept[:4], sums, grad_qkv, after_attn)
 
         @pl.when(step == steps - 1)
         def _():
-            write_sums(sums, members, g_mlp, g_attn, g_vec)
+            write_blocks(sums, members, blocks, g_out)
+            g_vec[...] = vector_sums(sums[4])
 
     rows = jax.ShapeDtypeStruct((steps * STEP, width), BF16)
     return kernel_call(
@@ -432,77 +458,589 @@
         steps,
         [spec((STEP, width), 0), spec((1, STEP), 1, steps), spec((STEP, width), 0, steps)]
         + weight_specs(weights, 1),
-        [spec((STEP, width), 0), spec((STEP, width), 0)] + specs,
-        [rows, rows] + outs,
+        [spec((STEP, width), 0)] * 3
+        + [
+            pl.BlockSpec(grads, lambda i, s: (0, 0, 0), pipeline_mode=pl.Buffered(1)),
+            pl.BlockSpec((VECTORS, width), lambda i, s: (0, 0), pipeline_mode=pl.Buffered(1)),
+        ],
+        [rows] * 3
+        + [jax.ShapeDtypeStruct(grads, BF16), jax.ShapeDtypeStruct((VECTORS, width), BF16)],
         sum_scratch(width, hidden)
         + [pltpu.VMEM(block, dtype) for _, dtype, block, _ in shapes]
-        + [pltpu.VMEM((STEP, width), BF16), pltpu.VMEM((STEP, 3 * width), BF16)],
+        + [
+            pltpu.VMEM((STEP, width), F32),
+            pltpu.VMEM((STEP, width), BF16),
+            pltpu.VMEM((STEP, 3 * width), BF16),
+            pltpu.VMEM((STEP, width), BF16),
+        ],
         "second_layer",
         steps * STEP * 12000000,
     )(section, x, seg, cotangent, *weights)
 
 
-def first_backward(section, seg, dout, kept, weights, steps, members):
+def place():
+    return lax.axis_index("section"), lax.axis_index("group"), lax.axis_index("member")
+
+
+def remote(src, dst, send, recv, device):
+    return pltpu.make_async_remote_copy(
+        src_ref=src, dst_ref=dst, send_sem=send, recv_sem=recv, device_id=device, device_id_type=MESH
+    )
+
+
+def greet(groups, members):
+    section, group, member = place()
+    peers = [
+        (lax.rem(section + ds, 2), group, lax.rem(member + dm, members))
+        for ds in range(2)
+        for dm in range(members)
+        if ds or dm
+    ] + [
+        (lax.rem(section + ds, 2), lax.rem(group + dg, groups), member)
+        for ds in range(2)
+        for dg in range(1, groups)
+    ]
+    barrier = pltpu.get_barrier_semaphore()
+    for peer in peers:
+        pl.semaphore_signal(barrier, inc=1, device_id=peer, device_id_type=MESH)
+    pl.semaphore_wait(barrier, len(peers))
+
+
+def rows_at(index, count):
+    return pl.ds(pl.multiple_of(index * count, 16), count)
+
+
+class Reduction:
+    def __init__(self, target, groups, members, count, width):
+        self.target, self.groups, self.members, self.count, self.width = target, groups, members, count, width
+        self.part = up16(-(-count // groups))
+
+    def scratch(self):
+        whole = (self.members * self.count, self.width)
+        sems = [1, 1, self.members, self.members, self.groups, self.groups, 2 * self.groups, 2 * self.groups]
+        return [
+            pltpu.VMEM(whole, BF16),
+            pltpu.VMEM(whole, BF16),
+            pltpu.VMEM((self.members - 1, self.count, self.width), BF16),
+            pltpu.VMEM((self.groups * self.part, self.width), BF16),
+            pltpu.VMEM((self.groups - 1, self.part, self.width), BF16),
+            pltpu.VMEM((self.part, self.width), BF16),
+        ] + [pltpu.SemaphoreType.DMA((n,)) for n in sems] + [pltpu.SemaphoreType.DMA]
+
+    def result(self):
+        return (2, self.groups, self.part, self.width)
+
+    def bind(self, refs, source, result):
+        self.mine, self.got, self.from_members, self.total, self.from_groups, self.piece = refs[:6]
+        self.sems = refs[6:14]
+        self.local = refs[14]
+        self.source, self.result_ref = source, result
+        return self
+
+    def section_copy(self):
+        section, group, member = place()
+        return remote(
+            self.source.at[1 - section], self.got, self.sems[0].at[0], self.sems[1].at[0], (1 - section, group, member)
+        )
+
+    def own_copy(self):
+        return pltpu.make_async_copy(self.source.at[lax.axis_index("section")], self.mine, self.local)
+
+    def member_copy(self, offset):
+        section, group, member = place()
+        to = lax.rem(member + offset, self.members)
+        return remote(
+            self.mine.at[rows_at(to, self.count)],
+            self.from_members.at[offset - 1],
+            self.sems[2].at[offset],
+            self.sems[3].at[offset],
+            (section, group, to),
+        )
+
+    def group_copy(self, offset):
+        section, group, member = place()
+        to = lax.rem(group + offset, self.groups)
+        return remote(
+            self.total.at[rows_at(to, self.part)],
+            self.from_groups.at[offset - 1],
+            self.sems[4].at[offset],
+            self.sems[5].at[offset],
+            (section, to, member),
+        )
+
+    def gather_copy(self, offset, across):
+        section, group, member = place()
+        slot = across * self.groups + offset
+        return remote(
+            self.piece,
+            self.result_ref.at[section, group],
+            self.sems[6].at[slot],
+            self.sems[7].at[slot],
+            (self.target, lax.rem(group + offset, self.groups), member),
+        )
+
+    def gathered(self, offset, across):
+        section, group, member = place()
+        slot = across * self.groups + offset
+        origin = lax.rem(group + self.groups - offset, self.groups)
+        half = 1 - section if across else section
+        return remote(
+            self.piece,
+            self.result_ref.at[half, origin],
+            self.sems[6].at[slot],
+            self.sems[7].at[slot],
+            (self.target, origin, member),
+        )
+
+    def start_section(self):
+        self.section_copy().start()
+        self.own_copy().start()
+
+    def start_members(self):
+        self.own_copy().wait()
+        self.section_copy().wait()
+        self.mine[...] = (self.mine[...].astype(F32) + self.got[...].astype(F32)).astype(BF16)
+        for offset in range(1, self.members):
+            self.member_copy(offset).start()
+
+    def start_groups(self):
+        for offset in range(1, self.members):
+            self.member_copy(offset).wait()
+        total = self.mine[rows_at(lax.axis_index("member"), self.count), :].astype(F32)
+        for offset in range(1, self.members):
+            total = total + self.from_members[offset - 1].astype(F32)
+        self.total[: self.count, :] = total.astype(BF16)
+        spare = self.groups * self.part - self.count
+        if spare:
+            self.total[self.count :, :] = jnp.zeros((spare, self.width), BF16)
+        for offset in range(1, self.groups):
+            self.group_copy(offset).start()
+
+    def start_gather(self):
+        section, group, member = place()
+        for offset in range(1, self.groups):
+            self.group_copy(offset).wait()
+        total = self.total[rows_at(group, self.part), :].astype(F32)
+        for offset in range(1, self.groups):
+            total = total + self.from_groups[offset - 1].astype(F32)
+        self.piece[...] = total.astype(BF16)
+
+        @pl.when(section == self.target)
+        def _():
+            for offset in range(1, self.groups):
+                self.gather_copy(offset, 0).start()
+            keep = pltpu.make_async_copy(self.piece, self.result_ref.at[section, group], self.local)
+            keep.start()
+            keep.wait()
+
+        @pl.when(section != self.target)
+        def _():
+            for offset in range(self.groups):
+                self.gather_copy(offset, 1).start()
+
+    def finish(self):
+        section, group, member = place()
+
+        @pl.when(section == self.target)
+        def _():
+            for offset in range(1, self.groups):
+                self.gather_copy(offset, 0).wait_send()
+                self.gathered(offset, 0).wait_recv()
+            for offset in range(self.groups):
+                self.gathered(offset, 1).wait_recv()
+
+        @pl.when(section != self.target)
+        def _():
+            for offset in range(self.groups):
+                self.gather_copy(offset, 1).wait_send()
+
+
+class VectorSum:
+    def __init__(self, groups, members, width):
+        self.groups, self.members, self.width = groups, members, width
+
+    def scratch(self):
+        return [
+            pltpu.VMEM((2 * self.members, VECTORS, self.width), BF16),
+            pltpu.VMEM((self.groups, VECTORS, self.width), BF16),
+            pltpu.VMEM((VECTORS, self.width), BF16),
+            pltpu.VMEM((VECTORS, self.width), BF16),
+        ] + [pltpu.SemaphoreType.DMA((n,)) for n in (2 * self.members,) * 2 + (self.groups,) * 2]
+
+    def bind(self, refs):
+        self.near, self.far, self.own, self.middle = refs[:4]
+        self.sems = refs[4:]
+        return self
+
+    def near_copy(self, offset):
+        section, group, member = place()
+        ds, dm = divmod(offset, self.members)
+        to = lax.rem(section + ds, 2), group, lax.rem(member + dm, self.members)
+        return remote(
+            self.own, self.near.at[section * self.members + member], self.sems[0].at[offset], self.sems[1].at[offset], to
+        )
+
+    def near_got(self, offset):
+        section, group, member = place()
+        ds, dm = divmod(offset, self.members)
+        origin = lax.rem(section + ds, 2), lax.rem(member + self.members - dm, self.members)
+        return remote(
+            self.own,
+            self.near.at[origin[0] * self.members + origin[1]],
+            self.sems[0].at[offset],
+            self.sems[1].at[offset],
+            (origin[0], group, origin[1]),
+        )
+
+    def far_copy(self, offset):
+        section, group, member = place()
+        to = section, lax.rem(group + offset, self.groups), member
+        return remote(self.middle, self.far.at[group], self.sems[2].at[offset], self.sems[3].at[offset], to)
+
+    def far_got(self, offset):
+        section, group, member = place()
+        origin = lax.rem(group + self.groups - offset, self.groups)
+        return remote(
+            self.middle, self.far.at[origin], self.sems[2].at[offset], self.sems[3].at[offset], (section, origin, member)
+        )
+
+    def start(self, values):
+        section, group, member = place()
+        self.own[...] = values
+        self.near[section * self.members + member] = values
+        for offset in range(1, 2 * self.members):
+            self.near_copy(offset).start()
+
+    def start_far(self):
+        for offset in range(1, 2 * self.members):
+            self.near_copy(offset).wait_send()
+            self.near_got(offset).wait_recv()
+        total = jnp.zeros((VECTORS, self.width), F32)
+        for index in range(2 * self.members):
+            total = total + self.near[index].astype(F32)
+        self.middle[...] = total.astype(BF16)
+        self.far[lax.axis_index("group")] = total.astype(BF16)
+        for offset in range(1, self.groups):
+            self.far_copy(offset).start()
+
+    def finish(self):
+        for offset in range(1, self.groups):
+            self.far_copy(offset).wait_send()
+            self.far_got(offset).wait_recv()
+        total = jnp.zeros((VECTORS, self.width), F32)
+        for index in range(self.groups):
+            total = total + self.far[index].astype(F32)
+        return total
+
+
+def first_backward(seg, dout, y_send, grads1, vec1, kept, weights, steps, groups, members):
     width, hidden = dout.shape[1], weights[3].shape[2]
     shapes = kept_shapes(steps, width, hidden)
-    outs, specs = grad_outs(width, hidden)
-
-    def body(s, seg, dout, vec, w_qkv, w_proj, w_fc1, w_fc2, *refs):
-        kept, (g, g_mlp, g_attn, g_vec) = refs[:9], refs[9:13]
-        sums, (grad_context, grad_qkv) = refs[13:18], refs[18:]
+    parts = hidden // width
+    size = half_rows(width // members)
+    mlp_blocks = range(2 * parts + 1)
+    attn_blocks = range(2 * parts + 1, 2 * parts + 4)
+    plans = [
+        Reduction(1, groups, members, (2 * parts + 4) * size, width),
+        Reduction(0, groups, members, len(mlp_blocks) * size, width),
+        Reduction(0, groups, members, len(attn_blocks) * size, width),
+    ]
+    vectors = [VectorSum(groups, members, width) for _ in range(2)]
+    counts = [len(plan.scratch()) for plan in plans] + [len(v.scratch()) for v in vectors]
+
+    def body(seg, dout, vec, w_qkv, w_proj, w_fc1, w_fc2, *refs):
+        kept, refs = refs[:9], refs[9:]
+        (y_send, grads1, vec1), refs = refs[:3], refs[3:]
+        (g_own, y_got, g_got, *finals), refs = refs[:8], refs[8:]
+        sums, refs = refs[:5], refs[5:]
+        (grad_after, grad_context, grad_qkv, g_send, grads_mlp, grads_attn), refs = refs[:6], refs[6:]
+        (row_send, row_recv), refs = refs[:2], refs[2:]
+        bound = []
+        for item, count in zip(plans + vectors, counts):
+            bound.append(refs[:count])
+            refs = refs[count:]
+        upper = plans[0].bind(bound[0], grads1, finals[0])
+        lower_mlp = plans[1].bind(bound[1], grads_mlp, finals[1])
+        lower_attn = plans[2].bind(bound[2], grads_attn, finals[2])
+        upper_vec, lower_vec = [v.bind(b) for v, b in zip(vectors, bound[3:])]
         weights = (vec, w_qkv, w_proj, w_fc1, w_fc2)
+        xhat1, r1, qkv, prob, *mlp_kept = kept
         step = pl.program_id(0)
+        section, group, member = place()
+        partner = (1 - section, group, member)
+
+        def y_copy():
+            return remote(y_send, y_got, row_send.at[steps], row_recv.at[steps], partner)
+
+        def g_copy(index):
+            return remote(
+                g_send.at[index],
+                g_got.at[rows_at(index, STEP)],
+                row_send.at[index],
+                row_recv.at[index],
+                partner,
+            )
 
         @pl.when(step == 0)
         def _():
+            greet(groups, members)
             clear(sums)
-
-        def write(values):
-            g[...] = values
-
-        backward(dout, seg, weights, kept, sums, grad_context, grad_qkv, write)
+            upper.start_section()
+            y_copy().start()
+
+        @pl.when(step == 1)
+        def _():
+            upper.start_members()
+            upper_vec.start(vec1[...])
+
+        @pl.when(step == steps)
+        def _():
+            upper.start_groups()
+            upper_vec.start_far()
+
+        @pl.when(step == steps + 1)
+        def _():
+            lower_mlp.start_members()
+
+        @pl.when(step == steps + 2)
+        def _():
+            upper.start_gather()
+            finals[3][...] = upper_vec.finish()
+
+        @pl.when(step < steps)
+        def _():
+            g_send[step] = dout[...]
+            rows = rows_at(step, STEP)
+
+            def after_mlp(after, context):
+                grad_after[rows, :] = after
+                grad_context[rows, :] = context
+
+            backward_mlp(dout, weights, mlp_kept, sums, after_mlp)
 
         @pl.when(step == steps - 1)
         def _():
-            write_sums(sums, members, g_mlp, g_attn, g_vec)
-
-    return kernel_call(
+            write_blocks(sums, members, mlp_blocks, grads_mlp)
+            lower_mlp.start_section()
+
+        @pl.when(step >= steps)
+        def _():
+            index = step - steps
+            rows = rows_at(index, STEP)
+
+            def after_attn(values):
+                low = values.astype(BF16)
+                kept_rows = g_send[index]
+                g_own[...] = jnp.where(section == 0, low, kept_rows)
+                g_send[index] = jnp.where(section == 0, kept_rows, low)
+                g_copy(index).start()
+
+            backward_attn(
+                grad_after.at[rows], grad_context.at[rows], seg, weights, kept[:4], sums, grad_qkv, after_attn
+            )
+
+        @pl.when(step == 2 * steps - 1)
+        def _():
+            write_blocks(sums, members, attn_blocks, grads_attn)
+            lower_attn.start_section()
+            lower_vec.start(vector_sums(sums[4]))
+            lower_mlp.start_groups()
+            lower_attn.start_members()
+            lower_vec.start_far()
+            lower_mlp.start_gather()
+            lower_attn.start_groups()
+            upper.finish()
+            y_copy().wait()
+            for index in range(steps):
+                g_copy(index).wait()
+            finals[4][...] = lower_vec.finish()
+            lower_attn.start_gather()
+            lower_mlp.finish()
+            lower_attn.finish()
+
+    def early(block, axis):
+        if axis == 0:
+            return pl.BlockSpec(block, lambda i: (jnp.minimum(i, steps - 1), 0))
+        return pl.BlockSpec(block, lambda i: (0, jnp.minimum(i, steps - 1)))
+
+    def late(block, axis):
+        if axis == 0:
+            return pl.BlockSpec(block, lambda i: (jnp.maximum(i - steps, 0), 0))
+        return pl.BlockSpec(block, lambda i: (0, jnp.maximum(i - steps, 0)))
+
+    anywhere = pl.BlockSpec(memory_space=pl.ANY)
+    low_rows = jax.ShapeDtypeStruct((steps * STEP, width), BF16)
+    vec_out = jax.ShapeDtypeStruct((VECTORS, width), F32)
+    vec_spec = pl.BlockSpec((VECTORS, width), lambda i: (0, 0))
+    scratch = sum_scratch(width, hidden) + [
+        pltpu.VMEM((steps * STEP, width), F32),
+        pltpu.VMEM((steps * STEP, width), BF16),
+        pltpu.VMEM((STEP, 3 * width), BF16),
+        pltpu.VMEM((steps, STEP, width), BF16),
+        pltpu.VMEM((2, members * plans[1].count, width), BF16),
+        pltpu.VMEM((2, members * plans[2].count, width), BF16),
+        pltpu.SemaphoreType.DMA((steps + 1,)),
+        pltpu.SemaphoreType.DMA((steps + 1,)),
+    ]
+    for item in plans + vectors:
+        scratch = scratch + item.scratch()
+    return pl.pallas_call(
         body,
-        steps,
-        [spec((1, STEP), 1, steps), spec((STEP, width), 0)]
-        + weight_specs(weights, 0)
-        + [spec(block, axis) for _, _, block, axis in shapes],
-        [spec((STEP, width), 0)] + specs,
-        [jax.ShapeDtypeStruct((steps * STEP, width), F32)] + outs,
-        sum_scratch(width, hidden)
-        + [pltpu.VMEM((STEP, width), BF16), pltpu.VMEM((STEP, 3 * width), BF16)],
-        "backward_first",
-        steps * STEP * 8000000,
-    )(section, seg, dout, *weights, *kept)
+        grid=(2 * steps,),
+        in_specs=[pl.BlockSpec((1, STEP), lambda i: (0, jnp.maximum(i - steps, 0))), early((STEP, width), 0)]
+        + [
+            pl.BlockSpec((1,) + w.shape[1:], lambda i: (0, 0, 0), pipeline_mode=pl.Buffered(1)) for w in weights
+        ]
+        + [late(block, axis) for _, _, block, axis in shapes[:4]]
+        + [early(block, axis) for _, _, block, axis in shapes[4:]]
+        + [anywhere, anywhere, vec_spec],
+        out_specs=[late((STEP, width), 0)] + [anywhere] * 5 + [vec_spec] * 2,
+        out_shape=[low_rows] * 3
+        + [jax.ShapeDtypeStruct(plan.result(), BF16) for plan in plans]
+        + [vec_out] * 2,
+        scratch_shapes=scratch,
+        compiler_params=pltpu.CompilerParams(
+            vmem_limit_bytes=60 * MIB, collective_id=1, has_side_effects=True
+        ),
+        cost_estimate=pl.CostEstimate(
+            flops=steps * STEP * 8000000, bytes_accessed=30 * MIB, transcendentals=0
+        ),
+        name="backward_first",
+    )(seg, dout, *weights, *kept, y_send, grads1, vec1)
+
+
+def finish(section, member, y_own, y_got, g_own, g_got, finals, width, hidden, steps, members):
+    parts = hidden // width
+    share = width // members
+    size = half_rows(share)
+    upper, lower_mlp, lower_attn, upper_vec, lower_vec = finals
+    upper, lower_mlp, lower_attn = [f.reshape(2, -1, width) for f in (upper, lower_mlp, lower_attn)]
+    lows = 2 * parts + 1
+
+    def body(s, y_own, y_got, g_own, g_got, upper, lower_mlp, lower_attn, upper_vec, lower_vec, *outs):
+        acts, grads, a_gain, a_shift, d_qkv, d_qv, d_proj, b_proj, m_gain, m_shift, d_fc1, b_fc1, d_fc2, b_fc2 = outs
+        step = pl.program_id(0)
+        first = s[0] == 0
+        mine = step // steps == s[0]
+        acts[0] = jnp.where(mine, y_own[...], y_got[...])
+        grads[0] = jnp.where(mine, g_own[...], g_got[...]).astype(F32)
+
+        @pl.when(step == 0)
+        def _():
+            for block in range(2 * parts + 4):
+                for half in range(2):
+                    top = half * (share - size)
+                    at = block * size
+                    low = (
+                        lower_mlp[half, at : at + size, :]
+                        if block < lows
+                        else lower_attn[half, at - lows * size : at - lows * size + size, :]
+                    )
+                    rows = jnp.where(first, low.astype(F32), upper[half, at : at + size, :].astype(F32))
+                    if block < parts:
+                        d_fc1[0, top : top + size, block * width : (block + 1) * width] = rows
+                    elif block < 2 * parts:
+                        base = (block - parts) * share + top
+                        d_fc2[0, base : base + size, :] = rows
+                    elif block == 2 * parts:
+                        d_proj[0, top : top + size, :] = rows
+                    else:
+                        left = (block - lows) * width
+                        d_qkv[0, top : top + size, left : left + width] = rows
+            vectors = jnp.where(first, lower_vec[...], upper_vec[...])
+
+            def put(out, row, count=1):
+                flat = jnp.concatenate([vectors[row + i : row + i + 1, :] for i in range(count)], axis=1)
+                length = count * width // members
+                value = flat[:, :length]
+                for m in range(1, members):
+                    value = jnp.where(s[1] == m, flat[:, m * length : (m + 1) * length], value)
+                out[...] = value
+
+            put(a_gain, ATTN_GAIN)
+            put(a_shift, ATTN_SHIFT)
+            put(d_qv, Q_BIAS, 2)
+            put(b_proj, PROJ_BIAS)
+            put(m_gain, MLP_GAIN)
+            put(m_shift, MLP_SHIFT)
+            put(b_fc1, FC1_BIAS, parts)
+            put(b_fc2, FC2_BIAS)
+
+    def whole(shape):
+        return pl.BlockSpec(shape, lambda i, s, n=len(shape): (0,) * n)
+
+    own = pl.BlockSpec((STEP, width), lambda i, s: (jnp.clip(i - s[0] * steps, 0, steps - 1), 0))
+    got = pl.BlockSpec((STEP, width), lambda i, s: (jnp.clip(i - (1 - s[0]) * steps, 0, steps - 1), 0))
+    total = 2 * steps * STEP
+    smalls = [
+        (1, share), (1, share), (1, share, 3 * width), (1, 2 * share), (1, share, width), (1, share), (1, share),
+        (1, share), (1, share, hidden), (1, hidden // members), (1, hidden // members, width), (1, share),
+    ]
+    rows_spec = pl.BlockSpec((1, STEP, width), lambda i, s: (0, i, 0))
+    inputs = [upper, lower_mlp, lower_attn, upper_vec, lower_vec]
+    return pl.pallas_call(
+        body,
+        grid_spec=pltpu.PrefetchScalarGridSpec(
+            num_scalar_prefetch=1,
+            grid=(2 * steps,),
+            in_specs=[own, got, own, got] + [whole(x.shape) for x in inputs],
+            out_specs=[rows_spec, rows_spec] + [whole(shape) for shape in smalls],
+        ),
+        out_shape=[
+            jax.ShapeDtypeStruct((1, total, width), BF16),
+            jax.ShapeDtypeStruct((1, total, width), F32),
+        ]
+        + [jax.ShapeDtypeStruct(shape, F32) for shape in smalls],
+        compiler_params=pltpu.CompilerParams(vmem_limit_bytes=40 * MIB),
+        cost_estimate=pl.CostEstimate(flops=0, bytes_accessed=16 * MIB, transcendentals=0),
+        name="finish",
+    )(jnp.stack([section, member]).astype(jnp.int32), y_own, y_got, g_own, g_got, *inputs)
+
+
+def gather_weights(own):
+    count = len(own)
+
+    def body(*refs):
+        mine, both, held = refs[:count], refs[count : 2 * count], refs[2 * count : 3 * count]
+        send, recv, load, store = refs[3 * count :]
+        section, group, member = place()
+        partner = (1 - section, group, member)
+        loads = [pltpu.make_async_copy(src.at[0], dst, load.at[i]) for i, (src, dst) in enumerate(zip(mine, held))]
+        for copy in loads:
+            copy.start()
+        barrier = pltpu.get_barrier_semaphore()
+        pl.semaphore_signal(barrier, inc=1, device_id=partner, device_id_type=MESH)
+        pl.semaphore_wait(barrier, 1)
+        copies = [
+            remote(src.at[0], dst.at[section], send.at[i], recv.at[i], partner)
+            for i, (src, dst) in enumerate(zip(mine, both))
+        ]
+        for copy in copies:
+            copy.start()
+        stores = [
+            pltpu.make_async_copy(src, dst.at[section], store.at[i]) for i, (src, dst) in enumerate(zip(held, both))
+        ]
+        for copy, later in zip(loads, stores):
+            copy.wait()
+            later.start()
+        for copy in copies + stores:
+            copy.wait()
+
+    anywhere = pl.BlockSpec(memory_space=pl.ANY)
+    return pl.pallas_call(
+        body,
+        in_specs=[anywhere] * count,
+        out_specs=[anywhere] * count,
+        out_shape=[jax.ShapeDtypeStruct((2,) + w.shape[1:], w.dtype) for w in own],
+        scratch_shapes=[pltpu.VMEM(w.shape[1:], w.dtype) for w in own] + [pltpu.SemaphoreType.DMA((count,))] * 4,
+        compiler_params=pltpu.CompilerParams(collective_id=0, has_side_effects=True),
+        name="gather_weights",
+    )(*own)
 
 
 def pack_vectors(vectors, width):
     flat = jnp.concatenate([v.reshape(-1, width) for v in vectors], axis=0)
     return jnp.pad(flat, ((0, VECTORS - flat.shape[0]), (0, 0)))[None]
-
-
-def local_part(section, tokens, segment, cotangent, weights, steps, members):
-    y0, *kept = first_forward(section, tokens, segment, weights, steps)
-    y1, g1, *grads1 = second_layer(section, y0, segment, cotangent, weights, steps, members)
-    g0, *grads0 = first_backward(section, segment, g1, kept, weights, steps, members)
-    return y0, y1, g0, g1, grads0, grads1
-
-
-def swap(value):
-    return lax.ppermute(value, "section", [(0, 1), (1, 0)])
-
-
-def gather_weights(own, here):
-    other = [swap(w) for w in own]
-    return [
-        jnp.concatenate([jnp.where(here, mine, got), jnp.where(here, got, mine)], axis=0)
-        for mine, got in zip(own, other)
-    ]
 
 
 def per_device(
@@ -522,70 +1060,24 @@
     fc2_weight,
     fc2_bias,
 ):
-    section = lax.axis_index("section")
-    here = section == 0
-    members = lax.axis_size("member")
+    section, member = lax.axis_index("section"), lax.axis_index("member")
+    groups, members = lax.axis_size("group"), lax.axis_size("member")
     rows, width = tokens.shape
+    hidden = fc1_weight.shape[2]
     steps = rows // 2 // STEP
     vec = pack_vectors(
         (attn_gain, attn_shift, qv_bias, proj_bias, mlp_gain, mlp_shift, fc2_bias, fc1_bias), width
     )
-    weights = gather_weights([vec, qkv_weight, proj_weight, fc1_weight, fc2_weight], here)
-    y0, y1, g0, g1, grads0, grads1 = local_part(
-        section.reshape(1).astype(jnp.int32), tokens, segment.reshape(1, rows), cotangent, weights, steps, members
+    weights = gather_weights([vec, qkv_weight, proj_weight, fc1_weight, fc2_weight])
+    at = section.reshape(1).astype(jnp.int32)
+    seg = segment.reshape(1, rows)
+    y0, *kept = first_forward(at, tokens, seg, weights, steps)
+    y_own, y_send, g1, grads1, vec1 = second_layer(at, y0, seg, cotangent, weights, steps, members)
+    seg_half = lax.dynamic_slice(seg, (0, section * (rows // 2)), (1, rows // 2))
+    g_own, y_got, g_got, *finals = first_backward(
+        seg_half, g1, y_send, grads1, vec1, kept, weights, steps, groups, members
     )
-
-    def joined(mine, got):
-        return jnp.where(here, jnp.concatenate([mine, got]), jnp.concatenate([got, mine]))[None]
-
-    def paired(first, second):
-        return joined(jnp.where(here, first, second), swap(jnp.where(here, second, first)))
-
-    activations = paired(y0, y1)
-    g0_low = g0.astype(BF16)
-    in_grads = joined(
-        jnp.where(here, g0, g1.astype(F32)), swap(jnp.where(here, g1, g0_low)).astype(F32)
-    )
-
-    def reduced(first, second):
-        total = lax.psum_scatter(jnp.stack([first, second]), "section", scatter_dimension=0, tiled=True)
-        total = total.reshape(2, members, -1, width)
-        total = lax.psum_scatter(total, "member", scatter_dimension=1, tiled=True)
-        return lax.psum(total, "group")[:, 0].astype(F32)
-
-    mlp = reduced(grads0[0], grads1[0])
-    attn = reduced(grads0[1], grads1[1])
-    vectors = lax.psum(
-        jnp.where(here, grads0[2] + swap(grads0[2]), grads1[2] + swap(grads1[2])), ("member", "group")
-    )
-    member = lax.axis_index("member")
-    hidden = fc1_weight.shape[2]
-    share = width // members
-    fc1 = mlp[0].reshape(hidden // width, share, width).transpose(1, 0, 2).reshape(share, hidden)
-    proj = attn[0, :share]
-    qkv = jnp.concatenate([attn[0, share:], attn[1, :share], attn[1, share:]], axis=1)
-
-    def piece(row, count=1):
-        flat = vectors[row : row + count].reshape(-1)
-        size = flat.shape[0] // members
-        return lax.dynamic_slice(flat, (member * size,), (size,))[None]
-
-    return (
-        activations,
-        in_grads,
-        piece(ATTN_GAIN),
-        piece(ATTN_SHIFT),
-        qkv[None],
-        piece(Q_BIAS, 2),
-        proj[None],
-        piece(PROJ_BIAS),
-        piece(MLP_GAIN),
-        piece(MLP_SHIFT),
-        fc1[None],
-        piece(FC1_BIAS, hidden // width),
-        mlp[1][None],
-        piece(FC2_BIAS),
-    )
+    return tuple(finish(section, member, y_own, y_got, g_own, g_got, finals, width, hidden, steps, members))
 
 
 def solution(mesh):

time: 386 us -> 222 us (0.58); the launches traced: 379 us -> 222 us
  waiting for transfers between devices: 81.4 us -> 0 us
  blocking collectives: 78.6 us -> 0 us
  Pallas kernels: 148 us -> 208 us
  other arithmetic: 38.6 us -> 1.49 us
  between operations: 14.4 us -> 0.91 us
  local copies, waits for them, and re-layouts: 16 us -> 11 us
    psum x1 -> x0, blocking collectives: 78.6 us -> none  [per_device(): lax.psum(jnp.where(here, grads0[2] + swap(grads0[2]), grads1[2] + swap(gr...]
    pallas_call x1 -> x3, Pallas kernels: 42.9 us -> 104 us  [the longest x1 90.1 us: first_backward(): pl.pallas_call(body, grid=(2 * steps,), in_specs=[pl.BlockSpec((1, STEP),...]
    psum x1 -> x0, waiting for transfers between devices: 41.1 us -> none  [reduced(): return lax.psum(total, 'group')[:, 0].astype(F32)]
    reduce_scatter x2 -> x0, waiting for transfers between devices: 21.3 us -> none  [reduced(): lax.psum_scatter(jnp.stack([first, second]), 'section', scatter_dimension...]
    unnamed x7 -> x0, waiting for transfers between devices: 16.1 us -> none
    select_n x9 -> x0, other arithmetic: 15.3 us -> none  [the longest x2 8.94 us: joined(): jnp.where(here, jnp.concatenate([mine, got]), jnp.concatenate([got, mine]))]
    concatenate x8 -> x0, other arithmetic: 13.8 us -> none  [the longest x3 7.59 us: joined(): jnp.concatenate([mine, got])]
    another operation x2 -> x1, other arithmetic: 6.1 us -> 0.08 us  [finish(): jnp.stack([section, member]).astype(jnp.int32)]
  transfers between devices with their start and end apart: 14 -> 0, of which waited for: 6 -> 0; matrix products, arithmetic and copies ran while one was open for 11% -> 0% of each run, Pallas kernels for 0% -> 0%
where the time goes in v2:
time: 222 us
  Pallas kernels  208 us (94%)
  local copies, waits for them, and re-layouts  11 us (5%)
    pallas_call x1, Pallas kernels, first_backward(): pl.pallas_call(body, grid=(2 * steps,), in_specs=[pl.BlockSpec((1, STEP),...  90.1 us
    pallas_call x1, Pallas kernels, second_layer(): kernel_call(body, steps, [spec((STEP, width), 0), spec((1, STEP), 1, step...  70.3 us
    pallas_call x1, Pallas kernels, first_forward(): kernel_call(body, steps, [spec((STEP, width), 0, steps), spec((1, STEP),...  34.6 us
    unnamed x20, local copies, waits for them, and re-layouts  8.93 us
    pallas_call x1, Pallas kernels, gather_weights(): pl.pallas_call(body, in_specs=[anywhere] * count, out_specs=[anywhere] *...  6.87 us
    pallas_call x1, Pallas kernels, finish(): pl.pallas_call(body, grid_spec=pltpu.PrefetchScalarGridSpec(num_scalar_pr...  6.57 us

profile of v2, /device:TPU:0, one launch (start us, length us, event | category | flops | bytes accessed | tf_op | source)
XLA Modules:
  0.0 221.8 jit_solution(8534729451201199655)
XLA Ops:
  0.6 0.1 pad_add_fusion.s
  0.7 0.7 reduce
  1.4 0.7 reduce.1
  2.2 0.8 concatenate.3
  3.0 0.6 pad_bitcast_fusion.refs_0_
  3.6 6.9 %gather_weights.1 = (f32[2,16,384]{2,1,0:T(8,128)}, bf16[2,384,1152]{2,1,0:T(8,128)(2,1)}, bf16[2,384,384]{2,1,0:T(8,128)(2,1)}, bf16[2,384,1536]{2,1,0:T(8,128)(2,1)}, bf16[2,1536,384]{2,1,0:T(8,128)(2,1)}) custom-call(f32[1,16,384]{2,1,0:T(8,128)} %pad_bitcast_fusion.refs_0_, bf16[1,384,1152]{2,1,0:T(8,128)(2,1)} %refs_1_.1, bf16[1,384,384]{2,1,0:T(8,128)(2,1)} %refs_2_.1, ...), custom_call_target="tpu_custom_call" | custom-call | tf_op jit(solution)/shard_map/gather_weights/pallas_call | solution.py:1030
  10.5 34.6 %forward_first.1 = (bf16[2048,384]{1,0:T(8,128)(2,1)}, bf16[2048,384]{1,0:T(8,128)(2,1)}, f32[2048,1]{1,0:T(8,128)}, bf16[2048,1152]{1,0:T(8,128)(2,1)}, bf16[84...) custom-call(s32[1]{0:T(128)} %bitcast.s, ...), custom_call_target="tpu_custom_call" | custom-call | flops 8192000000 | bytes 31457280 | tf_op jit(solution)/shard_map/forward_first/pallas_call | solution.py:407
  45.0 0.0 copy-start.9
  45.0 70.3 %second_layer.1 = (bf16[2048,384]{1,0:T(8,128)(2,1)}, bf16[2048,384]{1,0:T(8,128)(2,1)}, bf16[2048,384]{1,0:T(8,128)(2,1)}, bf16[2,2304,384]{2,1,0:T(8,128)(2,1)}, bf16[16,384]{1,0:T(8,128)(2,1)}) custom-call(s32[1]{0:T(128)} %bitcast.s, bf16[2048,384]{1,0:T(8,128)(2,1)} %get-tuple-element.47.x, s32[1,4096]{1,0:T(1,128)} %bitcast.14, bf16[4096,384]{1,0:T(8,128)(2,1)} %cot.1, ...), custom_call_target="tpu_custom_call" | custom-call | flops 24576000000 | bytes 31457280 | tf_op jit(solution)/shard_map/second_layer/pallas_call | solution.py:456
  115.4 0.0 copy-done.9
  115.4 0.6 dynamic-slice.3
  116.0 0.0 copy-start
  116.0 90.1 %backward_first.1 = (bf16[2048,384]{1,0:T(8,128)(2,1)}, bf16[2048,384]{1,0:T(8,128)(2,1)}, bf16[2048,384]{1,0:T(8,128)(2,1)}, bf16[2,4,144,384]{3,2,1,0:T(8,128)...) custom-call(s32[1,2048]{1,0:T(1,128)} %bitcast.12, ...), custom_call_target="tpu_custom_call" | custom-call | flops 16384000000 | bytes 31457280 | tf_op jit(solution)/shard_map/backward_first/pallas_call | solution.py:887
  206.1 0.0 copy-done
  206.1 0.0 copy-start.1
  206.1 1.4 copy-done.1
  207.5 1.4 copy-done.2
  208.9 1.4 copy-done.3
  210.3 1.2 copy-done.4
  211.5 1.1 copy-done.5
  212.6 1.0 copy-done.6
  213.6 0.7 copy-done.7
  214.3 0.7 copy-done.8
  215.0 6.6 %finish.1 = (bf16[1,4096,384]{2,1,0:T(8,128)(2,1)}, f32[1,4096,384]{2,1,0:T(8,128)}, f32[1,96]{1,0:T(1,128)}, f32[1,96]{1,0:T(1,128)}, f32[1,96,1152]{2,1,0:T(8,...) custom-call(s32[2]{0:T(128)S(1)} %pad_add_fusion.s, ...), custom_call_target="tpu_custom_call" | custom-call | bytes 16777216 | tf_op jit(solution)/shard_map/finish/pallas_call | solution.py:981
  (9 shorter events, 0.0 us)
Async XLA Ops:
  45.0 70.4 %copy-start.9 = (s32[4096]{0:T(1024)S(1)}, s32[4096]{0:T(1024)}, u32[]{:S(2)}) copy-start(s32[4096]{0:T(1024)} %param.16) | copy-start | bytes 49156
  116.0 90.1 %copy-start = (bf16[2048,384]{1,0:T(8,128)(2,1)S(1)}, bf16[2048,384]{1,0:T(8,128)(2,1)}, u32[]{:S(2)}) copy-start(bf16[2048,384]{1,0:T(8,128)(2,1)} %get-tuple-element.48.y_own) | copy-start | bytes 4718596
  206.1 1.4 copy-start.1
  207.5 1.4 copy-start.2
  208.9 1.4 copy-start.3
  210.3 1.2 copy-start.4
  211.5 1.1 copy-start.5
  212.6 1.0 copy-start.6
  213.6 0.7 copy-start.7
  214.3 0.7 copy-start.8

commit v3 on v2

v3 whole, which is shorter than its diff:
```python
import jax
import jax.numpy as jnp
from jax import lax
from jax.experimental import pallas as pl
from jax.experimental.pallas import tpu as pltpu
from jax.sharding import PartitionSpec as P

HD = 64
S = 256
HALF = S // 2
GLOBAL_LEN = 197
LOCAL_LEN = 37
PAIR = 2 * HD
STEP = 2 * S
EPS = 1e-06
SCALE = HD ** (-0.5)
LOG2E = 1.4426950408889634
CHUNK = 768
FORWARD_CHUNK = 256
DEPTH = 4
F32 = jnp.float32
BF16 = jnp.bfloat16
MIB = 1 << 20
MESH = pl.DeviceIdType.MESH

ATTN_GAIN, ATTN_SHIFT, Q_BIAS, V_BIAS, PROJ_BIAS, MLP_GAIN, MLP_SHIFT, FC2_BIAS, FC1_BIAS = range(9)
VECTORS = 16


def up16(value):
    return -(-value // 16) * 16


def key_windows(local):
    if not local:
        return ((0, up16(GLOBAL_LEN)),) * 2
    first_end = ((HALF - 1) // LOCAL_LEN + 1) * LOCAL_LEN
    second_start = HALF // LOCAL_LEN * LOCAL_LEN // 16 * 16
    return ((0, up16(first_end)), (second_start, up16(S // LOCAL_LEN * LOCAL_LEN)))


WINDOWS = tuple((local, key_windows(local)) for local in (False, True))
PROB_ROWS = sum(hi - lo for _, windows in WINDOWS for lo, hi in windows)


def prob_offset(pair, sequence, block):
    spans = [hi - lo for _, windows in WINDOWS for lo, hi in windows]
    return pair * PROB_ROWS + sum(spans[: 2 * sequence + block])


def nn(left, right):
    return jnp.dot(left, right, preferred_element_type=F32)


def nt(left, right):
    return lax.dot_general(left, right, (((1,), (1,)), ((), ())), preferred_element_type=F32)


def tn(left, right):
    return lax.dot_general(left, right, (((0,), (0,)), ((), ())), preferred_element_type=F32)


def column_sums(values):
    return jnp.sum(values.reshape(values.shape[0] // 8, 8, values.shape[1]), axis=0)


def normalized(values):
    centered = values - jnp.mean(values, axis=1, keepdims=True)
    inverse = lax.rsqrt(jnp.mean(centered * centered, axis=1, keepdims=True) + EPS)
    return centered * inverse, inverse


def norm_back(scaled, inverse, gain, grad):
    grad_scaled = grad * gain
    first = jnp.mean(grad_scaled, axis=1, keepdims=True)
    second = jnp.mean(grad_scaled * scaled, axis=1, keepdims=True)
    return inverse * (grad_scaled - first - scaled * second)


def crop_of(index):
    total = jnp.zeros_like(index)
    for crop in range(1, S // LOCAL_LEN + 1):
        total = total + (index >= crop * LOCAL_LEN).astype(jnp.int32)
    return total


def mask_bias(local, block, lo, hi):
    if not local:
        rows = lax.broadcasted_iota(jnp.int32, (hi - lo, HALF), 0) + lo
        return jnp.where(rows < GLOBAL_LEN, 0.0, -1e30)
    keys = crop_of(lax.broadcasted_iota(jnp.int32, (hi - lo, HALF), 0) + lo)
    queries = crop_of(lax.broadcasted_iota(jnp.int32, (hi - lo, HALF), 1) + block * HALF)
    return jnp.where(keys == queries, 0.0, -1e30)


def split_pair(rows):
    lane = lax.broadcasted_iota(jnp.int32, (1, PAIR), 1)
    first = (lane < HD).astype(rows.dtype)
    second = (lane >= HD).astype(rows.dtype)
    return jnp.concatenate([rows * first, rows * second], axis=0)


def padded(rows, lo, hi):
    parts = [rows]
    if lo:
        parts = [jnp.zeros((lo, rows.shape[1]), rows.dtype)] + parts
    if hi < S:
        parts = parts + [jnp.zeros((S - hi, rows.shape[1]), rows.dtype)]
    return jnp.concatenate(parts, axis=0) if len(parts) > 1 else rows


def diagonal(values):
    return jnp.concatenate([values[:HD, :HALF], values[HD:, HALF:]], axis=0)


def units_of(width):
    return [(sequence, pair, block) for sequence in range(2) for pair in range(width // PAIR) for block in range(2)]


def pipelined(units, depth, stages):
    held = [{} for _ in stages]
    for now in range(len(units) + depth * (len(stages) - 1)):
        for i, stage in enumerate(stages):
            at = now - i * depth
            if 0 <= at < len(units):
                before = [held[i - 1].pop(at)] if i else []
                held[i][at] = stage(units[at], *before)


class Once(dict):
    def get_or(self, key, make):
        if key not in self:
            self[key] = make()
        return self[key]


def place_of(unit):
    sequence, pair, block = unit
    lo, hi = WINDOWS[sequence][1][block]
    return sequence * S, pair * PAIR, block * HALF, lo, hi


def attend(seg, qkv, prob, ctx_t, width):
    once = Once()

    def valid_of(unit):
        base, _, at, _, _ = place_of(unit)
        return seg[0:1, base + at : base + at + HALF] >= 0

    def values_of(unit):
        base, left, _, _, _ = place_of(unit)
        cols = slice(2 * width + left, 2 * width + left + PAIR)
        return once.get_or(unit[:2], lambda: qkv[base : base + S, cols].T)

    def bias_of(unit):
        sequence, _, block = unit
        _, _, _, lo, hi = place_of(unit)

        def make():
            bias = mask_bias(WINDOWS[sequence][0], block, lo, hi)
            return jnp.concatenate([bias, bias], axis=1)

        return once.get_or(("bias", sequence, block), make)

    def raw_scores(unit):
        base, left, at, lo, hi = place_of(unit)
        values_of(unit)
        keys = qkv[base + lo : base + hi, width + left : width + left + PAIR]
        return nt(keys, split_pair(qkv[base + at : base + at + HALF, left : left + PAIR]))

    def softmax(unit, raw):
        sequence, pair, block = unit
        _, _, _, lo, hi = place_of(unit)
        scores = raw * (SCALE * LOG2E)
        cut = 0 if WINDOWS[sequence][0] else GLOBAL_LEN // 16 * 16 - lo
        tail = scores[cut:] + bias_of(unit)[cut:]
        scores = jnp.concatenate([scores[:cut], tail], axis=0) if cut else tail
        exponent = jnp.exp2(scores - jnp.max(scores, axis=0, keepdims=True))
        total = jnp.sum(exponent, axis=0, keepdims=True)
        valid = valid_of(unit)
        inverse = jnp.where(jnp.concatenate([valid, valid], axis=1), 1.0 / total, 0.0)
        probs = (exponent * inverse).astype(BF16)
        offset = prob_offset(pair, sequence, block)
        prob[offset : offset + hi - lo, :] = probs
        return probs

    def context(unit, probs):
        base, left, at, lo, hi = place_of(unit)
        values_t = values_of(unit)
        mixed = diagonal(nn(values_t, padded(probs, lo, hi)))
        own = values_t[:, at : at + HALF].astype(F32)
        ctx_t[left : left + PAIR, base + at : base + at + HALF] = jnp.where(
            valid_of(unit), mixed, own
        ).astype(BF16)

    pipelined(units_of(width), DEPTH, [raw_scores, softmax, context])


def attend_back(seg, qkv, prob, grad_context, grad_qkv, width):
    once = Once()

    def padding_of(unit):
        base = unit[0] * S

        def make():
            valid = (seg[0:1, base : base + S] >= 0).astype(jnp.int32)
            count = jnp.sum(valid, axis=1, keepdims=True)
            return lax.broadcasted_iota(jnp.int32, (S, PAIR), 0) >= count

        return once.get_or(("padding", unit[0]), make)

    def keys_of(unit):
        base, left, _, _, _ = place_of(unit)
        cols = slice(width + left, width + left + PAIR)
        return once.get_or(("keys", unit[:2]), lambda: qkv[base : base + S, cols].T)

    def grads_of(unit):
        base, left, at, _, _ = place_of(unit)
        rows = slice(base + at, base + at + HALF)
        return once.get_or(("grads", unit), lambda: split_pair(grad_context[rows, left : left + PAIR]))

    def grad_probs(unit):
        base, left, _, lo, hi = place_of(unit)
        keys_of(unit)
        return nt(qkv[base + lo : base + hi, 2 * width + left : 2 * width + left + PAIR], grads_of(unit))

    def grad_scores(unit, grads):
        sequence, pair, block = unit
        _, _, _, lo, hi = place_of(unit)
        offset = prob_offset(pair, sequence, block)
        probs_low = prob[offset : offset + hi - lo, :]
        probs = probs_low.astype(F32)
        product = probs * grads
        inner = jnp.sum(product, axis=0, keepdims=True)
        return (product - probs * inner).astype(BF16), probs_low

    def grad_rows(unit, given):
        grad_raw, probs_low = given
        base, left, at, lo, hi = place_of(unit)
        queries = split_pair(qkv[base + at : base + at + HALF, left : left + PAIR])
        grad_values = padded(nn(probs_low, grads_of(unit)), lo, hi)
        grad_keys = padded(nn(grad_raw, queries), lo, hi)
        grad_queries = diagonal(nn(keys_of(unit), padded(grad_raw, lo, hi))) * SCALE
        grad_qkv[base + at : base + at + HALF, left : left + PAIR] = grad_queries.astype(BF16).T
        if unit[2] == 0:
            once["first", unit[:2]] = grad_values, grad_keys
            return
        other_values, other_keys = once["first", unit[:2]]
        own = jnp.where(padding_of(unit), grad_context[base : base + S, left : left + PAIR].astype(F32), 0.0)
        grad_qkv[base : base + S, width + left : width + left + PAIR] = (
            (other_keys + grad_keys) * SCALE
        ).astype(BF16)
        grad_qkv[base : base + S, 2 * width + left : 2 * width + left + PAIR] = (
            other_values + grad_values + own
        ).astype(BF16)

    pipelined(units_of(width), DEPTH, [grad_probs, grad_scores, grad_rows])


def vector(vec, row, count=1):
    parts = [vec[0, row + i : row + i + 1, :] for i in range(count)]
    return parts[0] if count == 1 else jnp.concatenate(parts, axis=1)


def forward(x, seg, weights, kept, y, after_attention=None):
    vec, w_qkv, w_proj, w_fc1, w_fc2 = weights
    xhat1, r1, qkv, prob, ctx_t, xhat2, r2, act, dgelu = kept
    _, width = x.shape
    hidden = w_fc1.shape[2]
    scaled, inverse = normalized(x[...].astype(F32))
    xhat1[...] = scaled.astype(BF16)
    r1[...] = inverse
    normed = (scaled * vector(vec, ATTN_GAIN) + vector(vec, ATTN_SHIFT)).astype(BF16)
    for part, bias in ((0, Q_BIAS), (1, None), (2, V_BIAS)):
        mixed = nn(normed, w_qkv[0, :, part * width : (part + 1) * width])
        if bias is not None:
            mixed = mixed + vector(vec, bias)
        qkv[:, part * width : (part + 1) * width] = mixed.astype(BF16)
    attend(seg, qkv, prob, ctx_t, width)
    if after_attention is not None:
        after_attention()
    after = x[...].astype(F32) + tn(ctx_t[...], w_proj[0]) + vector(vec, PROJ_BIAS)
    scaled, inverse = normalized(after)
    xhat2[...] = scaled.astype(BF16)
    r2[...] = inverse
    normed = (scaled * vector(vec, MLP_GAIN) + vector(vec, MLP_SHIFT)).astype(BF16)
    output = after + vector(vec, FC2_BIAS)
    bias = vector(vec, FC1_BIAS, hidden // width)
    tops = list(range(0, hidden, FORWARD_CHUNK))

    def product(left):
        return nn(normed, w_fc1[0, :, left : left + FORWARD_CHUNK])

    coming = product(tops[0])
    for i, left in enumerate(tops):
        cols = slice(left, left + FORWARD_CHUNK)
        pre = coming + bias[:, cols]
        if i + 1 < len(tops):
            coming = product(tops[i + 1])
        below = 0.5 + 0.5 * lax.erf(pre * (0.5**0.5))
        density = jnp.exp2(pre * pre * (-0.5 * LOG2E)) * (1.0 / (2.0 * jnp.pi) ** 0.5)
        active = (pre * below).astype(BF16)
        act[:, cols] = active
        dgelu[:, cols] = (below + pre * density).astype(BF16)
        output = output + nn(active, w_fc2[0, cols, :])
    y[...] = output.astype(BF16)


def adder(sum_vec, width):
    def add(row, values):
        for i in range(values.shape[1] // width):
            at = (row + i) * 8
            sum_vec[at : at + 8, :] += column_sums(values[:, i * width : (i + 1) * width])

    return add


def backward_fc2(dout, act, sums):
    sum_fc2, sum_vec = sums[3:]
    top_grad = dout[...]
    adder(sum_vec, dout.shape[1])(FC2_BIAS, top_grad.astype(F32))
    sum_fc2[...] += nn(top_grad.T, act[...])


def backward_mlp(dout, weights, kept, sums, write, with_fc2=True):
    vec, _, w_proj, w_fc1, w_fc2 = weights
    ctx_t, xhat2, r2, act, dgelu = kept
    _, sum_proj, sum_fc1, _, sum_vec = sums
    rows, width = dout.shape
    hidden = w_fc1.shape[2]
    add = adder(sum_vec, width)
    top_grad = dout[...]
    top_wide = top_grad.astype(F32)
    if with_fc2:
        backward_fc2(dout, act, sums)
    scaled = xhat2[...].astype(F32)
    normed_t = (scaled * vector(vec, MLP_GAIN) + vector(vec, MLP_SHIFT)).astype(BF16).T
    grad_normed = jnp.zeros((rows, width), F32)
    column_parts = []
    for left in range(0, hidden, CHUNK):
        cols = slice(left, left + CHUNK)
        grad_pre = nt(top_grad, w_fc2[0, cols, :]) * dgelu[:, cols].astype(F32)
        column_parts.append(column_sums(grad_pre))
        grad_pre = grad_pre.astype(BF16)
        grad_normed = grad_normed + nt(grad_pre, w_fc1[0, :, cols])
        sum_fc1[:, cols] += nn(normed_t, grad_pre)
    columns = jnp.concatenate(column_parts, axis=1)
    for i in range(hidden // width):
        at = (FC1_BIAS + i) * 8
        sum_vec[at : at + 8, :] += columns[:, i * width : (i + 1) * width]
    add(MLP_GAIN, grad_normed * scaled)
    add(MLP_SHIFT, grad_normed)
    grad_after = top_wide + norm_back(scaled, r2[...], vector(vec, MLP_GAIN), grad_normed)
    add(PROJ_BIAS, grad_after)
    grad_branch = grad_after.astype(BF16)
    sum_proj[...] += nn(ctx_t[...], grad_branch)
    write(grad_after, nt(grad_branch, w_proj[0]).astype(BF16))


def backward_attn(grad_after, grad_context, seg, weights, kept, sums, grad_qkv, write, halfway=None):
    vec, w_qkv, _, _, _ = weights
    xhat1, r1, qkv, prob = kept
    sum_qkv, sum_vec = sums[0], sums[4]
    rows, width = grad_after.shape
    add = adder(sum_vec, width)
    attend_back(seg, qkv, prob, grad_context, grad_qkv, width)
    if halfway is not None:
        halfway()
    scaled = xhat1[...].astype(F32)
    normed_t = (scaled * vector(vec, ATTN_GAIN) + vector(vec, ATTN_SHIFT)).astype(BF16).T
    grad_normed = jnp.zeros((rows, width), F32)
    for part, row in ((0, Q_BIAS), (1, None), (2, V_BIAS)):
        cols = slice(part * width, (part + 1) * width)
        piece = grad_qkv[:, cols]
        if row is not None:
            add(row, piece.astype(F32))
        sum_qkv[:, cols] += nn(normed_t, piece)
        grad_normed = grad_normed + nt(piece, w_qkv[0, :, cols])
    add(ATTN_GAIN, grad_normed * scaled)
    add(ATTN_SHIFT, grad_normed)
    write(grad_after[...] + norm_back(scaled, r1[...], vector(vec, ATTN_GAIN), grad_normed))


def half_rows(share):
    return up16(share // 2)


def write_blocks(sums, members, blocks, out):
    sum_qkv, sum_proj, sum_fc1, sum_fc2, _ = sums
    width = sum_proj.shape[0]
    share = width // members
    size = half_rows(share)
    parts = sum_fc1.shape[1] // width

    def store(rows, member, block):
        at = (member * len(blocks) + blocks.index(block)) * size
        out[0, at : at + size, :] = rows[:size]
        out[1, at : at + size, :] = rows[share - size :]

    for block in blocks:
        if block < parts:
            whole = sum_fc1[:, block * width : (block + 1) * width]
        elif block < 2 * parts:
            chunk = block - parts
            whole = sum_fc2[:, chunk * width : (chunk + 1) * width].astype(BF16).T
            for place in range(members):
                row = chunk * members + place
                store(whole[place * share : (place + 1) * share], row // parts, parts + row % parts)
            continue
        elif block == 2 * parts:
            whole = sum_proj[...]
        else:
            part = block - 2 * parts - 1
            whole = sum_qkv[:, part * width : (part + 1) * width]
        whole = whole.astype(BF16)
        for member in range(members):
            store(whole[member * share : (member + 1) * share], member, block)


def vector_sums(sum_vec):
    return jnp.sum(sum_vec[...].reshape(VECTORS, 8, sum_vec.shape[1]), axis=1).astype(BF16)


def clear(refs):
    for ref in refs:
        ref[...] = jnp.zeros_like(ref)


def kept_shapes(steps, width, hidden):
    return (
        ((steps * STEP, width), BF16, (STEP, width), 0),
        ((steps * STEP, 1), F32, (STEP, 1), 0),
        ((steps * STEP, 3 * width), BF16, (STEP, 3 * width), 0),
        ((steps * PROB_ROWS * (width // PAIR), S), BF16, (PROB_ROWS * (width // PAIR), S), 0),
        ((width, steps * STEP), BF16, (width, STEP), 1),
        ((steps * STEP, width), BF16, (STEP, width), 0),
        ((steps * STEP, 1), F32, (STEP, 1), 0),
        ((steps * STEP, hidden), BF16, (STEP, hidden), 0),
        ((steps * STEP, hidden), BF16, (STEP, hidden), 0),
    )


def sum_scratch(width, hidden):
    return [
        pltpu.VMEM((width, 3 * width), F32),
        pltpu.VMEM((width, width), F32),
        pltpu.VMEM((width, hidden), F32),
        pltpu.VMEM((width, hidden), F32),
        pltpu.VMEM((8 * VECTORS, width), F32),
    ]


def place():
    return lax.axis_index("section"), lax.axis_index("group"), lax.axis_index("member")


def remote(src, dst, send, recv, device):
    return pltpu.make_async_remote_copy(
        src_ref=src, dst_ref=dst, send_sem=send, recv_sem=recv, device_id=device, device_id_type=MESH
    )


def greet(peers):
    barrier = pltpu.get_barrier_semaphore()
    for peer in peers:
        pl.semaphore_signal(barrier, inc=1, device_id=peer, device_id_type=MESH)
    pl.semaphore_wait(barrier, len(peers))


def near_peers(members, sections):
    section, group, member = place()
    return [
        (lax.rem(section + ds, 2), group, lax.rem(member + dm, members))
        for ds in range(2)
        for dm in range(members)
        if (ds or dm) and (sections or not (ds and dm))
    ]


def far_peers(groups):
    section, group, member = place()
    return [
        (lax.rem(section + ds, 2), lax.rem(group + dg, groups), member)
        for ds in range(2)
        for dg in range(1, groups)
    ]


def rows_at(index, count):
    return pl.ds(pl.multiple_of(index * count, 16), count)


class Near:
    def __init__(self, members, count, width):
        self.members, self.count, self.width = members, count, width

    def source_shape(self):
        return (2, self.members * self.count, self.width)

    def scratch(self):
        return [
            pltpu.VMEM((self.members * self.count, self.width), BF16),
            pltpu.VMEM((self.members - 1, self.count, self.width), BF16),
        ] + [pltpu.SemaphoreType.DMA((n,)) for n in (1, 1, self.members, self.members)]

    def bind(self, refs, source):
        self.got, self.from_members, *self.sems = refs
        self.source = source
        return self

    def section_copy(self):
        section, group, member = place()
        return remote(
            self.source.at[1 - section], self.got, self.sems[0].at[0], self.sems[1].at[0], (1 - section, group, member)
        )

    def member_copy(self, offset):
        section, group, member = place()
        to = lax.rem(member + offset, self.members)
        return remote(
            self.got.at[rows_at(to, self.count)],
            self.from_members.at[offset - 1],
            self.sems[2].at[offset],
            self.sems[3].at[offset],
            (section, group, to),
        )

    def start_section(self):
        self.section_copy().start()

    def start_members(self):
        self.section_copy().wait()
        own = self.source[lax.axis_index("section")].astype(F32)
        self.got[...] = (self.got[...].astype(F32) + own).astype(BF16)
        for offset in range(1, self.members):
            self.member_copy(offset).start()

    def finish(self, out):
        for offset in range(1, self.members):
            self.member_copy(offset).wait()
        total = self.got[rows_at(lax.axis_index("member"), self.count), :].astype(F32)
        for offset in range(1, self.members):
            total = total + self.from_members[offset - 1].astype(F32)
        out[: self.count, :] = total.astype(BF16)
        spare = out.shape[0] - self.count
        if spare:
            out[self.count :, :] = jnp.zeros((spare, self.width), BF16)


class Far:
    def __init__(self, target, groups, count, width):
        self.target, self.groups, self.width = target, groups, width
        self.part = up16(-(-count // groups))

    def total_shape(self):
        return (self.groups * self.part, self.width)

    def result_shape(self):
        return (2, self.groups, self.part, self.width)

    def scratch(self):
        return [
            pltpu.VMEM((self.groups - 1, self.part, self.width), BF16),
            pltpu.VMEM((self.part, self.width), BF16),
            pltpu.SemaphoreType.DMA,
        ] + [pltpu.SemaphoreType.DMA((n,)) for n in (self.groups,) * 2 + (2 * self.groups,) * 2]

    def bind(self, refs, total, result):
        self.from_groups, self.piece, self.local, *self.sems = refs
        self.total, self.result_ref = total, result
        return self

    def group_copy(self, offset):
        section, group, member = place()
        to = lax.rem(group + offset, self.groups)
        return remote(
            self.total.at[rows_at(to, self.part)],
            self.from_groups.at[offset - 1],
            self.sems[0].at[offset],
            self.sems[1].at[offset],
            (section, to, member),
        )

    def gather_copy(self, offset, across):
        section, group, member = place()
        slot = across * self.groups + offset
        return remote(
            self.piece,
            self.result_ref.at[section, group],
            self.sems[2].at[slot],
            self.sems[3].at[slot],
            (self.target, lax.rem(group + offset, self.groups), member),
        )

    def gathered(self, offset, across):
        section, group, member = place()
        slot = across * self.groups + offset
        origin = lax.rem(group + self.groups - offset, self.groups)
        half = 1 - section if across else section
        return remote(
            self.piece,
            self.result_ref.at[half, origin],
            self.sems[2].at[slot],
            self.sems[3].at[slot],
            (self.target, origin, member),
        )

    def start_groups(self):
        for offset in range(1, self.groups):
            self.group_copy(offset).start()

    def start_gather(self):
        section, group, member = place()
        for offset in range(1, self.groups):
            self.group_copy(offset).wait()
        total = self.total[rows_at(group, self.part), :].astype(F32)
        for offset in range(1, self.groups):
            total = total + self.from_groups[offset - 1].astype(F32)
        self.piece[...] = total.astype(BF16)

        @pl.when(section == self.target)
        def _():
            for offset in range(1, self.groups):
                self.gather_copy(offset, 0).start()
            keep = pltpu.make_async_copy(self.piece, self.result_ref.at[section, group], self.local)
            keep.start()
            keep.wait()

        @pl.when(section != self.target)
        def _():
            for offset in range(self.groups):
                self.gather_copy(offset, 1).start()

    def finish(self):
        section, group, member = place()

        @pl.when(section == self.target)
        def _():
            for offset in range(1, self.groups):
                self.gather_copy(offset, 0).wait_send()
                self.gathered(offset, 0).wait_recv()
            for offset in range(self.groups):
                self.gathered(offset, 1).wait_recv()

        @pl.when(section != self.target)
        def _():
            for offset in range(self.groups):
                self.gather_copy(offset, 1).wait_send()


class VectorSum:
    def __init__(self, groups, members, width):
        self.groups, self.members, self.width = groups, members, width

    def scratch(self):
        return [
            pltpu.VMEM((2 * self.members, VECTORS, self.width), BF16),
            pltpu.VMEM((self.groups, VECTORS, self.width), BF16),
            pltpu.VMEM((VECTORS, self.width), BF16),
            pltpu.VMEM((VECTORS, self.width), BF16),
        ] + [pltpu.SemaphoreType.DMA((n,)) for n in (2 * self.members,) * 2 + (self.groups,) * 2]

    def bind(self, refs):
        self.near, self.far, self.own, self.middle = refs[:4]
        self.sems = refs[4:]
        return self

    def near_copy(self, offset):
        section, group, member = place()
        ds, dm = divmod(offset, self.members)
        to = lax.rem(section + ds, 2), group, lax.rem(member + dm, self.members)
        return remote(
            self.own, self.near.at[section * self.members + member], self.sems[0].at[offset], self.sems[1].at[offset], to
        )

    def near_got(self, offset):
        section, group, member = place()
        ds, dm = divmod(offset, self.members)
        origin = lax.rem(section + ds, 2), lax.rem(member + self.members - dm, self.members)
        return remote(
            self.own,
            self.near.at[origin[0] * self.members + origin[1]],
            self.sems[0].at[offset],
            self.sems[1].at[offset],
            (origin[0], group, origin[1]),
        )

    def far_copy(self, offset):
        section, group, member = place()
        to = section, lax.rem(group + offset, self.groups), member
        return remote(self.middle, self.far.at[group], self.sems[2].at[offset], self.sems[3].at[offset], to)

    def far_got(self, offset):
        section, group, member = place()
        origin = lax.rem(group + self.groups - offset, self.groups)
        return remote(
            self.middle, self.far.at[origin], self.sems[2].at[offset], self.sems[3].at[offset], (section, origin, member)
        )

    def start(self, values):
        section, group, member = place()
        self.own[...] = values
        self.near[section * self.members + member] = values
        for offset in range(1, 2 * self.members):
            self.near_copy(offset).start()

    def start_far(self):
        for offset in range(1, 2 * self.members):
            self.near_copy(offset).wait_send()
            self.near_got(offset).wait_recv()
        total = jnp.zeros((VECTORS, self.width), F32)
        for index in range(2 * self.members):
            total = total + self.near[index].astype(F32)
        self.middle[...] = total.astype(BF16)
        self.far[lax.axis_index("group")] = total.astype(BF16)
        for offset in range(1, self.groups):
            self.far_copy(offset).start()

    def finish(self):
        for offset in range(1, self.groups):
            self.far_copy(offset).wait_send()
            self.far_got(offset).wait_recv()
        total = jnp.zeros((VECTORS, self.width), F32)
        for index in range(self.groups):
            total = total + self.far[index].astype(F32)
        return total


def take(refs, *counts):
    out, at = [], 0
    for count in counts:
        out.append(list(refs[at : at + count]))
        at += count
    assert at == len(refs)
    return out


def params(collective):
    return pltpu.CompilerParams(vmem_limit_bytes=62 * MIB, collective_id=collective, has_side_effects=True)


def cost(flops, moved):
    return pl.CostEstimate(flops=flops, bytes_accessed=moved * MIB, transcendentals=0)


def block_at(shape, axis, index):
    return pl.BlockSpec(shape, lambda i: tuple(index(i) if d == axis else 0 for d in range(len(shape))))


def fixed(shape):
    return pl.BlockSpec(shape, lambda i: (0,) * len(shape), pipeline_mode=pl.Buffered(1))


ANYWHERE = pl.BlockSpec(memory_space=pl.ANY)


def first_forward(tokens, seg, vectors, own, steps):
    width, hidden = tokens.shape[1], own[2].shape[2]
    shapes = kept_shapes(steps, width, hidden)
    held = [((2, VECTORS, width), F32)] + [((2,) + w.shape[1:], w.dtype) for w in own]
    count = len(own)

    def body(x, seg, *refs):
        vectors_in, own, (y,), kept, weights, held, sems = take(
            refs, len(vectors), count, 1, len(shapes), count + 1, count + 1, 5
        )
        load, send, recv, out, _ = sems
        step = pl.program_id(0)
        section, group, member = place()
        partner = (1 - section, group, member)
        order = list(range(count + 1))

        def own_load(i):
            return pltpu.make_async_copy(own[i - 1].at[0], held[i].at[section], load.at[i])

        def push(i, whose):
            source = own[i - 1].at[0] if i else held[0].at[whose]
            return remote(source, held[i].at[whose], send.at[i], recv.at[i], partner)

        def layer_zero(which):
            @pl.when(section == 0)
            def _():
                for i in which:
                    if i:
                        own_load(i).wait()

            @pl.when(section == 1)
            def _():
                for i in which:
                    push(i, 1 - section).wait_recv()

        def store(i):
            return pltpu.make_async_copy(held[i], weights[i], out.at[i])

        @pl.when(step == 0)
        def _():
            for i in order[1:]:
                own_load(i).start()
            row = 0
            for vector_in in vectors_in:
                for part in range(vector_in.shape[1] // width):
                    held[0][section, row : row + 1, :] = vector_in[:, part * width : (part + 1) * width]
                    row += 1
            held[0][section, row:, :] = jnp.zeros((VECTORS - row, width), F32)
            greet([partner])
            for i in order:
                push(i, section).start()
            layer_zero(order[:2])

        @pl.when(step == 1)
        def _():
            @pl.when(section == 0)
            def _():
                for i in order:
                    push(i, 1 - section).wait_recv()

            @pl.when(section == 1)
            def _():
                for i in order[1:]:
                    own_load(i).wait()

            for i in order:
                store(i).start()

        def after_attention():
            @pl.when(step == 0)
            def _():
                layer_zero(order[2:])

        forward(x, seg, held, kept, y, after_attention)

        @pl.when(step == steps - 1)
        def _():
            for i in order:
                store(i).wait()
                push(i, section).wait_send()

    def mine(i):
        return lax.axis_index("section") * steps + i

    return pl.pallas_call(
        body,
        grid=(steps,),
        in_specs=[block_at((STEP, width), 0, mine), block_at((1, STEP), 1, mine)]
        + [fixed(v.shape) for v in vectors]
        + [ANYWHERE] * count,
        out_specs=[block_at((STEP, width), 0, lambda i: i)]
        + [block_at(block, axis, lambda i: i) for _, _, block, axis in shapes]
        + [ANYWHERE] * (count + 1),
        out_shape=[jax.ShapeDtypeStruct((steps * STEP, width), BF16)]
        + [jax.ShapeDtypeStruct(shape, dtype) for shape, dtype, _, _ in shapes]
        + [jax.ShapeDtypeStruct(shape, dtype) for shape, dtype in held],
        scratch_shapes=[pltpu.VMEM(shape, dtype) for shape, dtype in held]
        + [pltpu.SemaphoreType.DMA((count + 1,))] * 5,
        compiler_params=params(0),
        cost_estimate=cost(steps * STEP * 4000000, 40),
        name="forward_first",
    )(tokens, seg, *vectors, *own)


def block_lists(parts):
    fc1, fc2, proj = list(range(parts)), list(range(parts, 2 * parts)), 2 * parts
    qkv = [proj + 1, proj + 2, proj + 3]
    upper = (fc2 + fc1[: parts // 2], fc1[parts // 2 :] + [proj] + qkv)
    lower = (fc2, fc1 + [proj], qkv)
    return upper, lower


def second_layer(x, seg, cotangent, weights, steps, groups, members):
    width, hidden = x.shape[1], weights[3].shape[2]
    shapes = kept_shapes(steps, width, hidden)
    size = half_rows(width // members)
    early, late = block_lists(hidden // width)[0]
    near = Near(members, len(early) * size, width)
    far = Far(1, groups, len(early) * size, width)
    late_shape = Near(members, len(late) * size, width).source_shape()

    def body(x, seg, cot, vec, w_qkv, w_proj, w_fc1, w_fc2, *refs):
        outs, sums, attn_kept, mlp_kept, rest, sems, near_refs = take(
            refs, 6, 5, 4, 5, 6, 2, len(near.scratch())
        )
        y_own, y_got, g, late_out, total_out, vec_out = outs
        grad_after, grad_context, grad_qkv, y, y_send, early_out = rest
        send, recv = sems
        near.bind(near_refs, early_out)
        weights = (vec, w_qkv, w_proj, w_fc1, w_fc2)
        step = pl.program_id(0)
        section, group, member = place()

        def y_copy(index):
            return remote(
                y_send.at[index], y_got.at[rows_at(index, STEP)], send.at[index], recv.at[index], (1 - section, group, member)
            )

        @pl.when(step == 0)
        def _():
            clear(sums)
            greet(near_peers(members, False))

        @pl.when(step < steps)
        def _():
            forward(x, seg, weights, [ref.at[step] for ref in attn_kept] + mlp_kept, y)
            y_own[...] = jnp.where(section == 0, x[...], y[...])
            y_send[step] = jnp.where(section == 0, y[...], x[...])
            y_copy(step).start()

            def write(after, context):
                grad_after[step] = after
                grad_context[step] = context

            backward_mlp(cot, weights, mlp_kept, sums, write)

        @pl.when(step == steps - 1)
        def _():
            write_blocks(sums, members, early, early_out)
            near.start_section()

        @pl.when(step >= steps)
        def _():
            index = step - steps

            def write(values):
                g[...] = values.astype(BF16)

            def halfway():
                @pl.when(step == steps)
                def _():
                    near.start_members()

            backward_attn(
                grad_after.at[index], grad_context.at[index], seg, weights,
                [ref.at[index] for ref in attn_kept], sums, grad_qkv, write, halfway,
            )

        @pl.when(step == 2 * steps - 1)
        def _():
            write_blocks(sums, members, late, late_out)
            vec_out[...] = vector_sums(sums[4])
            for index in range(steps):
                y_copy(index).wait()
            near.finish(total_out)

    def mine(index):
        return lambda i: lax.axis_index("section") * steps + index(i)

    def first(i):
        return jnp.minimum(i, steps - 1)

    def then(i):
        return jnp.maximum(i - steps, 0)

    rows = jax.ShapeDtypeStruct((steps * STEP, width), BF16)
    fixed_outs = [late_shape, far.total_shape(), (VECTORS, width)]
    return pl.pallas_call(
        body,
        grid=(2 * steps,),
        in_specs=[
            block_at((STEP, width), 0, first),
            block_at((1, STEP), 1, mine(lambda i: lax.rem(i, steps))),
            block_at((STEP, width), 0, mine(first)),
        ]
        + [pl.BlockSpec((1,) + w.shape[1:], lambda i: (1, 0, 0), pipeline_mode=pl.Buffered(1)) for w in weights],
        out_specs=[block_at((STEP, width), 0, first), ANYWHERE, block_at((STEP, width), 0, then)]
        + [fixed(shape) for shape in fixed_outs],
        out_shape=[rows] * 3 + [jax.ShapeDtypeStruct(shape, BF16) for shape in fixed_outs],
        scratch_shapes=sum_scratch(width, hidden)
        + [pltpu.VMEM((steps,) + block, dtype) for _, dtype, block, _ in shapes[:4]]
        + [pltpu.VMEM(block, dtype) for _, dtype, block, _ in shapes[4:]]
        + [
            pltpu.VMEM((steps, STEP, width), F32),
            pltpu.VMEM((steps, STEP, width), BF16),
            pltpu.VMEM((STEP, 3 * width), BF16),
            pltpu.VMEM((STEP, width), BF16),
            pltpu.VMEM((steps, STEP, width), BF16),
            pltpu.VMEM(near.source_shape(), BF16),
        ]
        + [pltpu.SemaphoreType.DMA((steps,))] * 2
        + near.scratch(),
        compiler_params=params(1),
        cost_estimate=cost(steps * STEP * 12000000, 20),
        name="second_layer",
    )(x, seg, cotangent, *weights)


def first_backward(seg, dout, late1, total1, vec1, kept, weights, steps, groups, members):
    width, hidden = dout.shape[1], weights[3].shape[2]
    shapes = kept_shapes(steps, width, hidden)
    size = half_rows(width // members)
    (upper_early, upper_late), lower = block_lists(hidden // width)
    fars = [
        Far(target, groups, len(blocks) * size, width)
        for target, blocks in [(1, upper_early), (1, upper_late)] + [(0, blocks) for blocks in lower]
    ]
    nears = [Near(members, len(blocks) * size, width) for blocks in (upper_late,) + lower]
    vector_plans = [VectorSum(groups, members, width) for _ in range(2)]
    plans = fars + nears + vector_plans

    def body(seg, dout, vec, w_qkv, w_proj, w_fc1, w_fc2, *refs):
        kept, (late1, total1, vec1), (g_own, g_got), results, vec_outs, sums, rest, sources, totals, sems, *bound = take(
            refs, 9, 3, 2, 5, 2, 5, 4, 3, 4, 2, *[len(plan.scratch()) for plan in plans]
        )
        grad_after, grad_context, grad_qkv, g_send = rest
        send, recv = sems
        for plan, plan_refs, total, result in zip(fars, bound[:5], [total1] + list(totals), results):
            plan.bind(plan_refs, total, result)
        for plan, plan_refs, source in zip(nears, bound[5:9], [late1] + list(sources)):
            plan.bind(plan_refs, source)
        for plan, plan_refs in zip(vector_plans, bound[9:]):
            plan.bind(plan_refs)
        far_a, far_b, far_fc2, far_fc1, far_qkv = fars
        near_b, near_fc2, near_fc1, near_qkv = nears
        total_b, total_fc2, total_fc1, total_qkv = totals
        upper_vec, lower_vec = vector_plans
        weights = (vec, w_qkv, w_proj, w_fc1, w_fc2)
        xhat1, r1, qkv, prob, ctx_t, xhat2, r2, act, dgelu = kept
        step = pl.program_id(0)
        section, group, member = place()

        def g_copy(index):
            return remote(
                g_send.at[index], g_got.at[rows_at(index, STEP)], send.at[index], recv.at[index], (1 - section, group, member)
            )

        @pl.when(step == 0)
        def _():
            greet(near_peers(members, True) + far_peers(groups))
            near_b.start_section()
            far_a.start_groups()
            upper_vec.start(vec1[...])
            clear(sums)

        @pl.when(step == steps)
        def _():
            near_b.start_members()

        @pl.when(step == steps + 1)
        def _():
            near_fc2.start_members()
            far_a.start_gather()
            upper_vec.start_far()

        @pl.when(step == 2 * steps)
        def _():
            near_b.finish(total_b)
            far_b.start_groups()
            vec_outs[0][...] = upper_vec.finish()

        @pl.when(step == 2 * steps + 1)
        def _():
            near_fc1.start_members()

        @pl.when(step == 2 * steps + 2)
        def _():
            near_fc2.finish(total_fc2)
            far_fc2.start_groups()
            far_b.start_gather()

        @pl.when(step == 2 * steps + 3)
        def _():
            far_fc2.start_gather()

        @pl.when(step < steps)
        def _():
            g_send[step] = dout[...]
            backward_fc2(dout, act, sums)

        @pl.when(step == steps - 1)
        def _():
            write_blocks(sums, members, lower[0], near_fc2.source)
            near_fc2.start_section()

        @pl.when(jnp.logical_and(step >= steps, step < 2 * steps))
        def _():
            index = step - steps

            def write(after, context):
                grad_after[index] = after
                grad_context[index] = context

            backward_mlp(g_send.at[index], weights, (ctx_t, xhat2, r2, None, dgelu), sums, write, False)

        @pl.when(step == 2 * steps - 1)
        def _():
            write_blocks(sums, members, lower[1], near_fc1.source)
            near_fc1.start_section()

        @pl.when(step >= 2 * steps)
        def _():
            index = step - 2 * steps

            def write(values):
                low = values.astype(BF16)
                upper_rows = g_send[index]
                g_own[...] = jnp.where(section == 0, low, upper_rows)
                g_send[index] = jnp.where(section == 0, upper_rows, low)
                g_copy(index).start()

            backward_attn(
                grad_after.at[index], grad_context.at[index], seg, weights, (xhat1, r1, qkv, prob), sums, grad_qkv, write
            )

        @pl.when(step == 3 * steps - 1)
        def _():
            write_blocks(sums, members, lower[2], near_qkv.source)
            near_qkv.start_section()
            lower_vec.start(vector_sums(sums[4]))
            near_fc1.finish(total_fc1)
            far_fc1.start_groups()
            near_qkv.start_members()
            lower_vec.start_far()
            far_fc1.start_gather()
            for index in range(steps):
                g_copy(index).wait()
            far_a.finish()
            far_b.finish()
            far_fc2.finish()
            vec_outs[1][...] = lower_vec.finish()
            near_qkv.finish(total_qkv)
            far_qkv.start_groups()
            far_qkv.start_gather()
            far_fc1.finish()
            far_qkv.finish()

    def phase(number):
        return lambda i: jnp.clip(i - number * steps, 0, steps - 1)

    def kept_spec(number, entry):
        _, _, block, axis = entry
        return block_at(block, axis, phase(number))

    phases = (2, 2, 2, 2, 1, 1, 1, 0, 1)
    low_rows = jax.ShapeDtypeStruct((steps * STEP, width), BF16)
    vec_shape = (VECTORS, width)
    return pl.pallas_call(
        body,
        grid=(3 * steps,),
        in_specs=[
            block_at((1, STEP), 1, lambda i: lax.axis_index("section") * steps + phase(2)(i)),
            block_at((STEP, width), 0, phase(0)),
        ]
        + [fixed((1,) + w.shape[1:]) for w in weights]
        + [kept_spec(number, entry) for number, entry in zip(phases, shapes)]
        + [fixed(late1.shape), fixed(total1.shape), fixed(vec_shape)],
        out_specs=[block_at((STEP, width), 0, phase(2)), ANYWHERE] + [ANYWHERE] * 5 + [fixed(vec_shape)] * 2,
        out_shape=[low_rows] * 2
        + [jax.ShapeDtypeStruct(far.result_shape(), BF16) for far in fars]
        + [jax.ShapeDtypeStruct(vec_shape, F32)] * 2,
        scratch_shapes=sum_scratch(width, hidden)
        + [
            pltpu.VMEM((steps, STEP, width), F32),
            pltpu.VMEM((steps, STEP, width), BF16),
            pltpu.VMEM((STEP, 3 * width), BF16),
            pltpu.VMEM((steps, STEP, width), BF16),
        ]
        + [pltpu.VMEM(near.source_shape(), BF16) for near in nears[1:]]
        + [pltpu.VMEM(far.total_shape(), BF16) for far in fars[1:]]
        + [pltpu.SemaphoreType.DMA((steps,))] * 2
        + [item for plan in plans for item in plan.scratch()],
        compiler_params=params(2),
        cost_estimate=cost(steps * STEP * 8000000, 40),
        name="backward_first",
    )(seg, dout, *weights, *kept, late1, total1, vec1)


def finish(y_own, y_got, g_own, g_got, results, vec_sums, width, hidden, steps, members):
    parts = hidden // width
    share = width // members
    size = half_rows(share)
    upper, lower = block_lists(parts)
    lists = list(upper) + list(lower)
    results = [result.reshape(2, -1, width) for result in results]
    at = jnp.stack([lax.axis_index("section"), lax.axis_index("member")]).astype(jnp.int32)

    def body(s, y_own, y_got, g_own, g_got, *refs):
        results, (upper_vec, lower_vec), (acts, grads), outs = take(refs, 5, 2, 2, 12)
        a_gain, a_shift, d_qkv, d_qv, d_proj, b_proj, m_gain, m_shift, d_fc1, b_fc1, d_fc2, b_fc2 = outs
        step = pl.program_id(0)
        first = s[0] == 0
        mine = step // steps == s[0]
        acts[0] = jnp.where(mine, y_own[...], y_got[...])
        grads[0] = jnp.where(mine, g_own[...], g_got[...]).astype(F32)

        def rows_of(which, block, half):
            for blocks, result in list(zip(lists, results))[which]:
                if block in blocks:
                    top = blocks.index(block) * size
                    return result[half, top : top + size, :].astype(F32)
            raise KeyError(block)

        @pl.when(step == 0)
        def _():
            for block in range(2 * parts + 4):
                for half in range(2):
                    top = half * (share - size)
                    rows = jnp.where(first, rows_of(slice(2, 5), block, half), rows_of(slice(0, 2), block, half))
                    if block < parts:
                        d_fc1[0, top : top + size, block * width : (block + 1) * width] = rows
                    elif block < 2 * parts:
                        base = (block - parts) * share + top
                        d_fc2[0, base : base + size, :] = rows
                    elif block == 2 * parts:
                        d_proj[0, top : top + size, :] = rows
                    else:
                        left = (block - 2 * parts - 1) * width
                        d_qkv[0, top : top + size, left : left + width] = rows
            vectors = jnp.where(first, lower_vec[...], upper_vec[...])

            def put(out, row, count=1):
                flat = jnp.concatenate([vectors[row + i : row + i + 1, :] for i in range(count)], axis=1)
                length = count * width // members
                value = flat[:, :length]
                for m in range(1, members):
                    value = jnp.where(s[1] == m, flat[:, m * length : (m + 1) * length], value)
                out[...] = value

            put(a_gain, ATTN_GAIN)
            put(a_shift, ATTN_SHIFT)
            put(d_qv, Q_BIAS, 2)
            put(b_proj, PROJ_BIAS)
            put(m_gain, MLP_GAIN)
            put(m_shift, MLP_SHIFT)
            put(b_fc1, FC1_BIAS, parts)
            put(b_fc2, FC2_BIAS)

    def whole(shape):
        return pl.BlockSpec(shape, lambda i, s, n=len(shape): (0,) * n)

    own = pl.BlockSpec((STEP, width), lambda i, s: (jnp.clip(i - s[0] * steps, 0, steps - 1), 0))
    got = pl.BlockSpec((STEP, width), lambda i, s: (jnp.clip(i - (1 - s[0]) * steps, 0, steps - 1), 0))
    total = 2 * steps * STEP
    smalls = [
        (1, share), (1, share), (1, share, 3 * width), (1, 2 * share), (1, share, width), (1, share), (1, share),
        (1, share), (1, share, hidden), (1, hidden // members), (1, hidden // members, width), (1, share),
    ]
    rows_spec = pl.BlockSpec((1, STEP, width), lambda i, s: (0, i, 0))
    inputs = results + list(vec_sums)
    return pl.pallas_call(
        body,
        grid_spec=pltpu.PrefetchScalarGridSpec(
            num_scalar_prefetch=1,
            grid=(2 * steps,),
            in_specs=[own, got, own, got] + [whole(x.shape) for x in inputs],
            out_specs=[rows_spec, rows_spec] + [whole(shape) for shape in smalls],
        ),
        out_shape=[
            jax.ShapeDtypeStruct((1, total, width), BF16),
            jax.ShapeDtypeStruct((1, total, width), F32),
        ]
        + [jax.ShapeDtypeStruct(shape, F32) for shape in smalls],
        compiler_params=pltpu.CompilerParams(vmem_limit_bytes=62 * MIB),
        cost_estimate=cost(0, 16),
        name="finish",
    )(at, y_own, y_got, g_own, g_got, *inputs)


def per_device(
    tokens,
    segment,
    cotangent,
    attn_gain,
    attn_shift,
    qkv_weight,
    qv_bias,
    proj_weight,
    proj_bias,
    mlp_gain,
    mlp_shift,
    fc1_weight,
    fc1_bias,
    fc2_weight,
    fc2_bias,
):
    groups, members = lax.axis_size("group"), lax.axis_size("member")
    rows, width = tokens.shape
    hidden = fc1_weight.shape[2]
    steps = rows // 2 // STEP
    seg = segment.reshape(1, rows)
    vectors = (attn_gain, attn_shift, qv_bias, proj_bias, mlp_gain, mlp_shift, fc2_bias, fc1_bias)
    y0, *rest = first_forward(
        tokens, seg, vectors, [qkv_weight, proj_weight, fc1_weight, fc2_weight], steps
    )
    kept, weights = rest[:9], rest[9:]
    y_own, y_got, g1, late1, total1, vec1 = second_layer(y0, seg, cotangent, weights, steps, groups, members)
    g_own, g_got, *grads = first_backward(seg, g1, late1, total1, vec1, kept, weights, steps, groups, members)
    return tuple(finish(y_own, y_got, g_own, g_got, grads[:5], grads[5:], width, hidden, steps, members))


def solution(mesh):
    row = P("section", None)
    mat = P("section", None, None)
    tokens = P(("group", "member"), None)
    split = P("section", "member")
    split_mat = P("section", "member", None)
    stacked = P("section", ("group", "member"), None)
    return jax.shard_map(
        per_device,
        mesh=mesh,
        in_specs=(
            tokens, P(("group", "member")), tokens,
            row, row, mat, row, mat, row, row, row, mat, row, mat, row,
        ),
        out_specs=(
            stacked, stacked,
            split, split, split_mat, split, split_mat, split, split, split, split_mat, split, split_mat, split,
        ),
        check_vma=False,
    )
```

time: 222 us -> 172 us (0.77)
  Pallas kernels: 208 us -> 170 us
  local copies, waits for them, and re-layouts: 11 us -> 0 us
    pallas_call x4 -> x3, Pallas kernels: 202 us -> 158 us  [the longest x1 71 us: first_backward(): pl.pallas_call(body, grid=(3 * steps,), in_specs=[block_at((1, STEP), 1,...]
    unnamed x20 -> x0, local copies, waits for them, and re-layouts: 8.93 us -> none
    pallas_call x1, Pallas kernels: 6.57 us -> 11.2 us  [finish(): pl.pallas_call(body, grid_spec=pltpu.PrefetchScalarGridSpec(num_scalar_pr...]
where the time goes in v3:
time: 172 us; the launch traced here: 171 us
  Pallas kernels  170 us (99%)
    pallas_call x1, Pallas kernels, first_backward(): pl.pallas_call(body, grid=(3 * steps,), in_specs=[block_at((1, STEP), 1,...  71 us
    pallas_call x1, Pallas kernels, second_layer(): pl.pallas_call(body, grid=(2 * steps,), in_specs=[block_at((STEP, width),...  61.2 us
    pallas_call x1, Pallas kernels, first_forward(): pl.pallas_call(body, grid=(steps,), in_specs=[block_at((STEP, width), 0,...  26.3 us
    pallas_call x1, Pallas kernels, finish(): pl.pallas_call(body, grid_spec=pltpu.PrefetchScalarGridSpec(num_scalar_pr...  11.2 us

profile of v3, /device:TPU:0, one launch (start us, length us, event | category | flops | bytes accessed | tf_op | source)
XLA Modules:
  0.0 171.2 jit_solution(12575028530266252409)
XLA Ops:
  0.7 26.3 %forward_first.1 = (bf16[2048,384]{1,0:T(8,128)(2,1)}, bf16[2048,384]{1,0:T(8,128)(2,1)}, f32[2048,1]{1,0:T(8,128)}, bf16[2048,1152]{1,0:T(8,128)(2,1)}, bf16[84...) custom-call(bf16[4096,384]{1,0:T(8,128)(2,1)} %x.1, ...), custom_call_target="tpu_custom_call" | custom-call | flops 8192000000 | bytes 41943040 | tf_op jit(solution)/shard_map/forward_first/pallas_call | solution.py:841
  26.9 61.2 %second_layer.1 = (bf16[2048,384]{1,0:T(8,128)(2,1)}, bf16[2048,384]{1,0:T(8,128)(2,1)}, bf16[2048,384]{1,0:T(8,128)(2,1)}, bf16[2,1152,384]{2,1,0:T(8,128)(2,1)...) custom-call(bf16[2048,384]{1,0:T(8,128)(2,1)} %get-tuple-element.44.x, s32[1,4096]{1,0:T(1,128)} %bitcast.14, ...), custom_call_target="tpu_custom_call" | custom-call | flops 24576000000 | bytes 20971520 | tf_op jit(solution)/shard_map/second_layer/pallas_call | solution.py:954
  88.1 71.0 %backward_first.1 = (bf16[2048,384]{1,0:T(8,128)(2,1)}, bf16[2048,384]{1,0:T(8,128)(2,1)}, bf16[2,4,80,384]{3,2,1,0:T(8,128)(2,1)}, bf16[2,4,80,384]{3,2,1,0:T(8...) custom-call(s32[1,4096]{1,0:T(1,128)} %bitcast.15, ...), custom_call_target="tpu_custom_call" | custom-call | flops 16384000000 | bytes 41943040 | tf_op jit(solution)/shard_map/backward_first/pallas_call | solution.py:1134
  159.1 0.6 pad_add_fusion.s
  159.8 11.2 %finish.1 = (bf16[1,4096,384]{2,1,0:T(8,128)(2,1)}, f32[1,4096,384]{2,1,0:T(8,128)}, f32[1,96]{1,0:T(1,128)}, f32[1,96]{1,0:T(1,128)}, f32[1,96,1152]{2,1,0:T(8,...) custom-call(s32[2]{0:T(128)} %pad_add_fusion.s, ...), custom_call_target="tpu_custom_call" | custom-call | bytes 16777216 | tf_op jit(solution)/shard_map/finish/pallas_call | solution.py:1237

commit v4 on v3

--- a/solution.py
+++ b/solution.py
@@ -196,8 +196,25 @@
     pipelined(units_of(width), DEPTH, [raw_scores, softmax, context])
 
 
-def attend_back(seg, qkv, prob, grad_context, grad_qkv, width):
+def span(start, size):
+    return pl.ds(start if isinstance(start, int) else pl.multiple_of(start, PAIR), size)
+
+
+def attend_back(seg, qkv, prob, grad_context, grad_qkv, pairs, sequences, place_in):
     once = Once()
+    width = qkv.shape[1] // 3
+    per_step = PROB_ROWS * (width // PAIR)
+
+    def rows_of(unit):
+        sequence, slot, block = unit
+        lo, hi = WINDOWS[sequence % 2][1][block]
+        return sequence * S, block * HALF, lo, hi
+
+    def pair_of(unit):
+        return pairs[unit[1]]
+
+    def columns(unit, part):
+        return span(part * width + pair_of(unit) * PAIR, PAIR)
 
     def padding_of(unit):
         base = unit[0] * S
@@ -210,25 +227,26 @@
         return once.get_or(("padding", unit[0]), make)
 
     def keys_of(unit):
-        base, left, _, _, _ = place_of(unit)
-        cols = slice(width + left, width + left + PAIR)
-        return once.get_or(("keys", unit[:2]), lambda: qkv[base : base + S, cols].T)
+        base = unit[0] * S
+        return once.get_or(("keys", unit[:2]), lambda: qkv[base : base + S, columns(unit, 1)].T)
 
     def grads_of(unit):
-        base, left, at, _, _ = place_of(unit)
+        base, at, _, _ = rows_of(unit)
         rows = slice(base + at, base + at + HALF)
-        return once.get_or(("grads", unit), lambda: split_pair(grad_context[rows, left : left + PAIR]))
+        return once.get_or(("grads", unit), lambda: split_pair(grad_context[rows, columns(unit, 0)]))
 
     def grad_probs(unit):
-        base, left, _, lo, hi = place_of(unit)
+        base, _, lo, hi = rows_of(unit)
         keys_of(unit)
-        return nt(qkv[base + lo : base + hi, 2 * width + left : 2 * width + left + PAIR], grads_of(unit))
+        return nt(qkv[base + lo : base + hi, columns(unit, 2)], grads_of(unit))
 
     def grad_scores(unit, grads):
-        sequence, pair, block = unit
-        _, _, _, lo, hi = place_of(unit)
-        offset = prob_offset(pair, sequence, block)
-        probs_low = prob[offset : offset + hi - lo, :]
+        sequence, _, block = unit
+        _, _, lo, hi = rows_of(unit)
+        start = sequence // 2 * per_step + prob_offset(0, sequence % 2, block)
+        pair = pair_of(unit)
+        start = start + pair * PROB_ROWS if isinstance(pair, int) else pl.multiple_of(start + pair * PROB_ROWS, 16)
+        probs_low = prob[pl.ds(start, hi - lo), :]
         probs = probs_low.astype(F32)
         product = probs * grads
         inner = jnp.sum(product, axis=0, keepdims=True)
@@ -236,25 +254,23 @@
 
     def grad_rows(unit, given):
         grad_raw, probs_low = given
-        base, left, at, lo, hi = place_of(unit)
-        queries = split_pair(qkv[base + at : base + at + HALF, left : left + PAIR])
+        base, at, lo, hi = rows_of(unit)
+        pair = pair_of(unit)
+        queries = split_pair(qkv[base + at : base + at + HALF, columns(unit, 0)])
         grad_values = padded(nn(probs_low, grads_of(unit)), lo, hi)
         grad_keys = padded(nn(grad_raw, queries), lo, hi)
         grad_queries = diagonal(nn(keys_of(unit), padded(grad_raw, lo, hi))) * SCALE
-        grad_qkv[base + at : base + at + HALF, left : left + PAIR] = grad_queries.astype(BF16).T
+        grad_qkv[base + at : base + at + HALF, span(place_in(0, pair), PAIR)] = grad_queries.astype(BF16).T
         if unit[2] == 0:
             once["first", unit[:2]] = grad_values, grad_keys
             return
         other_values, other_keys = once["first", unit[:2]]
-        own = jnp.where(padding_of(unit), grad_context[base : base + S, left : left + PAIR].astype(F32), 0.0)
-        grad_qkv[base : base + S, width + left : width + left + PAIR] = (
-            (other_keys + grad_keys) * SCALE
-        ).astype(BF16)
-        grad_qkv[base : base + S, 2 * width + left : 2 * width + left + PAIR] = (
-            other_values + grad_values + own
-        ).astype(BF16)
-
-    pipelined(units_of(width), DEPTH, [grad_probs, grad_scores, grad_rows])
+        own = jnp.where(padding_of(unit), grad_context[base : base + S, columns(unit, 0)].astype(F32), 0.0)
+        grad_qkv[base : base + S, span(place_in(1, pair), PAIR)] = ((other_keys + grad_keys) * SCALE).astype(BF16)
+        grad_qkv[base : base + S, span(place_in(2, pair), PAIR)] = (other_values + grad_values + own).astype(BF16)
+
+    units = [(q, slot, block) for q in range(sequences) for slot in range(len(pairs)) for block in range(2)]
+    pipelined(units, DEPTH, [grad_probs, grad_scores, grad_rows])
 
 
 def vector(vec, row, count=1):
@@ -262,7 +278,7 @@
     return parts[0] if count == 1 else jnp.concatenate(parts, axis=1)
 
 
-def forward(x, seg, weights, kept, y, after_attention=None):
+def forward(x, seg, weights, kept, y, before_weights=None, after_attention=None):
     vec, w_qkv, w_proj, w_fc1, w_fc2 = weights
     xhat1, r1, qkv, prob, ctx_t, xhat2, r2, act, dgelu = kept
     _, width = x.shape
@@ -270,6 +286,8 @@
     scaled, inverse = normalized(x[...].astype(F32))
     xhat1[...] = scaled.astype(BF16)
     r1[...] = inverse
+    if before_weights is not None:
+        before_weights()
     normed = (scaled * vector(vec, ATTN_GAIN) + vector(vec, ATTN_SHIFT)).astype(BF16)
     for part, bias in ((0, Q_BIAS), (1, None), (2, V_BIAS)):
         mixed = nn(normed, w_qkv[0, :, part * width : (part + 1) * width])
@@ -363,7 +381,10 @@
     sum_qkv, sum_vec = sums[0], sums[4]
     rows, width = grad_after.shape
     add = adder(sum_vec, width)
-    attend_back(seg, qkv, prob, grad_context, grad_qkv, width)
+    attend_back(
+        seg, qkv, prob, grad_context, grad_qkv, list(range(width // PAIR)), rows // S,
+        lambda part, pair: part * width + pair * PAIR,
+    )
     if halfway is not None:
         halfway()
     scaled = xhat1[...].astype(F32)
@@ -417,6 +438,15 @@
             store(whole[member * share : (member + 1) * share], member, block)
 
 
+def write_block(whole, members, store):
+    share = whole.shape[0] // members
+    size = half_rows(share)
+    for member in range(members):
+        rows = whole[member * share : (member + 1) * share]
+        store(0, member * size, rows[:size])
+        store(1, member * size, rows[share - size :])
+
+
 def vector_sums(sum_vec):
     return jnp.sum(sum_vec[...].reshape(VECTORS, 8, sum_vec.shape[1]), axis=1).astype(BF16)
 
@@ -805,7 +835,6 @@
             greet([partner])
             for i in order:
                 push(i, section).start()
-            layer_zero(order[:2])
 
         @pl.when(step == 1)
         def _():
@@ -822,12 +851,17 @@
             for i in order:
                 store(i).start()
 
+        def before_weights():
+            @pl.when(step == 0)
+            def _():
+                layer_zero(order[:2])
+
         def after_attention():
             @pl.when(step == 0)
             def _():
                 layer_zero(order[2:])
 
-        forward(x, seg, held, kept, y, after_attention)
+        forward(x, seg, held, kept, y, before_weights, after_attention)
 
         @pl.when(step == steps - 1)
         def _():
@@ -862,7 +896,7 @@
     fc1, fc2, proj = list(range(parts)), list(range(parts, 2 * parts)), 2 * parts
     qkv = [proj + 1, proj + 2, proj + 3]
     upper = (fc2 + fc1[: parts // 2], fc1[parts // 2 :] + [proj] + qkv)
-    lower = (fc2, fc1 + [proj], qkv)
+    lower = (fc2, fc1 + [proj])
     return upper, lower
 
 
@@ -876,14 +910,18 @@
     late_shape = Near(members, len(late) * size, width).source_shape()
 
     def body(x, seg, cot, vec, w_qkv, w_proj, w_fc1, w_fc2, *refs):
-        outs, sums, attn_kept, mlp_kept, rest, sems, near_refs = take(
-            refs, 6, 5, 4, 5, 6, 2, len(near.scratch())
+        outs, sums, attn_kept, mlp_kept, rest, sems, later, near_refs = take(
+            refs, 6, 5, 4, 5, 6, 3, 3, len(near.scratch())
         )
         y_own, y_got, g, late_out, total_out, vec_out = outs
         grad_after, grad_context, grad_qkv, y, y_send, early_out = rest
-        send, recv = sems
+        send, recv, load = sems
         near.bind(near_refs, early_out)
-        weights = (vec, w_qkv, w_proj, w_fc1, w_fc2)
+        loads = [
+            pltpu.make_async_copy(w.at[pl.ds(1, 1)], held, load.at[i])
+            for i, (w, held) in enumerate(zip((w_proj, w_fc1, w_fc2), later))
+        ]
+        weights = (vec, w_qkv, *later)
         step = pl.program_id(0)
         section, group, member = place()
 
@@ -894,12 +932,20 @@
 
         @pl.when(step == 0)
         def _():
+            for copy in loads:
+                copy.start()
             clear(sums)
             greet(near_peers(members, False))
 
         @pl.when(step < steps)
         def _():
-            forward(x, seg, weights, [ref.at[step] for ref in attn_kept] + mlp_kept, y)
+            def after_attention():
+                @pl.when(step == 0)
+                def _():
+                    for copy in loads:
+                        copy.wait()
+
+            forward(x, seg, weights, [ref.at[step] for ref in attn_kept] + mlp_kept, y, None, after_attention)
             y_own[...] = jnp.where(section == 0, x[...], y[...])
             y_send[step] = jnp.where(section == 0, y[...], x[...])
             y_copy(step).start()
@@ -959,7 +1005,11 @@
             block_at((1, STEP), 1, mine(lambda i: lax.rem(i, steps))),
             block_at((STEP, width), 0, mine(first)),
         ]
-        + [pl.BlockSpec((1,) + w.shape[1:], lambda i: (1, 0, 0), pipeline_mode=pl.Buffered(1)) for w in weights],
+        + [
+            pl.BlockSpec((1,) + w.shape[1:], lambda i: (1, 0, 0), pipeline_mode=pl.Buffered(1))
+            for w in weights[:2]
+        ]
+        + [ANYWHERE] * 3,
         out_specs=[block_at((STEP, width), 0, first), ANYWHERE, block_at((STEP, width), 0, then)]
         + [fixed(shape) for shape in fixed_outs],
         out_shape=[rows] * 3 + [jax.ShapeDtypeStruct(shape, BF16) for shape in fixed_outs],
@@ -975,6 +1025,8 @@
             pltpu.VMEM(near.source_shape(), BF16),
         ]
         + [pltpu.SemaphoreType.DMA((steps,))] * 2
+        + [pltpu.SemaphoreType.DMA((3,))]
+        + [pltpu.VMEM((1,) + w.shape[1:], w.dtype) for w in weights[2:]]
         + near.scratch(),
         compiler_params=params(1),
         cost_estimate=cost(steps * STEP * 12000000, 20),
@@ -986,231 +1038,341 @@
     width, hidden = dout.shape[1], weights[3].shape[2]
     shapes = kept_shapes(steps, width, hidden)
     size = half_rows(width // members)
+    pairs = width // PAIR
+    rows = steps * STEP
     (upper_early, upper_late), lower = block_lists(hidden // width)
-    fars = [
-        Far(target, groups, len(blocks) * size, width)
-        for target, blocks in [(1, upper_early), (1, upper_late)] + [(0, blocks) for blocks in lower]
-    ]
-    nears = [Near(members, len(blocks) * size, width) for blocks in (upper_late,) + lower]
+    counts = [len(blocks) * size for blocks in (upper_early, upper_late) + lower] + [size] * pairs
+    fars = [Far(1 if i < 2 else 0, groups, count, width) for i, count in enumerate(counts)]
+    nears = [Near(members, count, width) for count in counts[1:]]
     vector_plans = [VectorSum(groups, members, width) for _ in range(2)]
     plans = fars + nears + vector_plans
-
-    def body(seg, dout, vec, w_qkv, w_proj, w_fc1, w_fc2, *refs):
-        kept, (late1, total1, vec1), (g_own, g_got), results, vec_outs, sums, rest, sources, totals, sems, *bound = take(
-            refs, 9, 3, 2, 5, 2, 5, 4, 3, 4, 2, *[len(plan.scratch()) for plan in plans]
+    starts = [0, steps, 2 * steps, 2 * steps + pairs, 3 * steps + pairs]
+    last = starts[4] - 1
+
+    def body(seg, dout, act, ctx_t, xhat2, r2, dgelu, vec, late1, total1, vec1, *refs):
+        attn_in, weights_in, (g_own, g_got), results, vec_outs, *refs = take(
+            refs, 4, 4, 2, len(fars), 2, len(refs) - 12 - len(fars)
         )
-        grad_after, grad_context, grad_qkv, g_send = rest
-        send, recv = sems
-        for plan, plan_refs, total, result in zip(fars, bound[:5], [total1] + list(totals), results):
+        sums, rest, attn_kept, held, sources, totals, sems, *bound = take(
+            refs[0], 4, 8, 4, 4, 3, len(fars) - 1, 4, *[len(plan.scratch()) for plan in plans]
+        )
+        grad_after, grad_context, grad_qkv, g_send, scaled_t, paired, gain_part, shift_part = rest
+        send, recv, load, load_attn = sems
+        take_fars, take_nears = bound[: len(fars)], bound[len(fars) : len(fars) + len(nears)]
+        for plan, plan_refs, total, result in zip(fars, take_fars, [total1] + totals, results):
             plan.bind(plan_refs, total, result)
-        for plan, plan_refs, source in zip(nears, bound[5:9], [late1] + list(sources)):
+        pair_sources = [sources[2].at[pair] for pair in range(pairs)]
+        for plan, plan_refs, source in zip(nears, take_nears, [late1] + sources[:2] + pair_sources):
             plan.bind(plan_refs, source)
-        for plan, plan_refs in zip(vector_plans, bound[9:]):
+        for plan, plan_refs in zip(vector_plans, bound[len(fars) + len(nears) :]):
             plan.bind(plan_refs)
-        far_a, far_b, far_fc2, far_fc1, far_qkv = fars
-        near_b, near_fc2, near_fc1, near_qkv = nears
-        total_b, total_fc2, total_fc1, total_qkv = totals
+        far_a, far_b, far_fc2, far_fc1, *far_pairs = fars
+        near_b, near_fc2, near_fc1, *near_pairs = nears
+        total_b, total_fc2, total_fc1, *total_pairs = totals
         upper_vec, lower_vec = vector_plans
+        sum_proj, sum_fc1, sum_fc2, sum_vec = sums
+        all_sums = (None, sum_proj, sum_fc1, sum_fc2, sum_vec)
+        w_qkv, w_proj, w_fc1, w_fc2 = held
         weights = (vec, w_qkv, w_proj, w_fc1, w_fc2)
-        xhat1, r1, qkv, prob, ctx_t, xhat2, r2, act, dgelu = kept
+        xhat1, r1, qkv, prob = attn_kept
         step = pl.program_id(0)
         section, group, member = place()
+        loads = [pltpu.make_async_copy(a.at[pl.ds(0, 1)], b, load.at[i]) for i, (a, b) in enumerate(zip(weights_in, held))]
+        loads_attn = [pltpu.make_async_copy(a, b, load_attn.at[i]) for i, (a, b) in enumerate(zip(attn_in, attn_kept))]
 
         def g_copy(index):
             return remote(
                 g_send.at[index], g_got.at[rows_at(index, STEP)], send.at[index], recv.at[index], (1 - section, group, member)
             )
 
-        @pl.when(step == 0)
-        def _():
+        def at(number, offset=0):
+            return pl.when(step == starts[number] + offset)
+
+        def phase(number):
+            return pl.when(jnp.logical_and(step >= starts[number], step < starts[number + 1]))
+
+        @at(0)
+        def _():
+            for copy in loads + loads_attn:
+                copy.start()
+            clear(sums)
             greet(near_peers(members, True) + far_peers(groups))
             near_b.start_section()
             far_a.start_groups()
             upper_vec.start(vec1[...])
-            clear(sums)
-
-        @pl.when(step == steps)
+
+        @at(0, steps // 2)
         def _():
             near_b.start_members()
 
-        @pl.when(step == steps + 1)
+        @phase(0)
+        def _():
+            g_send[step] = dout[...]
+            backward_fc2(dout, act, all_sums)
+
+        @at(1, -1)
+        def _():
+            write_blocks(all_sums, members, lower[0], near_fc2.source)
+            near_fc2.start_section()
+
+        @at(1)
+        def _():
+            for copy in loads:
+                copy.wait()
+
+        @at(1, 1)
         def _():
             near_fc2.start_members()
             far_a.start_gather()
             upper_vec.start_far()
 
-        @pl.when(step == 2 * steps)
+        @at(2, -1)
         def _():
             near_b.finish(total_b)
             far_b.start_groups()
             vec_outs[0][...] = upper_vec.finish()
 
-        @pl.when(step == 2 * steps + 1)
-        def _():
-            near_fc1.start_members()
-
-        @pl.when(step == 2 * steps + 2)
+        @phase(1)
+        def _():
+            index = step - starts[1]
+
+            def write(after, context):
+                grad_after[index] = after
+                grad_context[rows_at(index, STEP), :] = context
+
+            backward_mlp(g_send.at[index], weights, (ctx_t, xhat2, r2, None, dgelu), all_sums, write, False)
+
+        @at(2, -1)
+        def _():
+            write_blocks(all_sums, members, lower[1], near_fc1.source)
+            near_fc1.start_section()
+
+        @at(2)
+        def _():
+            for copy in loads_attn:
+                copy.wait()
+            for chunk in range(steps):
+                here = slice(chunk * STEP, (chunk + 1) * STEP)
+                scaled_t[:width, here] = xhat1[here, :].T
+            scaled_t[width:, :] = jnp.ones((16, rows), BF16)
+            for pair in range(pairs):
+                for part in range(3):
+                    left = (3 * pair + part) * PAIR
+                    source = part * width + pair * PAIR
+                    paired[:, left : left + PAIR] = w_qkv[0, :, source : source + PAIR]
+            gain_part[...] = jnp.zeros_like(gain_part)
+            shift_part[...] = jnp.zeros_like(shift_part)
+
+        @at(2, 1)
         def _():
             near_fc2.finish(total_fc2)
             far_fc2.start_groups()
             far_b.start_gather()
 
-        @pl.when(step == 2 * steps + 3)
-        def _():
-            far_fc2.start_gather()
-
-        @pl.when(step < steps)
-        def _():
-            g_send[step] = dout[...]
-            backward_fc2(dout, act, sums)
-
-        @pl.when(step == steps - 1)
-        def _():
-            write_blocks(sums, members, lower[0], near_fc2.source)
-            near_fc2.start_section()
-
-        @pl.when(jnp.logical_and(step >= steps, step < 2 * steps))
-        def _():
-            index = step - steps
-
-            def write(after, context):
-                grad_after[index] = after
-                grad_context[index] = context
-
-            backward_mlp(g_send.at[index], weights, (ctx_t, xhat2, r2, None, dgelu), sums, write, False)
-
-        @pl.when(step == 2 * steps - 1)
-        def _():
-            write_blocks(sums, members, lower[1], near_fc1.source)
-            near_fc1.start_section()
-
-        @pl.when(step >= 2 * steps)
-        def _():
-            index = step - 2 * steps
-
-            def write(values):
-                low = values.astype(BF16)
-                upper_rows = g_send[index]
-                g_own[...] = jnp.where(section == 0, low, upper_rows)
-                g_send[index] = jnp.where(section == 0, upper_rows, low)
-                g_copy(index).start()
-
-            backward_attn(
-                grad_after.at[index], grad_context.at[index], seg, weights, (xhat1, r1, qkv, prob), sums, grad_qkv, write
+        @at(2, 2)
+        def _():
+            near_pairs[0].start_members()
+
+        @phase(2)
+        def _():
+            pair = step - starts[2]
+            attend_back(
+                seg, qkv, prob, grad_context, grad_qkv, [pair], 2 * steps,
+                lambda part, pair: pair * width + part * PAIR,
             )
 
-        @pl.when(step == 3 * steps - 1)
-        def _():
-            write_blocks(sums, members, lower[2], near_qkv.source)
-            near_qkv.start_section()
-            lower_vec.start(vector_sums(sums[4]))
+            @at(2)
+            def _():
+                near_fc1.start_members()
+
+            here = span(pair * width, width)
+            product = nn(scaled_t[...], grad_qkv[:, here])
+            scaled_sum, columns = product[:width], product[width : width + 1]
+            weight = paired[:, here].astype(F32)
+            gained, shifted = scaled_sum * weight, columns * weight
+            for part in range(3):
+                cols = slice(part * PAIR, (part + 1) * PAIR)
+                gain_part[...] += gained[:, cols]
+                shift_part[...] += shifted[:, cols]
+            sum_vec[Q_BIAS * 8 : Q_BIAS * 8 + 1, span(pair * PAIR, PAIR)] = columns[:, :PAIR]
+            sum_vec[V_BIAS * 8 : V_BIAS * 8 + 1, span(pair * PAIR, PAIR)] = columns[:, 2 * PAIR :]
+            gain, shift = [
+                jnp.broadcast_to(vector(vec, row), (8, width)).T[:, :1] for row in (ATTN_GAIN, ATTN_SHIFT)
+            ]
+            whole = (scaled_sum * gain + shift * columns).astype(BF16)
+
+            def store(half, top, rows):
+                sources[2][pair, half, top : top + size, :] = rows
+
+            write_block(whole, members, store)
+
+        for pair in range(pairs):
+
+            @at(2, pair)
+            def _(pair=pair):
+                near_pairs[pair].start_section()
+
+        @at(3)
+        def _():
+            sum_vec[ATTN_GAIN * 8 : ATTN_GAIN * 8 + 1, :] = jnp.sum(gain_part[...].T, axis=0, keepdims=True)
+            sum_vec[ATTN_SHIFT * 8 : ATTN_SHIFT * 8 + 1, :] = jnp.sum(shift_part[...].T, axis=0, keepdims=True)
+            lower_vec.start(vector_sums(sum_vec))
+            near_pairs[1].start_members()
             near_fc1.finish(total_fc1)
             far_fc1.start_groups()
-            near_qkv.start_members()
+            far_fc2.start_gather()
+
+        @at(3, 1)
+        def _():
+            near_pairs[2].start_members()
+
+        @at(3, 2)
+        def _():
+            near_pairs[0].finish(total_pairs[0])
+            far_pairs[0].start_groups()
             lower_vec.start_far()
+
+        @at(3, 3)
+        def _():
+            near_pairs[1].finish(total_pairs[1])
+            far_pairs[1].start_groups()
+
+        @phase(3)
+        def _():
+            index = step - starts[3]
+            here = rows_at(index, STEP)
+            grad_normed = nt(grad_qkv[here, :], paired[...])
+            scaled = xhat1[here, :].astype(F32)
+            grads = grad_after[index] + norm_back(scaled, r1[here, :], vector(vec, ATTN_GAIN), grad_normed)
+            low = grads.astype(BF16)
+            upper_rows = g_send[index]
+            g_own[...] = jnp.where(section == 0, low, upper_rows)
+            g_send[index] = jnp.where(section == 0, upper_rows, low)
+            g_copy(index).start()
+
+        @at(4, -1)
+        def _():
+            for pair in range(2, pairs):
+                near_pairs[pair].finish(total_pairs[pair])
+                far_pairs[pair].start_groups()
             far_fc1.start_gather()
+            vec_outs[1][...] = lower_vec.finish()
+            for far in far_pairs:
+                far.start_gather()
             for index in range(steps):
                 g_copy(index).wait()
-            far_a.finish()
-            far_b.finish()
-            far_fc2.finish()
-            vec_outs[1][...] = lower_vec.finish()
-            near_qkv.finish(total_qkv)
-            far_qkv.start_groups()
-            far_qkv.start_gather()
-            far_fc1.finish()
-            far_qkv.finish()
-
-    def phase(number):
-        return lambda i: jnp.clip(i - number * steps, 0, steps - 1)
-
-    def kept_spec(number, entry):
-        _, _, block, axis = entry
-        return block_at(block, axis, phase(number))
-
-    phases = (2, 2, 2, 2, 1, 1, 1, 0, 1)
-    low_rows = jax.ShapeDtypeStruct((steps * STEP, width), BF16)
+            for far in fars:
+                far.finish()
+
+    def clipped(number):
+        return lambda i: jnp.clip(i - starts[number], 0, steps - 1)
+
+    low_rows = jax.ShapeDtypeStruct((rows, width), BF16)
     vec_shape = (VECTORS, width)
+    xhat1, r1, qkv, prob, ctx_t, xhat2, r2, act, dgelu = kept
+    attn_in = (xhat1, r1, qkv, prob)
     return pl.pallas_call(
         body,
-        grid=(3 * steps,),
+        grid=(starts[4],),
         in_specs=[
-            block_at((1, STEP), 1, lambda i: lax.axis_index("section") * steps + phase(2)(i)),
-            block_at((STEP, width), 0, phase(0)),
+            block_at((1, rows), 1, lambda i: lax.axis_index("section")),
+            block_at((STEP, width), 0, clipped(0)),
+            block_at((STEP, hidden), 0, clipped(0)),
+            block_at((width, STEP), 1, clipped(1)),
+            block_at((STEP, width), 0, clipped(1)),
+            block_at((STEP, 1), 0, clipped(1)),
+            block_at((STEP, hidden), 0, clipped(1)),
+            fixed((1, VECTORS, width)),
+            fixed(late1.shape),
+            fixed(total1.shape),
+            fixed(vec_shape),
         ]
-        + [fixed((1,) + w.shape[1:]) for w in weights]
-        + [kept_spec(number, entry) for number, entry in zip(phases, shapes)]
-        + [fixed(late1.shape), fixed(total1.shape), fixed(vec_shape)],
-        out_specs=[block_at((STEP, width), 0, phase(2)), ANYWHERE] + [ANYWHERE] * 5 + [fixed(vec_shape)] * 2,
+        + [ANYWHERE] * 8,
+        out_specs=[block_at((STEP, width), 0, clipped(3)), ANYWHERE]
+        + [ANYWHERE] * len(fars)
+        + [fixed(vec_shape)] * 2,
         out_shape=[low_rows] * 2
         + [jax.ShapeDtypeStruct(far.result_shape(), BF16) for far in fars]
         + [jax.ShapeDtypeStruct(vec_shape, F32)] * 2,
-        scratch_shapes=sum_scratch(width, hidden)
+        scratch_shapes=sum_scratch(width, hidden)[1:]
         + [
             pltpu.VMEM((steps, STEP, width), F32),
+            pltpu.VMEM((rows, width), BF16),
+            pltpu.VMEM((rows, 3 * width), BF16),
             pltpu.VMEM((steps, STEP, width), BF16),
-            pltpu.VMEM((STEP, 3 * width), BF16),
-            pltpu.VMEM((steps, STEP, width), BF16),
+            pltpu.VMEM((width + 16, rows), BF16),
+            pltpu.VMEM((width, 3 * width), BF16),
+            pltpu.VMEM((width, PAIR), F32),
+            pltpu.VMEM((width, PAIR), F32),
         ]
-        + [pltpu.VMEM(near.source_shape(), BF16) for near in nears[1:]]
+        + [pltpu.VMEM(a.shape, a.dtype) for a in attn_in]
+        + [pltpu.VMEM((1,) + w.shape[1:], w.dtype) for w in weights[1:]]
+        + [pltpu.VMEM(near.source_shape(), BF16) for near in nears[1:3]]
+        + [pltpu.VMEM((pairs,) + nears[3].source_shape(), BF16)]
         + [pltpu.VMEM(far.total_shape(), BF16) for far in fars[1:]]
         + [pltpu.SemaphoreType.DMA((steps,))] * 2
+        + [pltpu.SemaphoreType.DMA((4,))] * 2
         + [item for plan in plans for item in plan.scratch()],
         compiler_params=params(2),
-        cost_estimate=cost(steps * STEP * 8000000, 40),
+        cost_estimate=cost(rows * 8000000, 40),
         name="backward_first",
-    )(seg, dout, *weights, *kept, late1, total1, vec1)
+    )(seg, dout, act, ctx_t, xhat2, r2, dgelu, weights[0], late1, total1, vec1, *attn_in, *weights[1:])
 
 
 def finish(y_own, y_got, g_own, g_got, results, vec_sums, width, hidden, steps, members):
     parts = hidden // width
+    pairs = width // PAIR
     share = width // members
     size = half_rows(share)
     upper, lower = block_lists(parts)
-    lists = list(upper) + list(lower)
     results = [result.reshape(2, -1, width) for result in results]
-    at = jnp.stack([lax.axis_index("section"), lax.axis_index("member")]).astype(jnp.int32)
-
-    def body(s, y_own, y_got, g_own, g_got, *refs):
-        results, (upper_vec, lower_vec), (acts, grads), outs = take(refs, 5, 2, 2, 12)
+    tall = 2 * STEP
+    steps = steps // 2
+
+    def body(y_own, y_got, g_own, g_got, *refs):
+        results, (upper_vec, lower_vec), (acts, grads), outs = take(refs, len(results_in), 2, 2, 12)
         a_gain, a_shift, d_qkv, d_qv, d_proj, b_proj, m_gain, m_shift, d_fc1, b_fc1, d_fc2, b_fc2 = outs
         step = pl.program_id(0)
-        first = s[0] == 0
-        mine = step // steps == s[0]
+        section, member = lax.axis_index("section"), lax.axis_index("member")
+        mine = step // steps == section
         acts[0] = jnp.where(mine, y_own[...], y_got[...])
         grads[0] = jnp.where(mine, g_own[...], g_got[...]).astype(F32)
 
-        def rows_of(which, block, half):
-            for blocks, result in list(zip(lists, results))[which]:
+        def rows_of(lists, results, block, half):
+            for blocks, result in zip(lists, results):
                 if block in blocks:
                     top = blocks.index(block) * size
                     return result[half, top : top + size, :].astype(F32)
             raise KeyError(block)
 
-        @pl.when(step == 0)
-        def _():
-            for block in range(2 * parts + 4):
-                for half in range(2):
-                    top = half * (share - size)
-                    rows = jnp.where(first, rows_of(slice(2, 5), block, half), rows_of(slice(0, 2), block, half))
+        def write(lists, results, vec_sum, paired):
+            for half in range(2):
+                top = half * (share - size)
+                for block in range(2 * parts + 1):
+                    rows = rows_of(lists, results, block, half)
                     if block < parts:
                         d_fc1[0, top : top + size, block * width : (block + 1) * width] = rows
                     elif block < 2 * parts:
                         base = (block - parts) * share + top
                         d_fc2[0, base : base + size, :] = rows
-                    elif block == 2 * parts:
+                    else:
                         d_proj[0, top : top + size, :] = rows
+                for index in range(3):
+                    if paired:
+                        rows = results[len(lists) + index][half, :size, :].astype(F32)
+                        for part in range(3):
+                            left = part * width + index * PAIR
+                            d_qkv[0, top : top + size, left : left + PAIR] = rows[:, part * PAIR : (part + 1) * PAIR]
                     else:
-                        left = (block - 2 * parts - 1) * width
-                        d_qkv[0, top : top + size, left : left + width] = rows
-            vectors = jnp.where(first, lower_vec[...], upper_vec[...])
+                        rows = rows_of(lists, results, 2 * parts + 1 + index, half)
+                        d_qkv[0, top : top + size, index * width : (index + 1) * width] = rows
 
             def put(out, row, count=1):
-                flat = jnp.concatenate([vectors[row + i : row + i + 1, :] for i in range(count)], axis=1)
+                flat = jnp.concatenate([vec_sum[row + i : row + i + 1, :] for i in range(count)], axis=1)
                 length = count * width // members
                 value = flat[:, :length]
                 for m in range(1, members):
-                    value = jnp.where(s[1] == m, flat[:, m * length : (m + 1) * length], value)
+                    value = jnp.where(member == m, flat[:, m * length : (m + 1) * length], value)
                 out[...] = value
 
             put(a_gain, ATTN_GAIN)
@@ -1222,26 +1384,34 @@
             put(b_fc1, FC1_BIAS, parts)
             put(b_fc2, FC2_BIAS)
 
+        @pl.when(jnp.logical_and(step == 0, section == 0))
+        def _():
+            write(lower, results[2:], lower_vec, True)
+
+        @pl.when(jnp.logical_and(step == 0, section == 1))
+        def _():
+            write(upper, results[:2], upper_vec, False)
+
     def whole(shape):
-        return pl.BlockSpec(shape, lambda i, s, n=len(shape): (0,) * n)
-
-    own = pl.BlockSpec((STEP, width), lambda i, s: (jnp.clip(i - s[0] * steps, 0, steps - 1), 0))
-    got = pl.BlockSpec((STEP, width), lambda i, s: (jnp.clip(i - (1 - s[0]) * steps, 0, steps - 1), 0))
-    total = 2 * steps * STEP
+        return pl.BlockSpec(shape, lambda i: (0,) * len(shape))
+
+    def rows_from(section):
+        return block_at((tall, width), 0, lambda i: jnp.clip(i - section() * steps, 0, steps - 1))
+
+    own = rows_from(lambda: lax.axis_index("section"))
+    got = rows_from(lambda: 1 - lax.axis_index("section"))
+    total = 2 * steps * tall
     smalls = [
         (1, share), (1, share), (1, share, 3 * width), (1, 2 * share), (1, share, width), (1, share), (1, share),
         (1, share), (1, share, hidden), (1, hidden // members), (1, hidden // members, width), (1, share),
     ]
-    rows_spec = pl.BlockSpec((1, STEP, width), lambda i, s: (0, i, 0))
-    inputs = results + list(vec_sums)
+    rows_spec = pl.BlockSpec((1, tall, width), lambda i: (0, i, 0))
+    results_in = results
     return pl.pallas_call(
         body,
-        grid_spec=pltpu.PrefetchScalarGridSpec(
-            num_scalar_prefetch=1,
-            grid=(2 * steps,),
-            in_specs=[own, got, own, got] + [whole(x.shape) for x in inputs],
-            out_specs=[rows_spec, rows_spec] + [whole(shape) for shape in smalls],
-        ),
+        grid=(2 * steps,),
+        in_specs=[own, got, own, got] + [whole(x.shape) for x in results + list(vec_sums)],
+        out_specs=[rows_spec, rows_spec] + [whole(shape) for shape in smalls],
         out_shape=[
             jax.ShapeDtypeStruct((1, total, width), BF16),
             jax.ShapeDtypeStruct((1, total, width), F32),
@@ -1250,7 +1420,7 @@
         compiler_params=pltpu.CompilerParams(vmem_limit_bytes=62 * MIB),
         cost_estimate=cost(0, 16),
         name="finish",
-    )(at, y_own, y_got, g_own, g_got, *inputs)
+    )(y_own, y_got, g_own, g_got, *results, *vec_sums)
 
 
 def per_device(
@@ -1282,7 +1452,7 @@
     kept, weights = rest[:9], rest[9:]
     y_own, y_got, g1, late1, total1, vec1 = second_layer(y0, seg, cotangent, weights, steps, groups, members)
     g_own, g_got, *grads = first_backward(seg, g1, late1, total1, vec1, kept, weights, steps, groups, members)
-    return tuple(finish(y_own, y_got, g_own, g_got, grads[:5], grads[5:], width, hidden, steps, members))
+    return tuple(finish(y_own, y_got, g_own, g_got, grads[:-2], grads[-2:], width, hidden, steps, members))
 
 
 def solution(mesh):

time: 172 us -> 164 us (0.953)
  Pallas kernels: 170 us -> 163 us
    pallas_call x2, Pallas kernels: 82.2 us -> 75.4 us  [the longest x1 66.3 us: first_backward(): pl.pallas_call(body, grid=(starts[4],), in_specs=[block_at((1, rows), 1,...]
where the time goes in v4:
time: 164 us
  Pallas kernels  163 us (99%)
    pallas_call x1, Pallas kernels, first_backward(): pl.pallas_call(body, grid=(starts[4],), in_specs=[block_at((1, rows), 1,...  66.3 us
    pallas_call x1, Pallas kernels, second_layer(): pl.pallas_call(body, grid=(2 * steps,), in_specs=[block_at((STEP, width),...  60.9 us
    pallas_call x1, Pallas kernels, first_forward(): pl.pallas_call(body, grid=(steps,), in_specs=[block_at((STEP, width), 0,...  26.3 us
    pallas_call x1, Pallas kernels, finish(): pl.pallas_call(body, grid=(2 * steps,), in_specs=[own, got, own, got] + [...  9.1 us

profile of v4, /device:TPU:0, one launch (start us, length us, event | category | flops | bytes accessed | tf_op | source)
XLA Modules:
  0.0 163.5 jit_solution(1595602315724314960)
XLA Ops:
  0.7 26.3 %forward_first.1 = (bf16[2048,384]{1,0:T(8,128)(2,1)}, bf16[2048,384]{1,0:T(8,128)(2,1)}, f32[2048,1]{1,0:T(8,128)}, bf16[2048,1152]{1,0:T(8,128)(2,1)}, bf16[84...) custom-call(bf16[4096,384]{1,0:T(8,128)(2,1)} %x.1, ...), custom_call_target="tpu_custom_call" | custom-call | flops 8192000000 | bytes 41943040 | tf_op jit(solution)/shard_map/forward_first/pallas_call | solution.py:875
  27.0 60.9 %second_layer.1 = (bf16[2048,384]{1,0:T(8,128)(2,1)}, bf16[2048,384]{1,0:T(8,128)(2,1)}, bf16[2048,384]{1,0:T(8,128)(2,1)}, bf16[2,1152,384]{2,1,0:T(8,128)(2,1)...) custom-call(bf16[2048,384]{1,0:T(8,128)(2,1)} %get-tuple-element.46.x, s32[1,4096]{1,0:T(1,128)} %bitcast.16, ...), custom_call_target="tpu_custom_call" | custom-call | flops 24576000000 | bytes 20971520 | tf_op jit(solution)/shard_map/second_layer/pallas_call | solution.py:1000
  87.9 66.3 %backward_first.1 = (bf16[2048,384]{1,0:T(8,128)(2,1)}, bf16[2048,384]{1,0:T(8,128)(2,1)}, bf16[2,4,80,384]{3,2,1,0:T(8,128)(2,1)}, bf16[2,4,80,384]{3,2,1,0:T(8...) custom-call(s32[1,4096]{1,0:T(1,128)} %bitcast.17, ...), custom_call_target="tpu_custom_call" | custom-call | flops 16384000000 | bytes 41943040 | tf_op jit(solution)/shard_map/backward_first/pallas_call | solution.py:1274
  154.2 9.1 %finish.1 = (bf16[1,4096,384]{2,1,0:T(8,128)(2,1)}, f32[1,4096,384]{2,1,0:T(8,128)}, f32[1,96]{1,0:T(1,128)}, f32[1,96]{1,0:T(1,128)}, f32[1,96,1152]{2,1,0:T(8,...) custom-call(bf16[2048,384]{1,0:T(8,128)(2,1)} %get-tuple-element.52., ...), custom_call_target="tpu_custom_call" | custom-call | bytes 16777216 | tf_op jit(solution)/shard_map/finish/pallas_call | solution.py:1410

commit v5 on v4

--- a/solution.py
+++ b/solution.py
@@ -15,9 +15,10 @@
 EPS = 1e-06
 SCALE = HD ** (-0.5)
 LOG2E = 1.4426950408889634
-CHUNK = 768
+CHUNK = 1536
 FORWARD_CHUNK = 256
 DEPTH = 4
+INTERLEAVED = 6
 F32 = jnp.float32
 BF16 = jnp.bfloat16
 MIB = 1 << 20
@@ -125,6 +126,7 @@
             if 0 <= at < len(units):
                 before = [held[i - 1].pop(at)] if i else []
                 held[i][at] = stage(units[at], *before)
+                yield
 
 
 class Once(dict):
@@ -193,7 +195,7 @@
             valid_of(unit), mixed, own
         ).astype(BF16)
 
-    pipelined(units_of(width), DEPTH, [raw_scores, softmax, context])
+    yield from pipelined(units_of(width), DEPTH, [raw_scores, softmax, context])
 
 
 def span(start, size):
@@ -270,7 +272,8 @@
         grad_qkv[base : base + S, span(place_in(2, pair), PAIR)] = (other_values + grad_values + own).astype(BF16)
 
     units = [(q, slot, block) for q in range(sequences) for slot in range(len(pairs)) for block in range(2)]
-    pipelined(units, DEPTH, [grad_probs, grad_scores, grad_rows])
+    for _ in pipelined(units, DEPTH, [grad_probs, grad_scores, grad_rows]):
+        pass
 
 
 def vector(vec, row, count=1):
@@ -278,11 +281,10 @@
     return parts[0] if count == 1 else jnp.concatenate(parts, axis=1)
 
 
-def forward(x, seg, weights, kept, y, before_weights=None, after_attention=None):
-    vec, w_qkv, w_proj, w_fc1, w_fc2 = weights
-    xhat1, r1, qkv, prob, ctx_t, xhat2, r2, act, dgelu = kept
-    _, width = x.shape
-    hidden = w_fc1.shape[2]
+def forward_qkv(x, weights, kept, before_weights=None):
+    vec, w_qkv, _, _, _ = weights
+    xhat1, r1, qkv, _ = kept
+    width = x.shape[1]
     scaled, inverse = normalized(x[...].astype(F32))
     xhat1[...] = scaled.astype(BF16)
     r1[...] = inverse
@@ -294,15 +296,18 @@
         if bias is not None:
             mixed = mixed + vector(vec, bias)
         qkv[:, part * width : (part + 1) * width] = mixed.astype(BF16)
-    attend(seg, qkv, prob, ctx_t, width)
-    if after_attention is not None:
-        after_attention()
+
+
+def forward_mlp(x, weights, kept, y, between=None):
+    vec, _, w_proj, w_fc1, w_fc2 = weights
+    ctx_t, xhat2, r2, act, dgelu = kept
+    width = x.shape[1]
+    hidden = w_fc1.shape[2]
     after = x[...].astype(F32) + tn(ctx_t[...], w_proj[0]) + vector(vec, PROJ_BIAS)
     scaled, inverse = normalized(after)
     xhat2[...] = scaled.astype(BF16)
     r2[...] = inverse
     normed = (scaled * vector(vec, MLP_GAIN) + vector(vec, MLP_SHIFT)).astype(BF16)
-    output = after + vector(vec, FC2_BIAS)
     bias = vector(vec, FC1_BIAS, hidden // width)
     tops = list(range(0, hidden, FORWARD_CHUNK))
 
@@ -317,11 +322,20 @@
             coming = product(tops[i + 1])
         below = 0.5 + 0.5 * lax.erf(pre * (0.5**0.5))
         density = jnp.exp2(pre * pre * (-0.5 * LOG2E)) * (1.0 / (2.0 * jnp.pi) ** 0.5)
-        active = (pre * below).astype(BF16)
-        act[:, cols] = active
+        act[:, cols] = (pre * below).astype(BF16)
         dgelu[:, cols] = (below + pre * density).astype(BF16)
-        output = output + nn(active, w_fc2[0, cols, :])
-    y[...] = output.astype(BF16)
+        if between is not None:
+            between()
+    y[...] = (after + vector(vec, FC2_BIAS) + nn(act[...], w_fc2[0])).astype(BF16)
+
+
+def forward(x, seg, weights, kept, y, after_attention=None):
+    forward_qkv(x, weights, kept[:4])
+    for _ in attend(seg, kept[2], kept[3], kept[4], x.shape[1]):
+        pass
+    if after_attention is not None:
+        after_attention()
+    forward_mlp(x, weights, kept[4:], y)
 
 
 def adder(sum_vec, width):
@@ -593,7 +607,7 @@
             pltpu.VMEM((self.groups - 1, self.part, self.width), BF16),
             pltpu.VMEM((self.part, self.width), BF16),
             pltpu.SemaphoreType.DMA,
-        ] + [pltpu.SemaphoreType.DMA((n,)) for n in (self.groups,) * 2 + (2 * self.groups,) * 2]
+        ] + [pltpu.SemaphoreType.DMA((n,)) for n in (self.groups,) * 4 + (1, 1)]
 
     def bind(self, refs, total, result):
         self.from_groups, self.piece, self.local, *self.sems = refs
@@ -611,28 +625,39 @@
             (section, to, member),
         )
 
-    def gather_copy(self, offset, across):
+    def gather_copy(self, offset):
         section, group, member = place()
-        slot = across * self.groups + offset
         return remote(
             self.piece,
             self.result_ref.at[section, group],
-            self.sems[2].at[slot],
-            self.sems[3].at[slot],
-            (self.target, lax.rem(group + offset, self.groups), member),
+            self.sems[2].at[offset],
+            self.sems[3].at[offset],
+            (section, lax.rem(group + offset, self.groups), member),
         )
 
-    def gathered(self, offset, across):
+    def gathered(self, offset):
         section, group, member = place()
-        slot = across * self.groups + offset
         origin = lax.rem(group + self.groups - offset, self.groups)
-        half = 1 - section if across else section
         return remote(
             self.piece,
-            self.result_ref.at[half, origin],
-            self.sems[2].at[slot],
-            self.sems[3].at[slot],
-            (self.target, origin, member),
+            self.result_ref.at[section, origin],
+            self.sems[2].at[offset],
+            self.sems[3].at[offset],
+            (section, origin, member),
+        )
+
+    def keep_copy(self):
+        section, group, _ = place()
+        return pltpu.make_async_copy(self.piece, self.result_ref.at[section, group], self.local)
+
+    def half_copy(self, half):
+        section, group, member = place()
+        return remote(
+            self.result_ref.at[half],
+            self.result_ref.at[half],
+            self.sems[4].at[0],
+            self.sems[5].at[0],
+            (1 - section, group, member),
         )
 
     def start_groups(self):
@@ -647,35 +672,31 @@
         for offset in range(1, self.groups):
             total = total + self.from_groups[offset - 1].astype(F32)
         self.piece[...] = total.astype(BF16)
+        for offset in range(1, self.groups):
+            self.gather_copy(offset).start()
+        self.keep_copy().start()
+
+    def hand_over(self):
+        section = lax.axis_index("section")
+        for offset in range(1, self.groups):
+            self.gather_copy(offset).wait_send()
+            self.gathered(offset).wait_recv()
+        self.keep_copy().wait()
+
+        @pl.when(section != self.target)
+        def _():
+            self.half_copy(section).start()
+
+    def finish(self):
+        section = lax.axis_index("section")
+
+        @pl.when(section != self.target)
+        def _():
+            self.half_copy(section).wait_send()
 
         @pl.when(section == self.target)
         def _():
-            for offset in range(1, self.groups):
-                self.gather_copy(offset, 0).start()
-            keep = pltpu.make_async_copy(self.piece, self.result_ref.at[section, group], self.local)
-            keep.start()
-            keep.wait()
-
-        @pl.when(section != self.target)
-        def _():
-            for offset in range(self.groups):
-                self.gather_copy(offset, 1).start()
-
-    def finish(self):
-        section, group, member = place()
-
-        @pl.when(section == self.target)
-        def _():
-            for offset in range(1, self.groups):
-                self.gather_copy(offset, 0).wait_send()
-                self.gathered(offset, 0).wait_recv()
-            for offset in range(self.groups):
-                self.gathered(offset, 1).wait_recv()
-
-        @pl.when(section != self.target)
-        def _():
-            for offset in range(self.groups):
-                self.gather_copy(offset, 1).wait_send()
+            self.half_copy(1 - section).wait_recv()
 
 
 class VectorSum:
@@ -791,8 +812,8 @@
     count = len(own)
 
     def body(x, seg, *refs):
-        vectors_in, own, (y,), kept, weights, held, sems = take(
-            refs, len(vectors), count, 1, len(shapes), count + 1, count + 1, 5
+        vectors_in, own, (y,), kept, weights, held, sems, (x_held, ctx_held) = take(
+            refs, len(vectors), count, 1, len(shapes), count + 1, count + 1, 5, 2
         )
         load, send, recv, out, _ = sems
         step = pl.program_id(0)
@@ -836,7 +857,49 @@
             for i in order:
                 push(i, section).start()
 
+        now, before = lax.rem(step, 2), lax.rem(step + 1, 2)
+        ctx_out, *mlp_kept = kept[4:]
+
+        def before_weights():
+            @pl.when(step == 0)
+            def _():
+                layer_zero(order[:2])
+
+        def start(hook=None):
+            x_held[now] = x[...]
+            forward_qkv(x, held, kept[:4], hook)
+            return attend(seg, kept[2], kept[3], ctx_held.at[now], width)
+
+        def end(between=None):
+            ctx_out[...] = ctx_held[before]
+            forward_mlp(x_held.at[before], held, [ctx_held.at[before]] + mlp_kept, y, between)
+
+        @pl.when(step < 2)
+        def _():
+            for _ in start(before_weights):
+                pass
+
         @pl.when(step == 1)
+        def _():
+            layer_zero(order[2:])
+
+        @pl.when(jnp.logical_or(step == 1, step == steps))
+        def _():
+            end()
+
+        @pl.when(jnp.logical_and(step > 1, step < steps))
+        def _():
+            parts = start()
+
+            def between():
+                for _ in range(INTERLEAVED):
+                    next(parts, None)
+
+            end(between)
+            for _ in parts:
+                pass
+
+        @pl.when(step == 2)
         def _():
             @pl.when(section == 0)
             def _():
@@ -851,41 +914,37 @@
             for i in order:
                 store(i).start()
 
-        def before_weights():
-            @pl.when(step == 0)
-            def _():
-                layer_zero(order[:2])
-
-        def after_attention():
-            @pl.when(step == 0)
-            def _():
-                layer_zero(order[2:])
-
-        forward(x, seg, held, kept, y, before_weights, after_attention)
-
-        @pl.when(step == steps - 1)
+        @pl.when(step == steps)
         def _():
             for i in order:
                 store(i).wait()
                 push(i, section).wait_send()
 
+    def first(i):
+        return jnp.minimum(i, steps - 1)
+
+    def then(i):
+        return jnp.maximum(i - 1, 0)
+
     def mine(i):
-        return lax.axis_index("section") * steps + i
+        return lax.axis_index("section") * steps + first(i)
 
     return pl.pallas_call(
         body,
-        grid=(steps,),
+        grid=(steps + 1,),
         in_specs=[block_at((STEP, width), 0, mine), block_at((1, STEP), 1, mine)]
         + [fixed(v.shape) for v in vectors]
         + [ANYWHERE] * count,
-        out_specs=[block_at((STEP, width), 0, lambda i: i)]
-        + [block_at(block, axis, lambda i: i) for _, _, block, axis in shapes]
+        out_specs=[block_at((STEP, width), 0, then)]
+        + [block_at(block, axis, first) for _, _, block, axis in shapes[:4]]
+        + [block_at(block, axis, then) for _, _, block, axis in shapes[4:]]
         + [ANYWHERE] * (count + 1),
         out_shape=[jax.ShapeDtypeStruct((steps * STEP, width), BF16)]
         + [jax.ShapeDtypeStruct(shape, dtype) for shape, dtype, _, _ in shapes]
         + [jax.ShapeDtypeStruct(shape, dtype) for shape, dtype in held],
         scratch_shapes=[pltpu.VMEM(shape, dtype) for shape, dtype in held]
-        + [pltpu.SemaphoreType.DMA((count + 1,))] * 5,
+        + [pltpu.SemaphoreType.DMA((count + 1,))] * 5
+        + [pltpu.VMEM((2, STEP, width), BF16), pltpu.VMEM((2, width, STEP), BF16)],
         compiler_params=params(0),
         cost_estimate=cost(steps * STEP * 4000000, 40),
         name="forward_first",
@@ -945,7 +1004,7 @@
                     for copy in loads:
                         copy.wait()
 
-            forward(x, seg, weights, [ref.at[step] for ref in attn_kept] + mlp_kept, y, None, after_attention)
+            forward(x, seg, weights, [ref.at[step] for ref in attn_kept] + mlp_kept, y, after_attention)
             y_own[...] = jnp.where(section == 0, x[...], y[...])
             y_send[step] = jnp.where(section == 0, y[...], x[...])
             y_copy(step).start()
@@ -1225,6 +1284,7 @@
         @at(3, 1)
         def _():
             near_pairs[2].start_members()
+            far_a.hand_over()
 
         @at(3, 2)
         def _():
@@ -1236,6 +1296,7 @@
         def _():
             near_pairs[1].finish(total_pairs[1])
             far_pairs[1].start_groups()
+            far_b.hand_over()
 
         @phase(3)
         def _():
@@ -1261,6 +1322,8 @@
                 far.start_gather()
             for index in range(steps):
                 g_copy(index).wait()
+            for far in fars[2:]:
+                far.hand_over()
             for far in fars:
                 far.finish()
 

time: 164 us -> 162 us (0.988)
  Pallas kernels: 163 us -> 161 us
    pallas_call x1, Pallas kernels: 60.9 us -> 58.6 us  [second_layer(): pl.pallas_call(body, grid=(2 * steps,), in_specs=[block_at((STEP, width),...]
where the time goes in v5:
time: 162 us
  Pallas kernels  161 us (99%)
    pallas_call x1, Pallas kernels, first_backward(): pl.pallas_call(body, grid=(starts[4],), in_specs=[block_at((1, rows), 1,...  65.9 us
    pallas_call x1, Pallas kernels, second_layer(): pl.pallas_call(body, grid=(2 * steps,), in_specs=[block_at((STEP, width),...  58.6 us
    pallas_call x1, Pallas kernels, first_forward(): pl.pallas_call(body, grid=(steps + 1,), in_specs=[block_at((STEP, width),...  27.5 us
    pallas_call x1, Pallas kernels, finish(): pl.pallas_call(body, grid=(2 * steps,), in_specs=[own, got, own, got] + [...  9.1 us

profile of v5, /device:TPU:0, one launch (start us, length us, event | category | flops | bytes accessed | tf_op | source)
XLA Modules:
  0.0 162.0 jit_solution(1488154924655527351)
XLA Ops:
  0.7 27.5 %forward_first.1 = (bf16[2048,384]{1,0:T(8,128)(2,1)}, bf16[2048,384]{1,0:T(8,128)(2,1)}, f32[2048,1]{1,0:T(8,128)}, bf16[2048,1152]{1,0:T(8,128)(2,1)}, bf16[84...) custom-call(bf16[4096,384]{1,0:T(8,128)(2,1)} %x.1, ...), custom_call_target="tpu_custom_call" | custom-call | flops 8192000000 | bytes 41943040 | tf_op jit(solution)/shard_map/forward_first/pallas_call | solution.py:932
  28.2 58.6 %second_layer.1 = (bf16[2048,384]{1,0:T(8,128)(2,1)}, bf16[2048,384]{1,0:T(8,128)(2,1)}, bf16[2048,384]{1,0:T(8,128)(2,1)}, bf16[2,1152,384]{2,1,0:T(8,128)(2,1)...) custom-call(bf16[2048,384]{1,0:T(8,128)(2,1)} %get-tuple-element.46.x, s32[1,4096]{1,0:T(1,128)} %bitcast.16, ...), custom_call_target="tpu_custom_call" | custom-call | flops 24576000000 | bytes 20971520 | tf_op jit(solution)/shard_map/second_layer/pallas_call | solution.py:1059
  86.7 65.9 %backward_first.1 = (bf16[2048,384]{1,0:T(8,128)(2,1)}, bf16[2048,384]{1,0:T(8,128)(2,1)}, bf16[2,4,80,384]{3,2,1,0:T(8,128)(2,1)}, bf16[2,4,80,384]{3,2,1,0:T(8...) custom-call(s32[1,4096]{1,0:T(1,128)} %bitcast.17, ...), custom_call_target="tpu_custom_call" | custom-call | flops 16384000000 | bytes 41943040 | tf_op jit(solution)/shard_map/backward_first/pallas_call | solution.py:1337
  152.7 9.1 %finish.1 = (bf16[1,4096,384]{2,1,0:T(8,128)(2,1)}, f32[1,4096,384]{2,1,0:T(8,128)}, f32[1,96]{1,0:T(1,128)}, f32[1,96]{1,0:T(1,128)}, f32[1,96,1152]{2,1,0:T(8,...) custom-call(bf16[2048,384]{1,0:T(8,128)(2,1)} %get-tuple-element.52., ...), custom_call_target="tpu_custom_call" | custom-call | bytes 16777216 | tf_op jit(solution)/shard_map/finish/pallas_call | solution.py:1473
